TPU v7x, 32 devices: a whole 2x2x4 slice. The times are simulated.
32 devices in a mesh: group: 2 (over y), sector: 4 (over z), op: 2 (over x), half: 2 (over core).
Axes of the slice: x: 2, y: 2, z: 4, core: 2. Of those that a mesh axis runs over, the one named last changes fastest.
Arguments:
- wavefunction: bfloat16 [24, 512, 512], P(('group', 'sector'), 'half'), parts along dimension 0, may hold values from -6 to 6
- left_env: bfloat16 [4, 24, 512, 512], P('op', ('group', 'sector'), 'half'), parts along dimension 1, may hold values from -0.25 to 0.25
- right_env: bfloat16 [4, 24, 512, 512], P('op', ('group', 'sector'), 'half'), parts along dimension 1, may hold values from -0.25 to 0.25
- source: int32 [4, 24], P(None, 'group'), parts along dimension 1, may hold values from 0 to 11, as said below
- left_dims: int32 [24], P('group'), parts along dimension 0, may hold values from 64 to 512
- right_dims: int32 [24], P('group'), parts along dimension 0, may hold values from 64 to 512
Outputs:
- sigma_product: bfloat16 [24, 512, 512], P(('group', 'sector'), 'half', 'op'), parts along dimension 0
There are 2 independent parts, one for each index of `group`. A program takes and returns all parts, laid end to end along the dimension named above; each array names one. Nothing has to cross between parts.
Inputs may be any that keep to these rules, and one draw needn't show every extreme that they name: For every op index o and sector index j, the sources source[k, t] over the 2 pairs of o and the 3 targets of j lie at most 2 in any one sector index (source // 3), and exactly 2 in some.
All inputs are finite; a program needn't handle non-finite values.
Results may differ from a plain program's by a relative error of at most 0.0049.
Values may be sent and summed in bfloat16 or wider, within the bound.
No kernel may reach another device: no remote copies, remote signals or barrier semaphores. Data moves between devices by JAX's collectives and lax.ppermute only.
A program may use at most 64 MiB of HBM per device.

v0:
```python
import jax
import jax.numpy as jnp
from jax import lax
from jax.sharding import PartitionSpec as P


def per_device(wavefunction, left_env, right_env, source, left_dims, right_dims):
    sec_local, half_rows, blk_cols = wavefunction.shape
    pair_local = left_env.shape[0]
    needed = pair_local * sec_local
    sector_count = lax.axis_size("sector")
    sector_me = lax.axis_index("sector")
    op_me = lax.axis_index("op")
    half_me = lax.axis_index("half")
    places = sector_me * sec_local + jnp.arange(sec_local, dtype=jnp.int32)
    row_ids = half_me * half_rows + jnp.arange(half_rows, dtype=jnp.int32)
    col_ids = jnp.arange(blk_cols, dtype=jnp.int32)
    left_live = jnp.take(left_dims, places)
    right_live = jnp.take(right_dims, places)
    live_mask = (row_ids[None, :, None] < left_live[:, None, None]) & (
        col_ids[None, None, :] < right_live[:, None, None]
    )
    masked = jnp.where(live_mask, wavefunction, jnp.zeros((), wavefunction.dtype))
    wanted = lax.dynamic_slice(source, (op_me * pair_local, 0), (pair_local, source.shape[1]))
    wanted = (
        wanted.reshape(pair_local, sector_count, sec_local)
        .transpose(1, 0, 2)
        .reshape(sector_count, needed)
    )
    own_needs = lax.dynamic_index_in_dim(wanted, sector_me, 0, keepdims=False)
    capacity = -(-needed // sector_count)
    holders = wanted // sec_local
    is_mine = (holders == sector_me).astype(jnp.int32)
    earlier_hits = jnp.cumsum(is_mine, axis=1) - is_mine
    slot_ids = jnp.arange(capacity, dtype=jnp.int32)
    pick_mask = (is_mine[:, :, None] == 1) & (earlier_hits[:, :, None] == slot_ids[None, None, :])
    local_slot = jnp.sum(jnp.where(pick_mask, (wanted % sec_local)[:, :, None], 0), axis=1)
    outgoing = jnp.take(masked, local_slot.reshape(-1), axis=0).reshape(
        sector_count, capacity, half_rows, blk_cols
    )
    incoming = lax.all_to_all(outgoing, "sector", split_axis=0, concat_axis=0, tiled=True)
    owners = own_needs // sec_local
    same_owner = owners[:, None] == owners[None, :]
    order_ids = jnp.arange(needed, dtype=jnp.int32)
    earlier = order_ids[None, :] < order_ids[:, None]
    rank_of = jnp.sum((same_owner & earlier).astype(jnp.int32), axis=1)
    fetched = jnp.take(
        incoming.reshape(sector_count * capacity, half_rows, blk_cols),
        owners * capacity + rank_of,
        axis=0,
    )
    right_rows = right_env.reshape(needed, right_env.shape[2], blk_cols)
    right_part = jnp.einsum(
        "nab,ncb->nac",
        lax.all_gather(fetched, "half", axis=1, tiled=True),
        right_rows,
        preferred_element_type=jnp.float32,
    ).astype(jnp.bfloat16)
    right_part = right_part.reshape(pair_local, sec_local, right_part.shape[1], right_part.shape[2])
    partial_sum = jnp.einsum(
        "ksrc,kscj->srj",
        left_env,
        lax.all_gather(right_part, "half", axis=3, tiled=True),
        preferred_element_type=jnp.float32,
    )
    summed = lax.psum_scatter(partial_sum, "op", scatter_dimension=2, tiled=True)
    col_width = summed.shape[2]
    out_cols = op_me * col_width + jnp.arange(col_width, dtype=jnp.int32)
    out_mask = (row_ids[None, :, None] < left_live[:, None, None]) & (
        out_cols[None, None, :] < right_live[:, None, None]
    )
    return jnp.where(out_mask, summed, jnp.zeros((), jnp.float32)).astype(jnp.bfloat16)


def solution(mesh):
    return jax.shard_map(
        per_device,
        mesh=mesh,
        in_specs=(
            P(("group", "sector"), "half", None),
            P("op", ("group", "sector"), "half", None),
            P("op", ("group", "sector"), "half", None),
            P(None, "group"),
            P("group"),
            P("group"),
        ),
        out_specs=P(("group", "sector"), "half", "op"),
        check_vma=False,
    )
```

profile of v0, /device:TPU:0, one launch (start us, length us, event | category | flops | bytes accessed | tf_op | source)
XLA Modules:
  0.0 144.3 jit_solution(7176255685843761287)
XLA Ops:
  6.5 0.0 copy-start
  6.5 0.0 copy-start.1
  6.5 0.8 constant_dynamic-slice_fusion.1
  7.4 0.1 reshape.308
  7.5 0.1 reshape.309
  7.6 0.2 reduce_window_sum.11
  7.8 0.1 select_reduce_fusion
  7.9 0.1 copy.17
  8.0 0.1 copy.16
  8.1 0.1 reshape.310
  8.2 1.3 gather_fusion.3
  9.5 1.3 gather_fusion.2
  10.8 0.1 iota_compare_fusion
  10.9 0.1 broadcast_compare_fusion.1
  11.0 0.0 copy-done.1
  11.0 0.3 and_select_fusion
  11.3 2.0 %gather_fusion = bf16[8,256,512]{2,1,0:T(8,128)(2,1)} fusion(bf16[3,256,512]{2,1,0:T(8,128)(2,1)S(1)} %and_select_fusion, s32[1024]{0:T(1024)S(1)} %pad_clamp_fusion.1), kind=kCustom, calls=%fused_computation.2 | custom fusion | bytes 4194336 | tf_op jit(solution)/shard_map/jit(_take)/gather | solution.py:38
  13.3 3.2 %broadcast_select_fusion = bf16[4,2,256,512]{3,2,1,0:T(8,128)(2,1)} fusion(bf16[4,2,256,512]{3,2,1,0:T(8,128)(2,1)} %bitcast.40, pred[4,2]{1,0:T(4,128)(4,1)S(1)} %copy.16), kind=kLoop, calls=%fused_computation.4 | loop fusion | flops 1048576 | bytes 4194312 | tf_op jit(solution)/shard_map/jit(_take)/select_n | solution.py:38
  16.5 6.3 %all-to-all-start = ((bf16[4,2,256,512]{3,2,1,0:T(8,128)(2,1)}), bf16[4,2,256,512]{3,2,1,0:T(8,128)(2,1)}, u32[]{:S(2)}, u32[]{:S(2)}) async-start(bf16[4,2,256,512]{3,2,1,0:T(8,128)(2,1)} %broadcast_select_fusion), calls=%async_computation | async-start | bytes 4194304 | tf_op jit(solution)/shard_map/all_to_all | solution.py:41
  22.8 0.0 all-gather.3.cloned.1.call-start
  22.8 0.2 convert_reduce_fusion
  23.1 48.0 %all-to-all-done = bf16[4,2,256,512]{3,2,1,0:T(8,128)(2,1)} async-done(((bf16[4,2,256,512]{3,2,1,0:T(8,128)(2,1)}), bf16[4,2,256,512]{3,2,1,0:T(8,128)(2,1)}, u32[]{:S(2)}, u32[]{:S(2)}) %all-to-all-start) | async-done | bytes 2097184 | tf_op jit(solution)/shard_map/all_to_all | solution.py:41
  71.1 2.2 %gather_fusion.1 = bf16[6,256,512]{2,1,0:T(8,128)(2,1)S(1)} fusion(bf16[8,256,512]{2,1,0:T(8,128)(2,1)} %bitcast.6, s32[1024]{0:T(1024)S(1)} %pad_clamp_fusion), kind=kCustom, calls=%fused_computation.3 | custom fusion | bytes 3145752 | tf_op jit(solution)/shard_map/jit(_take)/gather | solution.py:47
  73.3 1.4 broadcast_select_fusion.1
  74.7 0.0 all-gather.3.cloned.1.call-update
  74.7 0.0 all-gather.5.cloned.1.call-start
  74.8 11.3 %all-gather.3.cloned.1.call-done = bf16[6,512,512]{2,1,0:T(8,128)(2,1)} async-done(((bf16[6,256,512]{2,1,0:T(8,128)(2,1)}), bf16[6,512,512]{2,1,0:T(8,128)(2,1)}) %all-gather.3.cloned.1.call-update) | async-done | bytes 3145744 | tf_op jit(solution)/shard_map/all_gather | solution.py:55
  86.1 0.0 copy-done
  86.1 2.9 %convolution_convert_fusion = bf16[6,512,256]{2,1,0:T(8,128)(2,1)S(1)} fusion(bf16[6,512,512]{2,1,0:T(8,128)(2,1)} %all-gather.3.cloned.1.call-done, bf16[6,256,512]{2,1,0:T(8,128)(2,1)S(1)} %bitcast.39), kind=kOutput, calls=%fused_computation.5 | convolution fusion | flops 806092800 | bytes 6291456 | tf_op jit(solution)/shard_map/nab,ncb->nac/dot_general | solution.py:53
  89.1 1.6 %copy.18 = bf16[2,3,512,256]{2,3,0,1:T(8,128)(2,1)} copy(bf16[2,3,512,256]{3,2,1,0:T(8,128)(2,1)S(1)} %bitcast.41) | data formatting | bytes 3145728 | tf_op jit(solution)/shard_map/reshape | solution.py:59
  90.6 0.0 copy-start.2
  90.6 0.0 all-gather.5.cloned.1.call-update
  90.7 0.0 reduce-scatter.2.cloned.1.call-start
  90.7 13.4 %all-gather.5.cloned.1.call-done = bf16[2,3,512,512]{2,3,0,1:T(8,128)(2,1)} async-done(((bf16[2,3,512,256]{2,3,0,1:T(8,128)(2,1)}), bf16[2,3,512,512]{2,3,0,1:T(8,128)(2,1)}) %all-gather.5.cloned.1.call-update) | async-done | bytes 3145744 | tf_op jit(solution)/shard_map/all_gather | solution.py:63
  104.1 0.0 copy-done.2
  104.1 4.1 %fusion.2 = f32[3,256,512]{1,2,0:T(8,128)} fusion(bf16[2,3,512,512]{2,3,0,1:T(8,128)(2,1)} %all-gather.5.cloned.1.call-done, bf16[2,3,256,512]{3,2,1,0:T(8,128)(2,1)S(1)} %copy-done.2), kind=kOutput, calls=%fused_computation.10 | convolution fusion | flops 805306368 | bytes 6291456 | tf_op jit(solution)/shard_map/ksrc,kscj->srj/dot_general | solution.py:60
  108.2 0.0 reduce-scatter.2.cloned.1.call-update
  108.2 0.1 broadcast_compare_fusion
  108.3 27.3 %reduce-scatter.2.cloned.1.call-done = f32[3,256,256]{1,2,0:T(8,128)} async-done(((f32[3,256,512]{1,2,0:T(8,128)}), f32[3,256,256]{1,2,0:T(8,128)}) %reduce-scatter.2.cloned.1.call-update) | async-done | bytes 786448 | tf_op jit(solution)/shard_map/reduce_scatter | solution.py:66
  135.6 1.3 select_convert_fusion
  136.9 0.9 copy.20
  (17 shorter events, 0.1 us)
Async XLA Ops:
  6.5 79.6 %copy-start = (bf16[2,3,256,512]{3,2,1,0:T(8,128)(2,1)S(1)}, bf16[2,3,256,512]{3,2,1,0:T(8,128)(2,1)}, u32[]{:S(2)}) copy-start(bf16[2,3,256,512]{3,2,1,0:T(8,128)(2,1)} %param.10) | copy-start | bytes 4718596
  6.5 4.5 %copy-start.1 = (bf16[3,256,512]{2,1,0:T(8,128)(2,1)S(1)}, bf16[3,256,512]{2,1,0:T(8,128)(2,1)}, u32[]{:S(2)}) copy-start(bf16[3,256,512]{2,1,0:T(8,128)(2,1)} %param.8) | copy-start | bytes 2359300
  16.5 54.6 %all-to-all-start = ((bf16[4,2,256,512]{3,2,1,0:T(8,128)(2,1)}), bf16[4,2,256,512]{3,2,1,0:T(8,128)(2,1)}, u32[]{:S(2)}, u32[]{:S(2)}) async-start(bf16[4,2,256,512]{3,2,1,0:T(8,128)(2,1)} %broadcast_select_fusion), calls=%async_computation | async-start | bytes 4194304 | tf_op jit(solution)/shard_map/all_to_all | solution.py:41
  22.8 63.3 %all-gather.3.cloned.1.call-start = ((), (), s32[]{:S(2)}) async-start(), calls=%async_computation.2 | async-start | bytes 4718592 | tf_op jit(solution)/shard_map/all_gather | solution.py:55
  74.7 29.4 %all-gather.5.cloned.1.call-start = ((), (), s32[]{:S(2)}) async-start(), calls=%async_computation.3 | async-start | bytes 4718592 | tf_op jit(solution)/shard_map/all_gather | solution.py:63
  90.6 13.5 %copy-start.2 = (bf16[2,3,256,512]{3,2,1,0:T(8,128)(2,1)S(1)}, bf16[2,3,256,512]{3,2,1,0:T(8,128)(2,1)}, u32[]{:S(2)}) copy-start(bf16[2,3,256,512]{3,2,1,0:T(8,128)(2,1)} %param.9) | copy-start | bytes 4718596
  90.7 44.9 %reduce-scatter.2.cloned.1.call-start = ((), (), s32[]{:S(2)}) async-start(), calls=%async_computation.4 | async-start | bytes 2359296 | tf_op jit(solution)/shard_map/reduce_scatter | solution.py:66
Sparse Core Ops, SparseCore 0:
  74.9 11.2 all-gather.2
  90.8 13.2 all-gather.4
  108.3 27.2 reduce-scatter.1
where the time goes:
time: 145 us; the launch traced here: 144 us
  waiting for transfers between devices  100 us (69%)
  between operations  13.2 us (9%)
  local copies, waits for them, and re-layouts  10.6 us (7%)
  other arithmetic  7.04 us (5%)
  matrix products  6.96 us (5%)
  starting transfers between devices  6.4 us (4%)
    all_to_all x1, waiting for transfers between devices, per_device(): lax.all_to_all(outgoing, 'sector', split_axis=0, concat_axis=0, tiled=True)  48 us
    reduce_scatter x1, waiting for transfers between devices, per_device(): lax.psum_scatter(partial_sum, 'op', scatter_dimension=2, tiled=True)  27.3 us
    all_gather x1, waiting for transfers between devices, per_device(): lax.all_gather(right_part, 'half', axis=3, tiled=True)  13.4 us
    all_gather x1, waiting for transfers between devices, per_device(): lax.all_gather(fetched, 'half', axis=1, tiled=True)  11.3 us
    all_to_all x1, starting transfers between devices, per_device(): lax.all_to_all(outgoing, 'sector', split_axis=0, concat_axis=0, tiled=True)  6.32 us
    dot_general x1, matrix products, per_device(): jnp.einsum('ksrc,kscj->srj', left_env, lax.all_gather(right_part, 'half',...  4.06 us
    select_n x2, other arithmetic, per_device(): jnp.take(masked, local_slot.reshape(-1), axis=0)  3.2 us
    dot_general x1, matrix products, per_device(): jnp.einsum('nab,ncb->nac', lax.all_gather(fetched, 'half', axis=1, tiled=...  2.9 us
  transfers between devices with their start and end apart: 4, of which 4 were waited for; matrix products, arithmetic and copies ran while one was open for 0% of the time, Pallas kernels for 0%

commit v1 on v0

--- a/solution.py
+++ b/solution.py
@@ -1,10 +1,17 @@
+import functools
+
 import jax
 import jax.numpy as jnp
 from jax import lax
+from jax.experimental import pallas as pl
+from jax.experimental.pallas import tpu as pltpu
 from jax.sharding import PartitionSpec as P
 
-
-def per_device(wavefunction, left_env, right_env, source, left_dims, right_dims):
+BF16 = jnp.bfloat16
+F32 = jnp.float32
+
+
+def general(wavefunction, left_env, right_env, source, left_dims, right_dims):
     sec_local, half_rows, blk_cols = wavefunction.shape
     pair_local = left_env.shape[0]
     needed = pair_local * sec_local
@@ -54,14 +61,14 @@
         "nab,ncb->nac",
         lax.all_gather(fetched, "half", axis=1, tiled=True),
         right_rows,
-        preferred_element_type=jnp.float32,
-    ).astype(jnp.bfloat16)
+        preferred_element_type=F32,
+    ).astype(BF16)
     right_part = right_part.reshape(pair_local, sec_local, right_part.shape[1], right_part.shape[2])
     partial_sum = jnp.einsum(
         "ksrc,kscj->srj",
         left_env,
         lax.all_gather(right_part, "half", axis=3, tiled=True),
-        preferred_element_type=jnp.float32,
+        preferred_element_type=F32,
     )
     summed = lax.psum_scatter(partial_sum, "op", scatter_dimension=2, tiled=True)
     col_width = summed.shape[2]
@@ -69,12 +76,133 @@
     out_mask = (row_ids[None, :, None] < left_live[:, None, None]) & (
         out_cols[None, None, :] < right_live[:, None, None]
     )
-    return jnp.where(out_mask, summed, jnp.zeros((), jnp.float32)).astype(jnp.bfloat16)
+    return jnp.where(out_mask, summed, jnp.zeros((), F32)).astype(BF16)
+
+
+def sigma_kernel(
+    sizes, me, source, left_dims, right_dims, *refs
+):
+    pairs, secs, half_rows, blk = sizes
+    quarter = half_rows // 2
+    own, own_far = refs[0:2]
+    slabs = (refs[2:6], refs[6:10], refs[10:14])
+    left, right, right_far = refs[14:17]
+    send, keep = refs[17:19]
+    m_buf, r_buf, l_buf, m_sem, r_sem, l_sem = refs[19:25]
+    z, o, h = me[0], me[1], me[2]
+
+    def slot(n):
+        k, t = n // secs, n % secs
+        src = source[o * pairs + k, z * secs + t]
+        holder = src // secs
+        return k, t, src, holder ^ z, src - holder * secs
+
+    for n in range(pairs * secs):
+        k, t, src, kind, local = slot(n)
+        rows_mine = pl.multiple_of(h * half_rows, half_rows)
+        rows_far = pl.multiple_of((1 - h) * half_rows, half_rows)
+
+        @pl.when(kind == 0)
+        def _():
+            pltpu.make_async_copy(own.at[local], m_buf.at[n, pl.ds(rows_mine, half_rows)], m_sem.at[n]).start()
+            pltpu.make_async_copy(own_far.at[local], m_buf.at[n, pl.ds(rows_far, half_rows)], m_sem.at[n]).start()
+
+        for s in range(3):
+            @pl.when(kind == s + 1)
+            def _():
+                for piece, (base, at) in enumerate(
+                    ((rows_mine, o), (rows_mine, 1 - o), (rows_far, o), (rows_far, 1 - o))
+                ):
+                    first = pl.multiple_of(base + at * quarter, quarter)
+                    pltpu.make_async_copy(
+                        slabs[s][piece].at[local], m_buf.at[n, pl.ds(first, quarter)], m_sem.at[n]
+                    ).start()
+
+        at_mine = pl.multiple_of((h ^ o) * half_rows, half_rows)
+        at_far = pl.multiple_of((1 - (h ^ o)) * half_rows, half_rows)
+        pltpu.make_async_copy(right.at[k, t], r_buf.at[n, pl.ds(at_mine, half_rows)], r_sem.at[n]).start()
+        pltpu.make_async_copy(right_far.at[k, t], r_buf.at[n, pl.ds(at_far, half_rows)], r_sem.at[n]).start()
+        pltpu.make_async_copy(left.at[k, t], l_buf.at[n], l_sem.at[n]).start()
+
+    def one_slot(n):
+        k, t, src, kind, local = slot(n)
+        pltpu.make_async_copy(m_buf.at[n], m_buf.at[n], m_sem.at[n]).wait()
+        pltpu.make_async_copy(r_buf.at[n], r_buf.at[n], r_sem.at[n]).wait()
+        pltpu.make_async_copy(l_buf.at[n], l_buf.at[n], l_sem.at[n]).wait()
+        col = lax.broadcasted_iota(jnp.int32, (1, blk), 1)
+        col_live = (col < right_dims[src]).astype(F32).astype(BF16)
+        block = m_buf[n] * col_live
+        part = lax.dot_general(block, r_buf[n], (((1,), (1,)), ((), ())), preferred_element_type=F32)
+        row = lax.broadcasted_iota(jnp.int32, (blk, 1), 0)
+        part = jnp.where(row < left_dims[src], part, 0.0).astype(BF16)
+        return lax.dot_general(l_buf[n], part, (((1,), (0,)), ((), ())), preferred_element_type=F32)
+
+    for t in range(secs):
+        total = one_slot(t)
+        for k in range(1, pairs):
+            total = total + one_slot(k * secs + t)
+        keep[t] = total[:, : blk // 2]
+        send[t] = total[:, blk // 2 :].astype(BF16)
+
+
+def swap(x, axis):
+    return lax.ppermute(x, axis, [(0, 1), (1, 0)])
+
+
+def four_by_two(wavefunction, left_env, right_env, source, left_dims, right_dims):
+    secs, half_rows, blk = wavefunction.shape
+    pairs = left_env.shape[0]
+    quarter = half_rows // 2
+    z, o, h = lax.axis_index("sector"), lax.axis_index("op"), lax.axis_index("half")
+    me = jnp.stack([z, o, h]).astype(jnp.int32)
+    share = lax.dynamic_slice_in_dim(wavefunction, o * quarter, quarter, axis=1)
+    slabs = []
+    for kind in (1, 2, 3):
+        slabs.append(lax.ppermute(share, "sector", [(i, i ^ kind) for i in range(4)]))
+    own_far = swap(wavefunction, "half")
+    right_far = swap(right_env, "half")
+    pieces = []
+    for slab in slabs:
+        other = swap(slab, "op")
+        pieces += [slab, other, swap(slab, "half"), swap(other, "half")]
+    smem = pl.BlockSpec(memory_space=pltpu.SMEM)
+    any_spec = pl.BlockSpec(memory_space=pl.ANY)
+    vmem = pl.BlockSpec(memory_space=pltpu.VMEM)
+    needed = pairs * secs
+    send, keep = pl.pallas_call(
+        functools.partial(sigma_kernel, (pairs, secs, half_rows, blk)),
+        out_shape=(
+            jax.ShapeDtypeStruct((secs, half_rows, blk // 2), BF16),
+            jax.ShapeDtypeStruct((secs, half_rows, blk // 2), F32),
+        ),
+        in_specs=[smem] * 4 + [any_spec] * 17,
+        out_specs=(vmem, vmem),
+        scratch_shapes=[
+            pltpu.VMEM((needed, blk, blk), BF16),
+            pltpu.VMEM((needed, blk, blk), BF16),
+            pltpu.VMEM((needed, half_rows, blk), BF16),
+            pltpu.SemaphoreType.DMA((needed,)),
+            pltpu.SemaphoreType.DMA((needed,)),
+            pltpu.SemaphoreType.DMA((needed,)),
+        ],
+        compiler_params=pltpu.CompilerParams(vmem_limit_bytes=40 * 1024 * 1024),
+        name="sigma_slots",
+    )(me, source, left_dims, right_dims, wavefunction, own_far, *pieces, left_env, right_env, right_far)
+    total = keep + swap(send, "op").astype(F32)
+    places = z * secs + jnp.arange(secs, dtype=jnp.int32)
+    row_ids = h * half_rows + jnp.arange(half_rows, dtype=jnp.int32)
+    col_ids = o * (blk // 2) + jnp.arange(blk // 2, dtype=jnp.int32)
+    live = (row_ids[None, :, None] < jnp.take(left_dims, places)[:, None, None]) & (
+        col_ids[None, None, :] < jnp.take(right_dims, places)[:, None, None]
+    )
+    return jnp.where(live, total, 0.0).astype(BF16)
 
 
 def solution(mesh):
+    shape = mesh.shape
+    fits = (shape["sector"], shape["op"], shape["half"]) == (4, 2, 2)
     return jax.shard_map(
-        per_device,
+        four_by_two if fits else general,
         mesh=mesh,
         in_specs=(
             P(("group", "sector"), "half", None),

time: 145 us -> 83.1 us (0.57)
  waiting for transfers between devices: 100 us -> 49 us
  between operations: 13.2 us -> 0.06 us
  starting transfers between devices: 6.4 us -> 14 us
  matrix products: 6.96 us -> 0 us
  Pallas kernels: 0 us -> 6.96 us
  other arithmetic: 7.04 us -> 1.81 us
    ppermute x0 -> x15, waiting for transfers between devices: none -> 49 us  [the longest x3 29.9 us: four_by_two(): lax.ppermute(share, 'sector', [(i, i ^ kind) for i in range(4)])]
    all_to_all x1 -> x0, waiting for transfers between devices: 48 us -> none  [per_device(): lax.all_to_all(outgoing, 'sector', split_axis=0, concat_axis=0, tiled=True)]
    reduce_scatter x1 -> x0, waiting for transfers between devices: 27.3 us -> none  [per_device(): lax.psum_scatter(partial_sum, 'op', scatter_dimension=2, tiled=True)]
    all_gather x2 -> x0, waiting for transfers between devices: 24.7 us -> none  [the longest x1 13.4 us: per_device(): lax.all_gather(right_part, 'half', axis=3, tiled=True)]
    ppermute x0 -> x15, starting transfers between devices: none -> 14 us  [the longest x12 8.23 us: swap(): return lax.ppermute(x, axis, [(0, 1), (1, 0)])]
    pallas_call x0 -> x1, Pallas kernels: none -> 6.96 us  [four_by_two(): pl.pallas_call(functools.partial(sigma_kernel, (pairs, secs, half_rows, b...]
    dot_general x2 -> x0, matrix products: 6.96 us -> none  [the longest x1 4.06 us: per_device(): jnp.einsum('ksrc,kscj->srj', left_env, lax.all_gather(right_part, 'half',...]
    unnamed x6 -> x24, local copies, waits for them, and re-layouts: 0.01 us -> 6.74 us
  transfers between devices with their start and end apart: 4 -> 15, of which waited for: 4 -> 8; matrix products, arithmetic and copies ran while one was open for 0% -> 5% of each run, Pallas kernels for 0% -> 0%
where the time goes in v1:
time: 83.1 us; the launch traced here: 82.7 us
  waiting for transfers between devices  49 us (59%)
  starting transfers between devices  14 us (17%)
  local copies, waits for them, and re-layouts  10.8 us (13%)
  Pallas kernels  6.96 us (8%)
  other arithmetic  1.81 us (2%)
    ppermute x3, waiting for transfers between devices, four_by_two(): lax.ppermute(share, 'sector', [(i, i ^ kind) for i in range(4)])  29.9 us
    ppermute x12, waiting for transfers between devices, swap(): return lax.ppermute(x, axis, [(0, 1), (1, 0)])  19.1 us
    ppermute x12, starting transfers between devices, swap(): return lax.ppermute(x, axis, [(0, 1), (1, 0)])  8.23 us
    pallas_call x1, Pallas kernels, four_by_two(): pl.pallas_call(functools.partial(sigma_kernel, (pairs, secs, half_rows, b...  6.96 us
    unnamed x24, local copies, waits for them, and re-layouts  6.74 us
    ppermute x3, starting transfers between devices, four_by_two(): lax.ppermute(share, 'sector', [(i, i ^ kind) for i in range(4)])  5.76 us
    gather x1, local copies, waits for them, and re-layouts, four_by_two(): jnp.take(left_dims, places)[:, None, None]  1.82 us
  transfers between devices with their start and end apart: 15, of which 8 were waited for; matrix products, arithmetic and copies ran while one was open for 5% of the time, Pallas kernels for 0%

profile of v1, /device:TPU:0, one launch (start us, length us, event | category | flops | bytes accessed | tf_op | source)
XLA Modules:
  0.0 82.7 jit_solution(12977515588093828826)
XLA Ops:
  0.0 1.1 %constant_dynamic-slice_fusion = bf16[3,128,512]{2,1,0:T(8,128)(2,1)S(1)} fusion(bf16[3,256,512]{2,1,0:T(8,128)(2,1)} %refs_0_.1, s32[]{:T(128)S(6)} %select_n.14), kind=kLoop, calls=%fused_computation.13 | loop fusion | bytes 786436 | tf_op jit(solution)/shard_map/dynamic_slice | solution.py:158
  1.1 5.1 %collective-permute-start.9 = (bf16[3,128,512]{2,1,0:T(8,128)(2,1)S(1)}, bf16[3,128,512]{2,1,0:T(8,128)(2,1)S(1)}, u32[]{:S(2)}, u32[]{:S(2)}) collective-permute-start(bf16[3,128,512]{2,1,0:T(8,128)(2,1)S(1)} %constant_dynamic-slice_fusion), channel_id=1, source_target_pairs={{0,12},{4,8},{8,4},{12,0},{1,13},{5,9},{9,5},{13,1},{2,14},{6,10},... | collective-permute-start | bytes 1179656 | tf_op jit(solution)/shard_map/ppermute | solution.py:161
  6.2 0.0 collective-permute-start.1
  6.2 0.6 collective-permute-start.5
  6.9 0.0 collective-permute-start.13
  6.9 9.4 %collective-permute-done.9.refs_10_ = bf16[3,128,512]{2,1,0:T(8,128)(2,1)S(1)} collective-permute-done((bf16[3,128,512]{2,1,0:T(8,128)(2,1)S(1)}, bf16[3,128,512]{2,1,0:T(8,128)(2,1)S(1)}, u32[]{:S(2)}, u32[]{:S(2)}) %collective-permute-start.9) | collective-permute-done | bytes 393248 | tf_op jit(solution)/shard_map/ppermute | solution.py:161
  16.3 1.7 %collective-permute-start.10 = (bf16[3,128,512]{2,1,0:T(8,128)(2,1)S(1)}, bf16[3,128,512]{2,1,0:T(8,128)(2,1)S(1)}, u32[]{:S(2)}, u32[]{:S(2)}) collective-permute-start(bf16[3,128,512]{2,1,0:T(8,128)(2,1)S(1)} %collective-permute-done.9.refs_10_), channel_id=1, source_target_pairs={{0,2},{2,0},{1,3},{3,1},{4,6},{6,4},{5,7},{7,5},{8,10},{10,8},{9,1... | collective-permute-start | bytes 1179656 | tf_op jit(solution)/shard_map/ppermute | solution.py:149
  18.0 7.1 %collective-permute-done.1.refs_2_ = bf16[3,128,512]{2,1,0:T(8,128)(2,1)} collective-permute-done((bf16[3,128,512]{2,1,0:T(8,128)(2,1)S(1)}, bf16[3,128,512]{2,1,0:T(8,128)(2,1)}, u32[]{:S(2)}, u32[]{:S(2)}) %collective-permute-start.1) | collective-permute-done | bytes 393248 | tf_op jit(solution)/shard_map/ppermute | solution.py:161
  25.0 1.4 %collective-permute-start.2 = (bf16[3,128,512]{2,1,0:T(8,128)(2,1)}, bf16[3,128,512]{2,1,0:T(8,128)(2,1)S(1)}, u32[]{:S(2)}, u32[]{:S(2)}) collective-permute-start(bf16[3,128,512]{2,1,0:T(8,128)(2,1)} %collective-permute-done.1.refs_2_), channel_id=1, source_target_pairs={{0,2},{2,0},{1,3},{3,1},{4,6},{6,4},{5,7},{7,5},{8,10},{10,8},{9,1... | collective-permute-start | bytes 1179656 | tf_op jit(solution)/shard_map/ppermute | solution.py:149
  26.4 13.5 %collective-permute-done.5.refs_6_ = bf16[3,128,512]{2,1,0:T(8,128)(2,1)} collective-permute-done((bf16[3,128,512]{2,1,0:T(8,128)(2,1)S(1)}, bf16[3,128,512]{2,1,0:T(8,128)(2,1)}, u32[]{:S(2)}, u32[]{:S(2)}) %collective-permute-start.5) | collective-permute-done | bytes 393248 | tf_op jit(solution)/shard_map/ppermute | solution.py:161
  39.9 1.5 %collective-permute-start.6 = (bf16[3,128,512]{2,1,0:T(8,128)(2,1)}, bf16[3,128,512]{2,1,0:T(8,128)(2,1)S(1)}, u32[]{:S(2)}, u32[]{:S(2)}) collective-permute-start(bf16[3,128,512]{2,1,0:T(8,128)(2,1)} %collective-permute-done.5.refs_6_), channel_id=1, source_target_pairs={{0,2},{2,0},{1,3},{3,1},{4,6},{6,4},{5,7},{7,5},{8,10},{10,8},{9,1... | collective-permute-start | bytes 1179656 | tf_op jit(solution)/shard_map/ppermute | solution.py:149
  41.4 0.0 collective-permute-start.11
  41.4 0.0 collective-permute-done.10.refs_11_
  41.4 0.5 collective-permute-start.3
  41.9 0.0 collective-permute-done.2.refs_3_
  41.9 0.1 collective-permute-start.7
  42.0 0.2 copy-done.5
  42.2 8.1 %collective-permute-done.6.refs_7_ = bf16[3,128,512]{2,1,0:T(8,128)(2,1)S(1)} collective-permute-done((bf16[3,128,512]{2,1,0:T(8,128)(2,1)}, bf16[3,128,512]{2,1,0:T(8,128)(2,1)S(1)}, u32[]{:S(2)}, u32[]{:S(2)}) %collective-permute-start.6) | collective-permute-done | bytes 393248 | tf_op jit(solution)/shard_map/ppermute | solution.py:149
  50.3 0.8 copy-done.9
  51.0 0.0 collective-permute-start
  51.1 1.8 %gather_fusion = s32[3]{0:T(128)} fusion(s32[12]{0:T(128)} %left_dims.1, s32[1024]{0:T(1024)S(1)} %pad_clamp_fusion), kind=kCustom, calls=%fused_computation.clone | custom fusion | bytes 36 | tf_op jit(solution)/shard_map/jit(_take)/gather | solution.py:195
  52.9 0.0 copy-done.1
  52.9 1.1 %gather_fusion.1 = s32[3]{0:T(128)} fusion(s32[12]{0:T(128)S(1)} %copy-done.1, s32[1024]{0:T(1024)S(1)} %pad_clamp_fusion), kind=kCustom, calls=%fused_computation.1.clone | custom fusion | bytes 36 | tf_op jit(solution)/shard_map/jit(_take)/gather | solution.py:196
  54.0 0.0 collective-permute-done.11.refs_12_
  54.0 0.5 collective-permute-start.12
  54.5 0.0 collective-permute-done.3.refs_4_
  54.6 0.1 collective-permute-start.4
  54.6 0.0 collective-permute-done.7.refs_8_
  54.6 0.4 collective-permute-start.8
  55.1 0.1 pad_add_fusion.me
  55.1 0.6 broadcast_select_fusion
  55.8 0.0 collective-permute-done.refs_1_
  55.8 0.3 collective-permute-done.12.refs_13_
  56.1 0.6 collective-permute-done.4.refs_5_
  56.7 0.6 collective-permute-done.8.refs_9_
  57.2 0.0 collective-permute-done.13.refs_16_
  57.2 0.0 copy-start.3
  57.3 1.4 %copy-done.3 = bf16[2,3,256,512]{3,2,1,0:T(8,128)(2,1)S(1)} copy-done((bf16[2,3,256,512]{3,2,1,0:T(8,128)(2,1)S(1)}, bf16[2,3,256,512]{3,2,1,0:T(8,128)(2,1)}, u32[]{:S(2)}) %copy-start.3) | copy-done | bytes 1572888
  58.7 1.4 %copy-done.4 = bf16[2,3,256,512]{3,2,1,0:T(8,128)(2,1)S(1)} copy-done((bf16[2,3,256,512]{3,2,1,0:T(8,128)(2,1)S(1)}, bf16[2,3,256,512]{3,2,1,0:T(8,128)(2,1)}, u32[]{:S(2)}) %copy-start.4) | copy-done | bytes 1572888
  60.1 1.0 %copy-done.6 = bf16[3,128,512]{2,1,0:T(8,128)(2,1)S(1)} copy-done((bf16[3,128,512]{2,1,0:T(8,128)(2,1)S(1)}, bf16[3,128,512]{2,1,0:T(8,128)(2,1)}, u32[]{:S(2)}) %copy-start.6) | copy-done | bytes 393240
  61.1 1.0 %copy-done.8 = bf16[3,128,512]{2,1,0:T(8,128)(2,1)S(1)} copy-done((bf16[3,128,512]{2,1,0:T(8,128)(2,1)S(1)}, bf16[3,128,512]{2,1,0:T(8,128)(2,1)}, u32[]{:S(2)}) %copy-start.8) | copy-done | bytes 393240
  62.1 1.0 %copy-done.10 = bf16[3,128,512]{2,1,0:T(8,128)(2,1)S(1)} copy-done((bf16[3,128,512]{2,1,0:T(8,128)(2,1)S(1)}, bf16[3,128,512]{2,1,0:T(8,128)(2,1)}, u32[]{:S(2)}) %copy-start.10) | copy-done | bytes 393240
  63.1 7.0 %sigma_slots.1 = (bf16[3,256,256]{2,1,0:T(8,128)(2,1)S(1)}, f32[3,256,256]{2,1,0:T(8,128)S(1)}) custom-call(s32[3]{0:T(128)S(1)} %pad_add_fusion.me, s32[4,12]{1,0:T(4,128)S(1)} %copy-done.11, s32[12]{0:T(128)S(1)} %copy-done, s32[12]{0:T(128)S(1)} %copy-done.1, bf16[3,256,512]{2,1,0:T(8,128)(2,1)S(1)} %copy-done.2, ...), custom_call_target="tpu_custom_call" | custom-call | tf_op jit(solution)/shard_map/sigma_slots/pallas_call | solution.py:172
  70.0 2.0 %collective-permute-start.14 = (bf16[3,256,256]{2,1,0:T(8,128)(2,1)S(1)}, bf16[3,256,256]{2,1,0:T(8,128)(2,1)S(1)}, u32[]{:S(2)}, u32[]{:S(2)}) collective-permute-start(bf16[3,256,256]{2,1,0:T(8,128)(2,1)S(1)} %get-tuple-element.9), channel_id=1, source_target_pairs={{0,2},{2,0},{1,3},{3,1},{4,6},{6,4},{5,7},{7,5},{8,10},{10,8},{9,1... | collective-permute-start | bytes 1179656 | tf_op jit(solution)/shard_map/ppermute | solution.py:149
  72.1 0.1 broadcast_compare_fusion
  72.1 0.1 broadcast_compare_fusion.1
  72.2 9.5 %collective-permute-done.14 = bf16[3,256,256]{2,1,0:T(8,128)(2,1)S(1)} collective-permute-done((bf16[3,256,256]{2,1,0:T(8,128)(2,1)S(1)}, bf16[3,256,256]{2,1,0:T(8,128)(2,1)S(1)}, u32[]{:S(2)}, u32[]{:S(2)}) %collective-permute-start.14) | collective-permute-done | bytes 393248 | tf_op jit(solution)/shard_map/ppermute | solution.py:149
  81.7 0.9 %select_convert_fusion = bf16[3,256,256]{2,1,0:T(8,128)(2,1)} fusion(f32[3,256,256]{2,1,0:T(8,128)S(1)} %get-tuple-element.8, bf16[3,256,256]{2,1,0:T(8,128)(2,1)S(1)} %collective-permute-done.14, pred[3,256]{1,0:T(4,128)(4,1)S(1)} %broadcast_compare_fusion, pred[3,256]{1,0:T(4,128)(4,1)S(1)} %broadcast_compare_fusion.1), kind=kLoop, calls=%fused_computation.2 | loop fusion | flops 983040 | bytes 1574400 | tf_op jit(solution)/shard_map/convert_element_type | solution.py:198
  (19 shorter events, 0.0 us)
Async XLA Ops:
  0.0 57.2 %copy-start.2 = (bf16[3,256,512]{2,1,0:T(8,128)(2,1)S(1)}, bf16[3,256,512]{2,1,0:T(8,128)(2,1)}, u32[]{:S(2)}) copy-start(bf16[3,256,512]{2,1,0:T(8,128)(2,1)} %refs_0_.1) | copy-start | bytes 2359300
  0.0 57.2 %copy-start = (s32[12]{0:T(128)S(1)}, s32[12]{0:T(128)}, u32[]{:S(2)}) copy-start(s32[12]{0:T(128)} %left_dims.1) | copy-start | bytes 148
  0.0 52.9 %copy-start.1 = (s32[12]{0:T(128)S(1)}, s32[12]{0:T(128)}, u32[]{:S(2)}) copy-start(s32[12]{0:T(128)} %right_dims.1) | copy-start | bytes 148
  0.0 57.2 %copy-start.11 = (s32[4,12]{1,0:T(4,128)S(1)}, s32[4,12]{1,0:T(4,128)}, u32[]{:S(2)}) copy-start(s32[4,12]{1,0:T(4,128)} %source.1) | copy-start | bytes 580
  1.1 15.2 %collective-permute-start.9 = (bf16[3,128,512]{2,1,0:T(8,128)(2,1)S(1)}, bf16[3,128,512]{2,1,0:T(8,128)(2,1)S(1)}, u32[]{:S(2)}, u32[]{:S(2)}) collective-permute-start(bf16[3,128,512]{2,1,0:T(8,128)(2,1)S(1)} %constant_dynamic-slice_fusion), channel_id=1, source_target_pairs={{0,12},{4,8},{8,4},{12,0},{1,13},{5,9},{9,5},{13,1},{2,14},{6,10},... | collective-permute-start | bytes 1179656 | tf_op jit(solution)/shard_map/ppermute | solution.py:161
  6.2 18.8 %collective-permute-start.1 = (bf16[3,128,512]{2,1,0:T(8,128)(2,1)S(1)}, bf16[3,128,512]{2,1,0:T(8,128)(2,1)}, u32[]{:S(2)}, u32[]{:S(2)}) collective-permute-start(bf16[3,128,512]{2,1,0:T(8,128)(2,1)S(1)} %constant_dynamic-slice_fusion), channel_id=1, source_target_pairs={{0,4},{4,0},{8,12},{12,8},{1,5},{5,1},{9,13},{13,9},{2,6},{6,2},{1... | collective-permute-start | bytes 1179656 | tf_op jit(solution)/shard_map/ppermute | solution.py:161
  6.2 33.6 %collective-permute-start.5 = (bf16[3,128,512]{2,1,0:T(8,128)(2,1)S(1)}, bf16[3,128,512]{2,1,0:T(8,128)(2,1)}, u32[]{:S(2)}, u32[]{:S(2)}) collective-permute-start(bf16[3,128,512]{2,1,0:T(8,128)(2,1)S(1)} %constant_dynamic-slice_fusion), channel_id=1, source_target_pairs={{0,8},{4,12},{8,0},{12,4},{1,9},{5,13},{9,1},{13,5},{2,10},{6,14},... | collective-permute-start | bytes 1179656 | tf_op jit(solution)/shard_map/ppermute | solution.py:161
  6.9 50.4 %collective-permute-start.13 = (bf16[2,3,256,512]{3,2,1,0:T(8,128)(2,1)}, bf16[2,3,256,512]{3,2,1,0:T(8,128)(2,1)S(1)}, u32[]{:S(2)}, u32[]{:S(2)}) collective-permute-start(bf16[2,3,256,512]{3,2,1,0:T(8,128)(2,1)} %refs_15_.1), channel_id=1, source_target_pairs={{0,1},{1,0},{2,3},{3,2},{4,5},{5,4},{6,7},{7,6},{8,9},{9,8},{10,11... | collective-permute-start | bytes 4718600 | tf_op jit(solution)/shard_map/ppermute | solution.py:149
  16.3 25.1 %collective-permute-start.10 = (bf16[3,128,512]{2,1,0:T(8,128)(2,1)S(1)}, bf16[3,128,512]{2,1,0:T(8,128)(2,1)S(1)}, u32[]{:S(2)}, u32[]{:S(2)}) collective-permute-start(bf16[3,128,512]{2,1,0:T(8,128)(2,1)S(1)} %collective-permute-done.9.refs_10_), channel_id=1, source_target_pairs={{0,2},{2,0},{1,3},{3,1},{4,6},{6,4},{5,7},{7,5},{8,10},{10,8},{9,1... | collective-permute-start | bytes 1179656 | tf_op jit(solution)/shard_map/ppermute | solution.py:149
  25.0 16.9 %collective-permute-start.2 = (bf16[3,128,512]{2,1,0:T(8,128)(2,1)}, bf16[3,128,512]{2,1,0:T(8,128)(2,1)S(1)}, u32[]{:S(2)}, u32[]{:S(2)}) collective-permute-start(bf16[3,128,512]{2,1,0:T(8,128)(2,1)} %collective-permute-done.1.refs_2_), channel_id=1, source_target_pairs={{0,2},{2,0},{1,3},{3,1},{4,6},{6,4},{5,7},{7,5},{8,10},{10,8},{9,1... | collective-permute-start | bytes 1179656 | tf_op jit(solution)/shard_map/ppermute | solution.py:149
  39.9 10.4 %collective-permute-start.6 = (bf16[3,128,512]{2,1,0:T(8,128)(2,1)}, bf16[3,128,512]{2,1,0:T(8,128)(2,1)S(1)}, u32[]{:S(2)}, u32[]{:S(2)}) collective-permute-start(bf16[3,128,512]{2,1,0:T(8,128)(2,1)} %collective-permute-done.5.refs_6_), channel_id=1, source_target_pairs={{0,2},{2,0},{1,3},{3,1},{4,6},{6,4},{5,7},{7,5},{8,10},{10,8},{9,1... | collective-permute-start | bytes 1179656 | tf_op jit(solution)/shard_map/ppermute | solution.py:149
  41.4 12.7 %collective-permute-start.11 = (bf16[3,128,512]{2,1,0:T(8,128)(2,1)S(1)}, bf16[3,128,512]{2,1,0:T(8,128)(2,1)}, u32[]{:S(2)}, u32[]{:S(2)}) collective-permute-start(bf16[3,128,512]{2,1,0:T(8,128)(2,1)S(1)} %collective-permute-done.9.refs_10_), channel_id=1, source_target_pairs={{0,1},{1,0},{2,3},{3,2},{4,5},{5,4},{6,7},{7,6},{8,9},{9,8},{10,11... | collective-permute-start | bytes 1179656 | tf_op jit(solution)/shard_map/ppermute | solution.py:149
  41.4 0.8 copy-start.5
  41.4 13.2 %collective-permute-start.3 = (bf16[3,128,512]{2,1,0:T(8,128)(2,1)}, bf16[3,128,512]{2,1,0:T(8,128)(2,1)}, u32[]{:S(2)}, u32[]{:S(2)}) collective-permute-start(bf16[3,128,512]{2,1,0:T(8,128)(2,1)} %collective-permute-done.1.refs_2_), channel_id=1, source_target_pairs={{0,1},{1,0},{2,3},{3,2},{4,5},{5,4},{6,7},{7,6},{8,9},{9,8},{10,11... | collective-permute-start | bytes 1179656 | tf_op jit(solution)/shard_map/ppermute | solution.py:149
  41.9 8.4 %copy-start.7 = (bf16[3,128,512]{2,1,0:T(8,128)(2,1)}, bf16[3,128,512]{2,1,0:T(8,128)(2,1)S(1)}, u32[]{:S(2)}) copy-start(bf16[3,128,512]{2,1,0:T(8,128)(2,1)S(1)} %collective-permute-done.2.refs_3_) | copy-start | bytes 1179652
  41.9 12.7 %collective-permute-start.7 = (bf16[3,128,512]{2,1,0:T(8,128)(2,1)}, bf16[3,128,512]{2,1,0:T(8,128)(2,1)}, u32[]{:S(2)}, u32[]{:S(2)}) collective-permute-start(bf16[3,128,512]{2,1,0:T(8,128)(2,1)} %collective-permute-done.5.refs_6_), channel_id=1, source_target_pairs={{0,1},{1,0},{2,3},{3,2},{4,5},{5,4},{6,7},{7,6},{8,9},{9,8},{10,11... | collective-permute-start | bytes 1179656 | tf_op jit(solution)/shard_map/ppermute | solution.py:149
  50.3 0.8 copy-start.9
  51.0 4.7 %collective-permute-start = (bf16[3,256,512]{2,1,0:T(8,128)(2,1)}, bf16[3,256,512]{2,1,0:T(8,128)(2,1)S(1)}, u32[]{:S(2)}, u32[]{:S(2)}) collective-permute-start(bf16[3,256,512]{2,1,0:T(8,128)(2,1)} %refs_0_.1), channel_id=1, source_target_pairs={{0,1},{1,0},{2,3},{3,2},{4,5},{5,4},{6,7},{7,6},{8,9},{9,8},{10,11... | collective-permute-start | bytes 2359304 | tf_op jit(solution)/shard_map/ppermute | solution.py:149
  54.0 2.1 %collective-permute-start.12 = (bf16[3,128,512]{2,1,0:T(8,128)(2,1)}, bf16[3,128,512]{2,1,0:T(8,128)(2,1)S(1)}, u32[]{:S(2)}, u32[]{:S(2)}) collective-permute-start(bf16[3,128,512]{2,1,0:T(8,128)(2,1)} %copy-done.5), channel_id=1, source_target_pairs={{0,1},{1,0},{2,3},{3,2},{4,5},{5,4},{6,7},{7,6},{8,9},{9,8},{10,11... | collective-permute-start | bytes 1179656 | tf_op jit(solution)/shard_map/ppermute | solution.py:149
  54.6 2.1 %collective-permute-start.4 = (bf16[3,128,512]{2,1,0:T(8,128)(2,1)}, bf16[3,128,512]{2,1,0:T(8,128)(2,1)S(1)}, u32[]{:S(2)}, u32[]{:S(2)}) collective-permute-start(bf16[3,128,512]{2,1,0:T(8,128)(2,1)} %copy-done.7), channel_id=1, source_target_pairs={{0,1},{1,0},{2,3},{3,2},{4,5},{5,4},{6,7},{7,6},{8,9},{9,8},{10,11... | collective-permute-start | bytes 1179656 | tf_op jit(solution)/shard_map/ppermute | solution.py:149
  54.6 2.6 %collective-permute-start.8 = (bf16[3,128,512]{2,1,0:T(8,128)(2,1)}, bf16[3,128,512]{2,1,0:T(8,128)(2,1)S(1)}, u32[]{:S(2)}, u32[]{:S(2)}) collective-permute-start(bf16[3,128,512]{2,1,0:T(8,128)(2,1)} %copy-done.9), channel_id=1, source_target_pairs={{0,1},{1,0},{2,3},{3,2},{4,5},{5,4},{6,7},{7,6},{8,9},{9,8},{10,11... | collective-permute-start | bytes 1179656 | tf_op jit(solution)/shard_map/ppermute | solution.py:149
  57.2 1.4 %copy-start.3 = (bf16[2,3,256,512]{3,2,1,0:T(8,128)(2,1)S(1)}, bf16[2,3,256,512]{3,2,1,0:T(8,128)(2,1)}, u32[]{:S(2)}) copy-start(bf16[2,3,256,512]{3,2,1,0:T(8,128)(2,1)} %refs_14_.1) | copy-start | bytes 4718596
  58.7 1.4 %copy-start.4 = (bf16[2,3,256,512]{3,2,1,0:T(8,128)(2,1)S(1)}, bf16[2,3,256,512]{3,2,1,0:T(8,128)(2,1)}, u32[]{:S(2)}) copy-start(bf16[2,3,256,512]{3,2,1,0:T(8,128)(2,1)} %refs_15_.1) | copy-start | bytes 4718596
  60.1 1.0 %copy-start.6 = (bf16[3,128,512]{2,1,0:T(8,128)(2,1)S(1)}, bf16[3,128,512]{2,1,0:T(8,128)(2,1)}, u32[]{:S(2)}) copy-start(bf16[3,128,512]{2,1,0:T(8,128)(2,1)} %copy-done.5) | copy-start | bytes 1179652
  61.1 1.0 %copy-start.8 = (bf16[3,128,512]{2,1,0:T(8,128)(2,1)S(1)}, bf16[3,128,512]{2,1,0:T(8,128)(2,1)}, u32[]{:S(2)}) copy-start(bf16[3,128,512]{2,1,0:T(8,128)(2,1)} %copy-done.7) | copy-start | bytes 1179652
  62.1 1.0 %copy-start.10 = (bf16[3,128,512]{2,1,0:T(8,128)(2,1)S(1)}, bf16[3,128,512]{2,1,0:T(8,128)(2,1)}, u32[]{:S(2)}) copy-start(bf16[3,128,512]{2,1,0:T(8,128)(2,1)} %copy-done.9) | copy-start | bytes 1179652
  70.0 11.7 %collective-permute-start.14 = (bf16[3,256,256]{2,1,0:T(8,128)(2,1)S(1)}, bf16[3,256,256]{2,1,0:T(8,128)(2,1)S(1)}, u32[]{:S(2)}, u32[]{:S(2)}) collective-permute-start(bf16[3,256,256]{2,1,0:T(8,128)(2,1)S(1)} %get-tuple-element.9), channel_id=1, source_target_pairs={{0,2},{2,0},{1,3},{3,1},{4,6},{6,4},{5,7},{7,5},{8,10},{10,8},{9,1... | collective-permute-start | bytes 1179656 | tf_op jit(solution)/shard_map/ppermute | solution.py:149

commit v2 on v0

--- a/solution.py
+++ b/solution.py
@@ -1,10 +1,19 @@
+import functools
+
 import jax
 import jax.numpy as jnp
 from jax import lax
+from jax.experimental import pallas as pl
+from jax.experimental.pallas import tpu as pltpu
 from jax.sharding import PartitionSpec as P
 
-
-def per_device(wavefunction, left_env, right_env, source, left_dims, right_dims):
+BF16 = jnp.bfloat16
+F32 = jnp.float32
+VMEM_EARLY = 48 * 1024 * 1024
+VMEM_LATE = 56 * 1024 * 1024
+
+
+def general(wavefunction, left_env, right_env, source, left_dims, right_dims):
     sec_local, half_rows, blk_cols = wavefunction.shape
     pair_local = left_env.shape[0]
     needed = pair_local * sec_local
@@ -54,14 +63,14 @@
         "nab,ncb->nac",
         lax.all_gather(fetched, "half", axis=1, tiled=True),
         right_rows,
-        preferred_element_type=jnp.float32,
-    ).astype(jnp.bfloat16)
+        preferred_element_type=F32,
+    ).astype(BF16)
     right_part = right_part.reshape(pair_local, sec_local, right_part.shape[1], right_part.shape[2])
     partial_sum = jnp.einsum(
         "ksrc,kscj->srj",
         left_env,
         lax.all_gather(right_part, "half", axis=3, tiled=True),
-        preferred_element_type=jnp.float32,
+        preferred_element_type=F32,
     )
     summed = lax.psum_scatter(partial_sum, "op", scatter_dimension=2, tiled=True)
     col_width = summed.shape[2]
@@ -69,12 +78,335 @@
     out_mask = (row_ids[None, :, None] < left_live[:, None, None]) & (
         out_cols[None, None, :] < right_live[:, None, None]
     )
-    return jnp.where(out_mask, summed, jnp.zeros((), jnp.float32)).astype(jnp.bfloat16)
+    return jnp.where(out_mask, summed, jnp.zeros((), F32)).astype(BF16)
+
+
+def kinds_of(source, me, pairs, secs, op):
+    z = me[0]
+    found = []
+    for n in range(pairs * secs):
+        src = source[op * pairs + n // secs, z * secs + n % secs]
+        holder = src // secs
+        found.append((holder ^ z, src - holder * secs, src))
+    return found
+
+
+def ranked(slots, kind, rank):
+    slot, local, source = jnp.int32(-1), jnp.int32(0), jnp.int32(0)
+    seen = jnp.int32(0)
+    for n, (k, b, s) in enumerate(slots):
+        hit = (k == kind) & (seen == rank)
+        slot = jnp.where(hit, n, slot)
+        local = jnp.where(hit, b, local)
+        source = jnp.where(hit, s, source)
+        seen = seen + (k == kind).astype(jnp.int32)
+    return slot, local, source
+
+
+def plan_kernel(sizes, me, source, left, right, left_out, right_out, picks, sem):
+    pairs, secs, half_rows, blk = sizes
+    quarter = half_rows // 2
+    o = me[1]
+    mine = kinds_of(source, me, pairs, secs, o)
+    theirs = kinds_of(source, me, pairs, secs, 1 - o)
+    copies = []
+    for j in range(2):
+        n = jnp.maximum(ranked(mine, 3, j)[0], 0)
+        k, t = n // secs, n % secs
+        copies.append(pltpu.make_async_copy(right.at[k, t], right_out.at[j], sem.at[len(copies)]))
+        for part in range(2):
+            first = pl.multiple_of(part * half_rows + (1 - o) * quarter, quarter)
+            copies.append(
+                pltpu.make_async_copy(
+                    left.at[k, t, :, pl.ds(first, quarter)],
+                    left_out.at[j, :, pl.ds(part * quarter, quarter)],
+                    sem.at[len(copies)],
+                )
+            )
+    for copy in copies:
+        copy.start()
+    for kind in (1, 2):
+        for j in range(2):
+            picks[kind - 1, j] = ranked(theirs, kind, j)[1]
+    for copy in copies:
+        copy.wait()
+
+
+def full_slot(sizes, n, src, left_dims, right_dims, m, r, l):
+    blk = sizes[3]
+    col = lax.broadcasted_iota(jnp.int32, (1, blk), 1)
+    col_live = (col < right_dims[src]).astype(F32).astype(BF16)
+    part = lax.dot_general(m * col_live, r, (((1,), (1,)), ((), ())), preferred_element_type=F32)
+    row = lax.broadcasted_iota(jnp.int32, (blk, 1), 0)
+    part = jnp.where(row < left_dims[src], part, 0.0).astype(BF16)
+    return lax.dot_general(l, part, (((1,), (0,)), ((), ())), preferred_element_type=F32)
+
+
+def start_env(me, k, t, sizes, left, right, right_far, r_dst, l_dst, r_sem, l_sem):
+    half_rows = sizes[2]
+    o, h = me[1], me[2]
+    at_mine = pl.multiple_of((h ^ o) * half_rows, half_rows)
+    at_far = pl.multiple_of((1 - (h ^ o)) * half_rows, half_rows)
+    pltpu.make_async_copy(right.at[k, t], r_dst.at[pl.ds(at_mine, half_rows)], r_sem).start()
+    pltpu.make_async_copy(right_far.at[k, t], r_dst.at[pl.ds(at_far, half_rows)], r_sem).start()
+    if l_dst is not None:
+        pltpu.make_async_copy(left.at[k, t], l_dst, l_sem).start()
+
+
+def start_pieces(me, sizes, local, rank, pieces, m_dst, m_sem):
+    half_rows = sizes[2]
+    quarter = half_rows // 2
+    o, h = me[1], me[2]
+    for piece, (half, at) in zip(pieces, ((h, o), (h, 1 - o), (1 - h, o), (1 - h, 1 - o))):
+        first = pl.multiple_of(half * half_rows + at * quarter, quarter)
+        index = local if piece.shape[0] == sizes[1] else rank
+        pltpu.make_async_copy(piece.at[index], m_dst.at[pl.ds(first, quarter)], m_sem).start()
+
+
+def early_kernel(sizes, me, source, left_dims, right_dims, *refs):
+    pairs, secs, half_rows, blk = sizes
+    own, own_far = refs[0:2]
+    near = refs[2:6]
+    left, right, right_far = refs[6:9]
+    acc, m_buf, r_buf, l_buf, m_sem, r_sem, l_sem = refs[9:]
+    o, h = me[1], me[2]
+    slots = kinds_of(source, me, pairs, secs, o)
+    rank = jnp.int32(0)
+    for n, (kind, local, src) in enumerate(slots):
+        @pl.when(kind == 0)
+        def _():
+            mine = pl.multiple_of(h * half_rows, half_rows)
+            far = pl.multiple_of((1 - h) * half_rows, half_rows)
+            pltpu.make_async_copy(own.at[local], m_buf.at[n, pl.ds(mine, half_rows)], m_sem.at[n]).start()
+            pltpu.make_async_copy(own_far.at[local], m_buf.at[n, pl.ds(far, half_rows)], m_sem.at[n]).start()
+
+        @pl.when(kind == 1)
+        def _(rank=rank):
+            start_pieces(me, sizes, local, rank, near, m_buf.at[n], m_sem.at[n])
+
+        @pl.when(kind <= 1)
+        def _():
+            start_env(
+                me, n // secs, n % secs, sizes, left, right, right_far,
+                r_buf.at[n], l_buf.at[n], r_sem.at[n], l_sem.at[n],
+            )
+
+        rank = rank + (kind == 1).astype(jnp.int32)
+
+    acc[...] = jnp.zeros_like(acc)
+    for n, (kind, local, src) in enumerate(slots):
+        @pl.when(kind <= 1)
+        def _():
+            pltpu.make_async_copy(m_buf.at[n], m_buf.at[n], m_sem.at[n]).wait()
+            pltpu.make_async_copy(r_buf.at[n], r_buf.at[n], r_sem.at[n]).wait()
+            pltpu.make_async_copy(l_buf.at[n], l_buf.at[n], l_sem.at[n]).wait()
+            acc[n % secs] += full_slot(sizes, n, src, left_dims, right_dims, m_buf[n], r_buf[n], l_buf[n])
+
+
+def late_kernel(sizes, me, source, left_dims, right_dims, *refs):
+    pairs, secs, half_rows, blk = sizes
+    quarter = half_rows // 2
+    mid = refs[0:4]
+    late_end, late_end_far, late_mid, late_mid_far = refs[4:8]
+    left, right, right_far, left_x, right_x, right_x_far, early = refs[8:15]
+    send, keep = refs[15:17]
+    acc, m_buf, r_buf, l_buf, lm_buf, lr_buf, ll_buf = refs[17:24]
+    m_sem, r_sem, l_sem, lm_sem, lr_sem, ll_sem, acc_sem = refs[24:]
+    z, o, h = me[0], me[1], me[2]
+    is_end = (z == 0) | (z == 3)
+    mine = kinds_of(source, me, pairs, secs, o)
+    theirs = kinds_of(source, me, pairs, secs, 1 - o)
+    pltpu.make_async_copy(early, acc, acc_sem).start()
+
+    a_slots = [ranked(mine, 2, j) for j in range(2)]
+    for j, (n, local, src) in enumerate(a_slots):
+        @pl.when(n >= 0)
+        def _():
+            start_env(
+                me, n // secs, n % secs, sizes, left, right, right_far,
+                r_buf.at[j], l_buf.at[j], r_sem.at[j], l_sem.at[j],
+            )
+            start_pieces(me, sizes, local, j, mid, m_buf.at[j], m_sem.at[j])
+
+    late_slots = [ranked(mine, 3, j) for j in range(2)] + [ranked(theirs, 3, j) for j in range(2)]
+    for i, (n, local, src) in enumerate(late_slots):
+        j = i % 2
+
+        @pl.when(n >= 0)
+        def _():
+            if i < 2:
+                k, t = n // secs, n % secs
+                start_env(
+                    me, k, t, sizes, left, right, right_far, lr_buf.at[i], None, lr_sem.at[i], None
+                )
+                for part in range(2):
+                    first = pl.multiple_of(part * half_rows + o * quarter, quarter)
+                    pltpu.make_async_copy(
+                        left.at[k, t, :, pl.ds(first, quarter)],
+                        ll_buf.at[i, :, pl.ds(part * quarter, quarter)],
+                        ll_sem.at[i],
+                    ).start()
+            else:
+                at_mine = pl.multiple_of((h ^ o) * half_rows, half_rows)
+                at_far = pl.multiple_of((1 - (h ^ o)) * half_rows, half_rows)
+                pltpu.make_async_copy(right_x.at[j], lr_buf.at[i, pl.ds(at_mine, half_rows)], lr_sem.at[i]).start()
+                pltpu.make_async_copy(right_x_far.at[j], lr_buf.at[i, pl.ds(at_far, half_rows)], lr_sem.at[i]).start()
+                pltpu.make_async_copy(left_x.at[j], ll_buf.at[i], ll_sem.at[i]).start()
+            row_mine = pl.multiple_of(h * quarter, quarter)
+            row_far = pl.multiple_of((1 - h) * quarter, quarter)
+
+            @pl.when(is_end)
+            def _():
+                pltpu.make_async_copy(late_end.at[local], lm_buf.at[i, pl.ds(row_mine, quarter)], lm_sem.at[i]).start()
+                pltpu.make_async_copy(late_end_far.at[local], lm_buf.at[i, pl.ds(row_far, quarter)], lm_sem.at[i]).start()
+
+            @pl.when(jnp.logical_not(is_end))
+            def _():
+                pltpu.make_async_copy(late_mid.at[local], lm_buf.at[i, pl.ds(row_mine, quarter)], lm_sem.at[i]).start()
+                pltpu.make_async_copy(late_mid_far.at[local], lm_buf.at[i, pl.ds(row_far, quarter)], lm_sem.at[i]).start()
+
+    pltpu.make_async_copy(early, acc, acc_sem).wait()
+    for j, (n, local, src) in enumerate(a_slots):
+        @pl.when(n >= 0)
+        def _():
+            pltpu.make_async_copy(m_buf.at[j], m_buf.at[j], m_sem.at[j]).wait()
+            pltpu.make_async_copy(r_buf.at[j], r_buf.at[j], r_sem.at[j]).wait()
+            pltpu.make_async_copy(l_buf.at[j], l_buf.at[j], l_sem.at[j]).wait()
+            acc[n % secs] += full_slot(sizes, n, src, left_dims, right_dims, m_buf[j], r_buf[j], l_buf[j])
+
+    for i, (n, local, src) in enumerate(late_slots):
+        @pl.when(n >= 0)
+        def _():
+            pltpu.make_async_copy(lm_buf.at[i], lm_buf.at[i], lm_sem.at[i]).wait()
+            pltpu.make_async_copy(lr_buf.at[i], lr_buf.at[i], lr_sem.at[i]).wait()
+            pltpu.make_async_copy(ll_buf.at[i], ll_buf.at[i], ll_sem.at[i]).wait()
+            col = lax.broadcasted_iota(jnp.int32, (1, blk), 1)
+            col_live = (col < right_dims[src]).astype(F32).astype(BF16)
+            part = lax.dot_general(
+                lm_buf[i] * col_live, lr_buf[i], (((1,), (1,)), ((), ())), preferred_element_type=F32
+            )
+            at = lax.broadcasted_iota(jnp.int32, (half_rows, 1), 0)
+            row = at + o * quarter + jnp.where(at < quarter, 0, quarter)
+            part = jnp.where(row < left_dims[src], part, 0.0).astype(BF16)
+            acc[n % secs] += lax.dot_general(
+                ll_buf[i], part, (((1,), (0,)), ((), ())), preferred_element_type=F32
+            )
+
+    keep[...] = acc[:, :, : blk // 2]
+    send[...] = acc[:, :, blk // 2 :].astype(BF16)
+
+
+def swap(x, axis):
+    return lax.ppermute(x, axis, [(0, 1), (1, 0)])
+
+
+def swap_on(x, axis, sectors):
+    return lax.ppermute(x, ("sector", axis), [(2 * s + i, 2 * s + 1 - i) for s in sectors for i in range(2)])
+
+
+def four_by_two(wavefunction, left_env, right_env, source, left_dims, right_dims):
+    secs, half_rows, blk = wavefunction.shape
+    pairs = left_env.shape[0]
+    quarter = half_rows // 2
+    sizes = (pairs, secs, half_rows, blk)
+    z, o, h = lax.axis_index("sector"), lax.axis_index("op"), lax.axis_index("half")
+    me = jnp.stack([z, o, h]).astype(jnp.int32)
+    smem = pl.BlockSpec(memory_space=pltpu.SMEM)
+    any_spec = pl.BlockSpec(memory_space=pl.ANY)
+    vmem = pl.BlockSpec(memory_space=pltpu.VMEM)
+    needed = pairs * secs
+
+    share = lax.dynamic_slice_in_dim(wavefunction, o * quarter, quarter, axis=1)
+    near = lax.ppermute(share, "sector", [(i, i ^ 1) for i in range(4)])
+    mid = lax.ppermute(share, "sector", [(i, i ^ 2) for i in range(4)])
+    late_mid = lax.ppermute(share, "sector", [(1, 2), (2, 1)])
+    late_end = lax.ppermute(mid, "sector", [(1, 0), (2, 3)])
+
+    left_out, right_out, picks = pl.pallas_call(
+        functools.partial(plan_kernel, sizes),
+        out_shape=(
+            jax.ShapeDtypeStruct((2, half_rows, blk // 2), BF16),
+            jax.ShapeDtypeStruct((2, half_rows, blk), BF16),
+            jax.ShapeDtypeStruct((2, 2), jnp.int32),
+        ),
+        in_specs=[smem, smem, any_spec, any_spec],
+        out_specs=(any_spec, any_spec, smem),
+        scratch_shapes=[pltpu.SemaphoreType.DMA((6,))],
+        name="plan",
+    )(me, source, left_env, right_env)
+    right_x = swap(right_out, "op")
+    left_x = swap(left_out, "op")
+    own_far = swap(wavefunction, "half")
+    right_far = swap(right_env, "half")
+    right_x_far = swap(right_x, "half")
+
+    def pick(slab, row):
+        return jnp.stack([lax.dynamic_index_in_dim(slab, picks[row, j], 0, keepdims=False) for j in range(2)])
+
+    near_x = swap(pick(near, 0), "op")
+    mid_x = swap(pick(mid, 1), "op")
+    near_refs = (near, near_x, swap(near, "half"), swap(near_x, "half"))
+    mid_refs = (mid, mid_x, swap(mid, "half"), swap(mid_x, "half"))
+    late_refs = (late_end, swap_on(late_end, "half", (0, 3)), late_mid, swap_on(late_mid, "half", (1, 2)))
+
+    early = pl.pallas_call(
+        functools.partial(early_kernel, sizes),
+        out_shape=jax.ShapeDtypeStruct((secs, half_rows, blk), F32),
+        in_specs=[smem] * 4 + [any_spec] * 9,
+        out_specs=vmem,
+        scratch_shapes=[
+            pltpu.VMEM((needed, blk, blk), BF16),
+            pltpu.VMEM((needed, blk, blk), BF16),
+            pltpu.VMEM((needed, half_rows, blk), BF16),
+        ] + [pltpu.SemaphoreType.DMA((needed,))] * 3,
+        compiler_params=pltpu.CompilerParams(vmem_limit_bytes=VMEM_EARLY),
+        cost_estimate=pl.CostEstimate(flops=2 * 10**9, bytes_accessed=8 * 10**6, transcendentals=0),
+        name="early_slots",
+    )(me, source, left_dims, right_dims, wavefunction, own_far, *near_refs, left_env, right_env, right_far)
+
+    send, keep = pl.pallas_call(
+        functools.partial(late_kernel, sizes),
+        out_shape=(
+            jax.ShapeDtypeStruct((secs, half_rows, blk // 2), BF16),
+            jax.ShapeDtypeStruct((secs, half_rows, blk // 2), F32),
+        ),
+        in_specs=[smem] * 4 + [any_spec] * 15,
+        out_specs=(vmem, vmem),
+        scratch_shapes=[
+            pltpu.VMEM((secs, half_rows, blk), F32),
+            pltpu.VMEM((2, blk, blk), BF16),
+            pltpu.VMEM((2, blk, blk), BF16),
+            pltpu.VMEM((2, half_rows, blk), BF16),
+            pltpu.VMEM((4, half_rows, blk), BF16),
+            pltpu.VMEM((4, blk, blk), BF16),
+            pltpu.VMEM((4, half_rows, half_rows), BF16),
+        ]
+        + [pltpu.SemaphoreType.DMA((2,))] * 3
+        + [pltpu.SemaphoreType.DMA((4,))] * 3
+        + [pltpu.SemaphoreType.DMA],
+        compiler_params=pltpu.CompilerParams(vmem_limit_bytes=VMEM_LATE),
+        cost_estimate=pl.CostEstimate(flops=2 * 10**9, bytes_accessed=8 * 10**6, transcendentals=0),
+        name="late_slots",
+    )(
+        me, source, left_dims, right_dims, *mid_refs, *late_refs,
+        left_env, right_env, right_far, left_x, right_x, right_x_far, early,
+    )
+    total = keep + swap(send, "op").astype(F32)
+    row_ids = h * half_rows + jnp.arange(half_rows, dtype=jnp.int32)
+    col_ids = o * (blk // 2) + jnp.arange(blk // 2, dtype=jnp.int32)
+    left_live = lax.dynamic_slice_in_dim(left_dims, z * secs, secs)
+    right_live = lax.dynamic_slice_in_dim(right_dims, z * secs, secs)
+    live = (row_ids[None, :, None] < left_live[:, None, None]) & (
+        col_ids[None, None, :] < right_live[:, None, None]
+    )
+    return jnp.where(live, total, 0.0).astype(BF16)
 
 
 def solution(mesh):
+    shape = mesh.shape
+    fits = (shape["sector"], shape["op"], shape["half"]) == (4, 2, 2)
     return jax.shard_map(
-        per_device,
+        four_by_two if fits else general,
         mesh=mesh,
         in_specs=(
             P(("group", "sector"), "half", None),

time: 145 us -> 107 us (0.74)
  waiting for transfers between devices: 100 us -> 27.9 us
  Pallas kernels: 0 us -> 37.6 us
  starting transfers between devices: 6.4 us -> 19.7 us
  matrix products: 6.96 us -> 0 us
  between operations: 13.2 us -> 7.8 us
  other arithmetic: 7.04 us -> 2.85 us
    all_to_all x1 -> x0, waiting for transfers between devices: 48 us -> none  [per_device(): lax.all_to_all(outgoing, 'sector', split_axis=0, concat_axis=0, tiled=True)]
    pallas_call x0 -> x3, Pallas kernels: none -> 37.6 us  [the longest x1 26.4 us: four_by_two(): pl.pallas_call(functools.partial(plan_kernel, sizes), out_shape=(jax.Shap...]
    ppermute x0 -> x18, waiting for transfers between devices: none -> 27.9 us  [the longest x12 23.2 us: swap(): return lax.ppermute(x, axis, [(0, 1), (1, 0)])]
    reduce_scatter x1 -> x0, waiting for transfers between devices: 27.3 us -> none  [per_device(): lax.psum_scatter(partial_sum, 'op', scatter_dimension=2, tiled=True)]
    all_gather x2 -> x0, waiting for transfers between devices: 24.7 us -> none  [the longest x1 13.4 us: per_device(): lax.all_gather(right_part, 'half', axis=3, tiled=True)]
    ppermute x0 -> x18, starting transfers between devices: none -> 19.7 us  [the longest x12 8.54 us: swap(): return lax.ppermute(x, axis, [(0, 1), (1, 0)])]
    dot_general x2 -> x0, matrix products: 6.96 us -> none  [the longest x1 4.06 us: per_device(): jnp.einsum('ksrc,kscj->srj', left_env, lax.all_gather(right_part, 'half',...]
    gather x4 -> x0, local copies, waits for them, and re-layouts: 6.81 us -> none  [the longest x1 2.24 us: per_device(): jnp.take(incoming.reshape(sector_count * capacity, half_rows, blk_cols),...]
  transfers between devices with their start and end apart: 4 -> 18, of which waited for: 4 -> 5; matrix products, arithmetic and copies ran while one was open for 0% -> 5% of each run, Pallas kernels for 0% -> 29%
where the time goes in v2:
time: 107 us; the launch traced here: 106 us
  Pallas kernels  37.6 us (35%)
  waiting for transfers between devices  27.9 us (26%)
  starting transfers between devices  19.7 us (18%)
  local copies, waits for them, and re-layouts  10.6 us (10%)
  between operations  7.8 us (7%)
  other arithmetic  2.85 us (3%)
    pallas_call x1, Pallas kernels, four_by_two(): pl.pallas_call(functools.partial(plan_kernel, sizes), out_shape=(jax.Shap...  26.4 us
    ppermute x12, waiting for transfers between devices, swap(): return lax.ppermute(x, axis, [(0, 1), (1, 0)])  23.2 us
    ppermute x12, starting transfers between devices, swap(): return lax.ppermute(x, axis, [(0, 1), (1, 0)])  8.54 us
    pallas_call x1, Pallas kernels, four_by_two(): pl.pallas_call(functools.partial(late_kernel, sizes), out_shape=(jax.Shap...  7.14 us
    unnamed x26, local copies, waits for them, and re-layouts  6.21 us
    ppermute x1, waiting for transfers between devices, four_by_two(): late_end = lax.ppermute(mid, 'sector', [(1, 0), (2, 3)])  4.61 us
    pallas_call x1, Pallas kernels, four_by_two(): pl.pallas_call(functools.partial(early_kernel, sizes), out_shape=jax.Shap...  4.04 us
    ppermute x2, starting transfers between devices, swap_on(): lax.ppermute(x, ('sector', axis), [(2 * s + i, 2 * s + 1 - i) for s in se...  3.32 us
  transfers between devices with their start and end apart: 18, of which 5 were waited for; matrix products, arithmetic and copies ran while one was open for 5% of the time, Pallas kernels for 29%

profile of v2, /device:TPU:0, one launch (start us, length us, event | category | flops | bytes accessed | tf_op | source)
XLA Modules:
  0.0 106.5 jit_solution(9033108541351137048)
XLA Ops:
  0.0 0.5 collective-permute-start.8
  0.5 1.8 %constant_dynamic-slice_fusion.4 = bf16[3,128,512]{2,1,0:T(8,128)(2,1)} fusion(bf16[3,256,512]{2,1,0:T(8,128)(2,1)} %refs_0_.1, s32[]{:T(128)S(6)} %select_n.25), kind=kLoop, calls=%fused_computation.9 | loop fusion | bytes 786436 | tf_op jit(solution)/shard_map/dynamic_slice | solution.py:319
  2.2 2.6 %collective-permute-start.13 = (bf16[3,128,512]{2,1,0:T(8,128)(2,1)}, bf16[3,128,512]{2,1,0:T(8,128)(2,1)S(1)}, u32[]{:S(2)}, u32[]{:S(2)}) collective-permute-start(bf16[3,128,512]{2,1,0:T(8,128)(2,1)} %constant_dynamic-slice_fusion.4), channel_id=1, source_target_pairs={{0,4},{4,0},{8,12},{12,8},{1,5},{5,1},{9,13},{13,9},{2,6},{6,2},{1... | collective-permute-start | bytes 1179656 | tf_op jit(solution)/shard_map/ppermute | solution.py:320
  4.8 2.6 %collective-permute-start = (bf16[3,128,512]{2,1,0:T(8,128)(2,1)}, bf16[3,128,512]{2,1,0:T(8,128)(2,1)}, u32[]{:S(2)}, u32[]{:S(2)}) collective-permute-start(bf16[3,128,512]{2,1,0:T(8,128)(2,1)} %constant_dynamic-slice_fusion.4), channel_id=1, source_target_pairs={{0,8},{4,12},{8,0},{12,4},{1,9},{5,13},{9,1},{13,5},{2,10},{6,14},... | collective-permute-start | bytes 1179656 | tf_op jit(solution)/shard_map/ppermute | solution.py:321
  7.4 0.7 pad_add_fusion.me
  8.0 26.4 %plan.1 = (bf16[2,256,256]{2,1,0:T(8,128)(2,1)}, bf16[2,256,512]{2,1,0:T(8,128)(2,1)}, s32[2,2]{1,0:T(2,128)}) custom-call(s32[3]{0:T(128)} %pad_add_fusion.me, s32[4,12]{1,0:T(4,128)} %source.5, bf16[2,3,256,512]{3,2,1,0:T(8,128)(2,1)} %refs_8_.1, bf16[2,3,256,512]{3,2,1,0:T(8,128)(2,1)} %refs_9_.1), custom_call_target="tpu_custom_call" | custom-call | tf_op jit(solution)/shard_map/plan/pallas_call | solution.py:325
  34.5 0.0 copy-start.11
  34.5 0.0 copy-start.12
  34.5 0.0 copy-start
  34.5 0.0 copy-start.9
  34.6 1.6 %collective-permute-start.9 = (bf16[2,256,256]{2,1,0:T(8,128)(2,1)}, bf16[2,256,256]{2,1,0:T(8,128)(2,1)}, u32[]{:S(2)}, u32[]{:S(2)}) collective-permute-start(bf16[2,256,256]{2,1,0:T(8,128)(2,1)} %get-tuple-element.11), channel_id=1, source_target_pairs={{0,2},{2,0},{1,3},{3,1},{4,6},{6,4},{5,7},{7,5},{8,10},{10,8},{9,1... | collective-permute-start | bytes 786440 | tf_op jit(solution)/shard_map/ppermute | solution.py:300
  36.1 0.5 collective-permute-start.10
  36.6 1.5 %fusion = (s32[1,1]{1,0:T(1,128)}, s32[1,1]{1,0:T(1,128)}, s32[1,1]{1,0:T(1,128)}, s32[1,1]{1,0:T(1,128)}) fusion(s32[2,2]{1,0:T(2,128)} %get-tuple-element.10), kind=kLoop, calls=%fused_computation.13 | loop fusion | bytes 32 | tf_op jit(solution)/shard_map/slice | solution.py:344
  45.7 0.0 collective-permute-done.13.refs_2_
  45.7 1.4 %collective-permute-start.6 = (bf16[3,128,512]{2,1,0:T(8,128)(2,1)}, bf16[3,128,512]{2,1,0:T(8,128)(2,1)}, u32[]{:S(2)}, u32[]{:S(2)}) collective-permute-start(bf16[3,128,512]{2,1,0:T(8,128)(2,1)} %constant_dynamic-slice_fusion.4), channel_id=1, source_target_pairs={{4,8},{8,4},{5,9},{9,5},{6,10},{10,6},{7,11},{11,7},{20,24},{24,20... | collective-permute-start | bytes 1179656 | tf_op jit(solution)/shard_map/ppermute | solution.py:322
  47.1 0.0 collective-permute-done.9.refs_11_
  47.2 0.1 collective-permute-start.12
  47.3 0.0 collective-permute-done.refs_0_
  47.3 1.6 %collective-permute-start.14 = (bf16[2,128,512]{2,1,0:T(8,128)(2,1)S(1)}, bf16[2,128,512]{2,1,0:T(8,128)(2,1)S(1)}, u32[]{:S(2)}, u32[]{:S(2)}) collective-permute-start(bf16[2,128,512]{2,1,0:T(8,128)(2,1)S(1)} %pad_maximum_fusion.1), channel_id=1, source_target_pairs={{0,2},{2,0},{1,3},{3,1},{4,6},{6,4},{5,7},{7,5},{8,10},{10,8},{9,1... | collective-permute-start | bytes 786440 | tf_op jit(solution)/shard_map/ppermute | solution.py:300
  48.8 1.0 constant_dynamic-slice_fusion.3
  49.9 0.0 collective-permute-done.6.refs_6_
  49.9 0.6 collective-permute-start.1
  50.5 4.9 %collective-permute-done.10.refs_12_ = bf16[2,256,512]{2,1,0:T(8,128)(2,1)} collective-permute-done((bf16[2,256,512]{2,1,0:T(8,128)(2,1)}, bf16[2,256,512]{2,1,0:T(8,128)(2,1)}, u32[]{:S(2)}, u32[]{:S(2)}) %collective-permute-start.10) | collective-permute-done | bytes 524320 | tf_op jit(solution)/shard_map/ppermute | solution.py:300
  55.4 5.5 %collective-permute-done.14.refs_3_ = bf16[2,128,512]{2,1,0:T(8,128)(2,1)S(1)} collective-permute-done((bf16[2,128,512]{2,1,0:T(8,128)(2,1)S(1)}, bf16[2,128,512]{2,1,0:T(8,128)(2,1)S(1)}, u32[]{:S(2)}, u32[]{:S(2)}) %collective-permute-start.14) | collective-permute-done | bytes 262176 | tf_op jit(solution)/shard_map/ppermute | solution.py:300
  60.9 1.3 %collective-permute-start.4 = (bf16[3,128,512]{2,1,0:T(8,128)(2,1)}, bf16[3,128,512]{2,1,0:T(8,128)(2,1)}, u32[]{:S(2)}, u32[]{:S(2)}) collective-permute-start(bf16[3,128,512]{2,1,0:T(8,128)(2,1)} %collective-permute-done.refs_0_), channel_id=1, source_target_pairs={{4,0},{8,12},{5,1},{9,13},{6,2},{10,14},{7,3},{11,15},{20,16},{24,... | collective-permute-start | bytes 1179656 | tf_op jit(solution)/shard_map/ppermute | solution.py:323
  62.1 3.4 %collective-permute-done.1.refs_1_ = bf16[2,128,512]{2,1,0:T(8,128)(2,1)} collective-permute-done((bf16[2,128,512]{2,1,0:T(8,128)(2,1)S(1)}, bf16[2,128,512]{2,1,0:T(8,128)(2,1)}, u32[]{:S(2)}, u32[]{:S(2)}) %collective-permute-start.1) | collective-permute-done | bytes 262176 | tf_op jit(solution)/shard_map/ppermute | solution.py:300
  65.6 0.0 collective-permute-start.16
  65.6 0.7 copy-done.5
  66.3 0.7 copy-done.3
  67.0 0.5 collective-permute-start.11
  67.5 0.0 collective-permute-start.2
  67.5 4.6 %collective-permute-done.4.refs_4_ = bf16[3,128,512]{2,1,0:T(8,128)(2,1)} collective-permute-done((bf16[3,128,512]{2,1,0:T(8,128)(2,1)}, bf16[3,128,512]{2,1,0:T(8,128)(2,1)}, u32[]{:S(2)}, u32[]{:S(2)}) %collective-permute-start.4) | collective-permute-done | bytes 393248 | tf_op jit(solution)/shard_map/ppermute | solution.py:323
  72.1 1.4 %collective-permute-start.7 = (bf16[3,128,512]{2,1,0:T(8,128)(2,1)}, bf16[3,128,512]{2,1,0:T(8,128)(2,1)}, u32[]{:S(2)}, u32[]{:S(2)}) collective-permute-start(bf16[3,128,512]{2,1,0:T(8,128)(2,1)} %collective-permute-done.6.refs_6_), channel_id=1, source_target_pairs={{4,5},{5,4},{8,9},{9,8},{6,7},{7,6},{10,11},{11,10},{20,21},{21,20... | collective-permute-start | bytes 1179656 | tf_op jit(solution)/shard_map/ppermute | solution.py:304
  73.6 0.7 copy-done.7
  74.3 1.9 %collective-permute-start.5 = (bf16[3,128,512]{2,1,0:T(8,128)(2,1)}, bf16[3,128,512]{2,1,0:T(8,128)(2,1)}, u32[]{:S(2)}, u32[]{:S(2)}) collective-permute-start(bf16[3,128,512]{2,1,0:T(8,128)(2,1)} %collective-permute-done.4.refs_4_), channel_id=1, source_target_pairs={{0,1},{1,0},{12,13},{13,12},{2,3},{3,2},{14,15},{15,14},{16,17},{1... | collective-permute-start | bytes 1179656 | tf_op jit(solution)/shard_map/ppermute | solution.py:304
  76.2 0.6 collective-permute-start.3
  76.7 0.1 dynamic_slice.22
  76.8 0.1 dynamic_slice.23
  76.9 1.0 copy-done.4
  77.9 0.9 copy-done.6
  78.9 0.9 copy-done.8
  79.8 4.0 %early_slots.1.refs_14_ = f32[3,256,512]{2,1,0:T(8,128)S(1)} custom-call(s32[3]{0:T(128)S(1)} %copy-done.10, s32[4,12]{1,0:T(4,128)S(1)} %copy-done.9, s32[12]{0:T(128)S(1)} %copy-done.11, s32[12]{0:T(128)S(1)} %copy-done.12, bf16[3,256,512]{2,1,0:T(8,128)(2,1)S(1)} %copy-done.2, bf16[3,256,512]{2,1,0:T(8,128)(2,1)S(1)} %collective-permute-done.12.refs_1_, ...), custom_call_target="tpu_custom_call" | custom-call | flops 2000000000 | bytes 8000000 | tf_op jit(solution)/shard_map/early_slots/pallas_call | solution.py:352
  83.9 1.1 %copy-done.1 = f32[3,256,512]{2,1,0:T(8,128)} copy-done((f32[3,256,512]{2,1,0:T(8,128)}, f32[3,256,512]{2,1,0:T(8,128)S(1)}, u32[]{:S(2)}) %copy-start.1) | copy-done | bytes 1572888
  85.0 7.1 %late_slots.1 = (bf16[3,256,256]{2,1,0:T(8,128)(2,1)}, f32[3,256,256]{2,1,0:T(8,128)}) custom-call(s32[3]{0:T(128)} %pad_add_fusion.me, s32[4,12]{1,0:T(4,128)} %source.5, s32[12]{0:T(128)} %left_dims.3, s32[12]{0:T(128)} %right_dims.3, bf16[3,128,512]{2,1,0:T(8,128)(2,1)} %collective-permute-done.refs_0_, ...), custom_call_target="tpu_custom_call" | custom-call | flops 2000000000 | bytes 8000000 | tf_op jit(solution)/shard_map/late_slots/pallas_call | solution.py:367
  92.2 2.7 %collective-permute-start.17 = (bf16[3,256,256]{2,1,0:T(8,128)(2,1)}, bf16[3,256,256]{2,1,0:T(8,128)(2,1)S(1)}, u32[]{:S(2)}, u32[]{:S(2)}) collective-permute-start(bf16[3,256,256]{2,1,0:T(8,128)(2,1)} %get-tuple-element.14), channel_id=1, source_target_pairs={{0,2},{2,0},{1,3},{3,1},{4,6},{6,4},{5,7},{7,5},{8,10},{10,8},{9,1... | collective-permute-start | bytes 1179656 | tf_op jit(solution)/shard_map/ppermute | solution.py:300
  94.9 0.1 broadcast_compare_fusion
  95.0 9.4 %collective-permute-done.17 = bf16[3,256,256]{2,1,0:T(8,128)(2,1)S(1)} collective-permute-done((bf16[3,256,256]{2,1,0:T(8,128)(2,1)}, bf16[3,256,256]{2,1,0:T(8,128)(2,1)S(1)}, u32[]{:S(2)}, u32[]{:S(2)}) %collective-permute-start.17) | collective-permute-done | bytes 393248 | tf_op jit(solution)/shard_map/ppermute | solution.py:300
  104.4 2.1 %select_convert_fusion = bf16[3,256,256]{2,1,0:T(8,128)(2,1)} fusion(f32[3,256,256]{2,1,0:T(8,128)} %get-tuple-element.13, bf16[3,256,256]{2,1,0:T(8,128)(2,1)S(1)} %collective-permute-done.17, pred[3,256]{1,0:T(4,128)(4,1)S(1)} %get-tuple-element.23, pred[3,256]{1,0:T(4,128)(4,1)S(1)} %get-tuple-element.24), kind=kLoop, calls=%fused_computation | loop fusion | flops 983040 | bytes 1574400 | tf_op jit(solution)/shard_map/convert_element_type | solution.py:402
  (30 shorter events, 0.1 us)
Async XLA Ops:
  0.0 76.2 %collective-permute-start.8 = (bf16[2,3,256,512]{3,2,1,0:T(8,128)(2,1)}, bf16[2,3,256,512]{3,2,1,0:T(8,128)(2,1)}, u32[]{:S(2)}, u32[]{:S(2)}) collective-permute-start(bf16[2,3,256,512]{3,2,1,0:T(8,128)(2,1)} %refs_9_.1), channel_id=1, source_target_pairs={{0,1},{1,0},{2,3},{3,2},{4,5},{5,4},{6,7},{7,6},{8,9},{9,8},{10,11... | collective-permute-start | bytes 4718600 | tf_op jit(solution)/shard_map/ppermute | solution.py:300
  2.2 43.5 %collective-permute-start.13 = (bf16[3,128,512]{2,1,0:T(8,128)(2,1)}, bf16[3,128,512]{2,1,0:T(8,128)(2,1)S(1)}, u32[]{:S(2)}, u32[]{:S(2)}) collective-permute-start(bf16[3,128,512]{2,1,0:T(8,128)(2,1)} %constant_dynamic-slice_fusion.4), channel_id=1, source_target_pairs={{0,4},{4,0},{8,12},{12,8},{1,5},{5,1},{9,13},{13,9},{2,6},{6,2},{1... | collective-permute-start | bytes 1179656 | tf_op jit(solution)/shard_map/ppermute | solution.py:320
  4.8 42.5 %collective-permute-start = (bf16[3,128,512]{2,1,0:T(8,128)(2,1)}, bf16[3,128,512]{2,1,0:T(8,128)(2,1)}, u32[]{:S(2)}, u32[]{:S(2)}) collective-permute-start(bf16[3,128,512]{2,1,0:T(8,128)(2,1)} %constant_dynamic-slice_fusion.4), channel_id=1, source_target_pairs={{0,8},{4,12},{8,0},{12,4},{1,9},{5,13},{9,1},{13,5},{2,10},{6,14},... | collective-permute-start | bytes 1179656 | tf_op jit(solution)/shard_map/ppermute | solution.py:321
  8.0 39.1 %copy-start.2 = (bf16[3,256,512]{2,1,0:T(8,128)(2,1)S(1)}, bf16[3,256,512]{2,1,0:T(8,128)(2,1)}, u32[]{:S(2)}) copy-start(bf16[3,256,512]{2,1,0:T(8,128)(2,1)} %refs_0_.1) | copy-start | bytes 2359300
  34.5 42.3 %copy-start.11 = (s32[12]{0:T(128)S(1)}, s32[12]{0:T(128)}, u32[]{:S(2)}) copy-start(s32[12]{0:T(128)} %left_dims.3) | copy-start | bytes 148
  34.5 42.3 %copy-start.12 = (s32[12]{0:T(128)S(1)}, s32[12]{0:T(128)}, u32[]{:S(2)}) copy-start(s32[12]{0:T(128)} %right_dims.3) | copy-start | bytes 148
  34.5 42.4 %copy-start = (bf16[2,3,256,512]{3,2,1,0:T(8,128)(2,1)S(1)}, bf16[2,3,256,512]{3,2,1,0:T(8,128)(2,1)}, u32[]{:S(2)}) copy-start(bf16[2,3,256,512]{3,2,1,0:T(8,128)(2,1)} %refs_8_.1) | copy-start | bytes 4718596
  34.5 42.4 %copy-start.9 = (s32[4,12]{1,0:T(4,128)S(1)}, s32[4,12]{1,0:T(4,128)}, u32[]{:S(2)}) copy-start(s32[4,12]{1,0:T(4,128)} %source.5) | copy-start | bytes 580
  34.5 42.4 %copy-start.10 = (s32[3]{0:T(128)S(1)}, s32[3]{0:T(128)}, u32[]{:S(2)}) copy-start(s32[3]{0:T(128)} %pad_add_fusion.me) | copy-start | bytes 40
  34.6 12.6 %collective-permute-start.9 = (bf16[2,256,256]{2,1,0:T(8,128)(2,1)}, bf16[2,256,256]{2,1,0:T(8,128)(2,1)}, u32[]{:S(2)}, u32[]{:S(2)}) collective-permute-start(bf16[2,256,256]{2,1,0:T(8,128)(2,1)} %get-tuple-element.11), channel_id=1, source_target_pairs={{0,2},{2,0},{1,3},{3,1},{4,6},{6,4},{5,7},{7,5},{8,10},{10,8},{9,1... | collective-permute-start | bytes 786440 | tf_op jit(solution)/shard_map/ppermute | solution.py:300
  36.1 19.2 %collective-permute-start.10 = (bf16[2,256,512]{2,1,0:T(8,128)(2,1)}, bf16[2,256,512]{2,1,0:T(8,128)(2,1)}, u32[]{:S(2)}, u32[]{:S(2)}) collective-permute-start(bf16[2,256,512]{2,1,0:T(8,128)(2,1)} %get-tuple-element.12), channel_id=1, source_target_pairs={{0,2},{2,0},{1,3},{3,1},{4,6},{6,4},{5,7},{7,5},{8,10},{10,8},{9,1... | collective-permute-start | bytes 1572872 | tf_op jit(solution)/shard_map/ppermute | solution.py:300
  45.7 4.2 %collective-permute-start.6 = (bf16[3,128,512]{2,1,0:T(8,128)(2,1)}, bf16[3,128,512]{2,1,0:T(8,128)(2,1)}, u32[]{:S(2)}, u32[]{:S(2)}) collective-permute-start(bf16[3,128,512]{2,1,0:T(8,128)(2,1)} %constant_dynamic-slice_fusion.4), channel_id=1, source_target_pairs={{4,8},{8,4},{5,9},{9,5},{6,10},{10,6},{7,11},{11,7},{20,24},{24,20... | collective-permute-start | bytes 1179656 | tf_op jit(solution)/shard_map/ppermute | solution.py:322
  47.2 20.4 %collective-permute-start.12 = (bf16[3,256,512]{2,1,0:T(8,128)(2,1)S(1)}, bf16[3,256,512]{2,1,0:T(8,128)(2,1)S(1)}, u32[]{:S(2)}, u32[]{:S(2)}) collective-permute-start(bf16[3,256,512]{2,1,0:T(8,128)(2,1)S(1)} %copy-done.2), channel_id=1, source_target_pairs={{0,1},{1,0},{2,3},{3,2},{4,5},{5,4},{6,7},{7,6},{8,9},{9,8},{10,11... | collective-permute-start | bytes 2359304 | tf_op jit(solution)/shard_map/ppermute | solution.py:300
  47.3 13.6 %collective-permute-start.14 = (bf16[2,128,512]{2,1,0:T(8,128)(2,1)S(1)}, bf16[2,128,512]{2,1,0:T(8,128)(2,1)S(1)}, u32[]{:S(2)}, u32[]{:S(2)}) collective-permute-start(bf16[2,128,512]{2,1,0:T(8,128)(2,1)S(1)} %pad_maximum_fusion.1), channel_id=1, source_target_pairs={{0,2},{2,0},{1,3},{3,1},{4,6},{6,4},{5,7},{7,5},{8,10},{10,8},{9,1... | collective-permute-start | bytes 786440 | tf_op jit(solution)/shard_map/ppermute | solution.py:300
  49.9 15.7 %collective-permute-start.1 = (bf16[2,128,512]{2,1,0:T(8,128)(2,1)S(1)}, bf16[2,128,512]{2,1,0:T(8,128)(2,1)}, u32[]{:S(2)}, u32[]{:S(2)}) collective-permute-start(bf16[2,128,512]{2,1,0:T(8,128)(2,1)S(1)} %pad_maximum_fusion), channel_id=1, source_target_pairs={{0,2},{2,0},{1,3},{3,1},{4,6},{6,4},{5,7},{7,5},{8,10},{10,8},{9,1... | collective-permute-start | bytes 786440 | tf_op jit(solution)/shard_map/ppermute | solution.py:300
  55.3 10.9 %collective-permute-start.15 = (bf16[3,128,512]{2,1,0:T(8,128)(2,1)S(1)}, bf16[3,128,512]{2,1,0:T(8,128)(2,1)S(1)}, u32[]{:S(2)}, u32[]{:S(2)}) collective-permute-start(bf16[3,128,512]{2,1,0:T(8,128)(2,1)S(1)} %collective-permute-done.13.refs_2_), channel_id=1, source_target_pairs={{0,1},{1,0},{2,3},{3,2},{4,5},{5,4},{6,7},{7,6},{8,9},{9,8},{10,11... | collective-permute-start | bytes 1179656 | tf_op jit(solution)/shard_map/ppermute | solution.py:300
  60.9 11.3 %collective-permute-start.4 = (bf16[3,128,512]{2,1,0:T(8,128)(2,1)}, bf16[3,128,512]{2,1,0:T(8,128)(2,1)}, u32[]{:S(2)}, u32[]{:S(2)}) collective-permute-start(bf16[3,128,512]{2,1,0:T(8,128)(2,1)} %collective-permute-done.refs_0_), channel_id=1, source_target_pairs={{4,0},{8,12},{5,1},{9,13},{6,2},{10,14},{7,3},{11,15},{20,16},{24,... | collective-permute-start | bytes 1179656 | tf_op jit(solution)/shard_map/ppermute | solution.py:323
  65.6 8.0 %collective-permute-start.16 = (bf16[2,128,512]{2,1,0:T(8,128)(2,1)S(1)}, bf16[2,128,512]{2,1,0:T(8,128)(2,1)S(1)}, u32[]{:S(2)}, u32[]{:S(2)}) collective-permute-start(bf16[2,128,512]{2,1,0:T(8,128)(2,1)S(1)} %collective-permute-done.14.refs_3_), channel_id=1, source_target_pairs={{0,1},{1,0},{2,3},{3,2},{4,5},{5,4},{6,7},{7,6},{8,9},{9,8},{10,11... | collective-permute-start | bytes 786440 | tf_op jit(solution)/shard_map/ppermute | solution.py:300
  65.6 0.7 copy-start.5
  66.3 0.7 copy-start.3
  67.0 18.0 %collective-permute-start.11 = (bf16[2,256,512]{2,1,0:T(8,128)(2,1)}, bf16[2,256,512]{2,1,0:T(8,128)(2,1)}, u32[]{:S(2)}, u32[]{:S(2)}) collective-permute-start(bf16[2,256,512]{2,1,0:T(8,128)(2,1)} %collective-permute-done.10.refs_12_), channel_id=1, source_target_pairs={{0,1},{1,0},{2,3},{3,2},{4,5},{5,4},{6,7},{7,6},{8,9},{9,8},{10,11... | collective-permute-start | bytes 1572872 | tf_op jit(solution)/shard_map/ppermute | solution.py:300
  67.5 17.5 %collective-permute-start.2 = (bf16[3,128,512]{2,1,0:T(8,128)(2,1)}, bf16[3,128,512]{2,1,0:T(8,128)(2,1)}, u32[]{:S(2)}, u32[]{:S(2)}) collective-permute-start(bf16[3,128,512]{2,1,0:T(8,128)(2,1)} %collective-permute-done.refs_0_), channel_id=1, source_target_pairs={{0,1},{1,0},{2,3},{3,2},{4,5},{5,4},{6,7},{7,6},{8,9},{9,8},{10,11... | collective-permute-start | bytes 1179656 | tf_op jit(solution)/shard_map/ppermute | solution.py:300
  72.1 12.9 %collective-permute-start.7 = (bf16[3,128,512]{2,1,0:T(8,128)(2,1)}, bf16[3,128,512]{2,1,0:T(8,128)(2,1)}, u32[]{:S(2)}, u32[]{:S(2)}) collective-permute-start(bf16[3,128,512]{2,1,0:T(8,128)(2,1)} %collective-permute-done.6.refs_6_), channel_id=1, source_target_pairs={{4,5},{5,4},{8,9},{9,8},{6,7},{7,6},{10,11},{11,10},{20,21},{21,20... | collective-permute-start | bytes 1179656 | tf_op jit(solution)/shard_map/ppermute | solution.py:304
  73.6 0.7 copy-start.7
  74.3 10.8 %collective-permute-start.5 = (bf16[3,128,512]{2,1,0:T(8,128)(2,1)}, bf16[3,128,512]{2,1,0:T(8,128)(2,1)}, u32[]{:S(2)}, u32[]{:S(2)}) collective-permute-start(bf16[3,128,512]{2,1,0:T(8,128)(2,1)} %collective-permute-done.4.refs_4_), channel_id=1, source_target_pairs={{0,1},{1,0},{12,13},{13,12},{2,3},{3,2},{14,15},{15,14},{16,17},{1... | collective-permute-start | bytes 1179656 | tf_op jit(solution)/shard_map/ppermute | solution.py:304
  76.2 8.8 %collective-permute-start.3 = (bf16[2,128,512]{2,1,0:T(8,128)(2,1)}, bf16[2,128,512]{2,1,0:T(8,128)(2,1)}, u32[]{:S(2)}, u32[]{:S(2)}) collective-permute-start(bf16[2,128,512]{2,1,0:T(8,128)(2,1)} %collective-permute-done.1.refs_1_), channel_id=1, source_target_pairs={{0,1},{1,0},{2,3},{3,2},{4,5},{5,4},{6,7},{7,6},{8,9},{9,8},{10,11... | collective-permute-start | bytes 786440 | tf_op jit(solution)/shard_map/ppermute | solution.py:300
  76.9 1.0 copy-start.4
  77.9 0.9 copy-start.6
  78.9 0.9 copy-start.8
  83.9 1.1 %copy-start.1 = (f32[3,256,512]{2,1,0:T(8,128)}, f32[3,256,512]{2,1,0:T(8,128)S(1)}, u32[]{:S(2)}) copy-start(f32[3,256,512]{2,1,0:T(8,128)S(1)} %early_slots.1.refs_14_) | copy-start | bytes 4718596
  92.2 12.2 %collective-permute-start.17 = (bf16[3,256,256]{2,1,0:T(8,128)(2,1)}, bf16[3,256,256]{2,1,0:T(8,128)(2,1)S(1)}, u32[]{:S(2)}, u32[]{:S(2)}) collective-permute-start(bf16[3,256,256]{2,1,0:T(8,128)(2,1)} %get-tuple-element.14), channel_id=1, source_target_pairs={{0,2},{2,0},{1,3},{3,1},{4,6},{6,4},{5,7},{7,5},{8,10},{10,8},{9,1... | collective-permute-start | bytes 1179656 | tf_op jit(solution)/shard_map/ppermute | solution.py:300

commit v3 on v0

--- a/solution.py
+++ b/solution.py
@@ -1,10 +1,18 @@
+import functools
+
 import jax
 import jax.numpy as jnp
 from jax import lax
+from jax.experimental import pallas as pl
+from jax.experimental.pallas import tpu as pltpu
 from jax.sharding import PartitionSpec as P
 
-
-def per_device(wavefunction, left_env, right_env, source, left_dims, right_dims):
+BF16 = jnp.bfloat16
+F32 = jnp.float32
+VMEM_LIMIT = 16 * 1024 * 1024
+
+
+def general(wavefunction, left_env, right_env, source, left_dims, right_dims):
     sec_local, half_rows, blk_cols = wavefunction.shape
     pair_local = left_env.shape[0]
     needed = pair_local * sec_local
@@ -54,14 +62,14 @@
         "nab,ncb->nac",
         lax.all_gather(fetched, "half", axis=1, tiled=True),
         right_rows,
-        preferred_element_type=jnp.float32,
-    ).astype(jnp.bfloat16)
+        preferred_element_type=F32,
+    ).astype(BF16)
     right_part = right_part.reshape(pair_local, sec_local, right_part.shape[1], right_part.shape[2])
     partial_sum = jnp.einsum(
         "ksrc,kscj->srj",
         left_env,
         lax.all_gather(right_part, "half", axis=3, tiled=True),
-        preferred_element_type=jnp.float32,
+        preferred_element_type=F32,
     )
     summed = lax.psum_scatter(partial_sum, "op", scatter_dimension=2, tiled=True)
     col_width = summed.shape[2]
@@ -69,12 +77,279 @@
     out_mask = (row_ids[None, :, None] < left_live[:, None, None]) & (
         out_cols[None, None, :] < right_live[:, None, None]
     )
-    return jnp.where(out_mask, summed, jnp.zeros((), jnp.float32)).astype(jnp.bfloat16)
+    return jnp.where(out_mask, summed, jnp.zeros((), F32)).astype(BF16)
+
+
+def place():
+    return lax.axis_index("sector"), lax.axis_index("op"), lax.axis_index("half")
+
+
+def slots_of(sizes, source, z, op):
+    pairs, secs = sizes[:2]
+    found = []
+    for n in range(pairs * secs):
+        src = source[op * pairs + n // secs, z * secs + n % secs]
+        holder = src // secs
+        found.append((holder ^ z, src - holder * secs, src))
+    return found
+
+
+def ranked(slots, kind, rank):
+    slot, local, source = jnp.int32(-1), jnp.int32(0), jnp.int32(0)
+    seen = jnp.int32(0)
+    for n, (k, b, s) in enumerate(slots):
+        hit = (k == kind) & (seen == rank)
+        slot = jnp.where(hit, n, slot)
+        local = jnp.where(hit, b, local)
+        source = jnp.where(hit, s, source)
+        seen = seen + (k == kind).astype(jnp.int32)
+    return slot, local, source
+
+
+def split_kernel(sizes, source, own, share, near_out):
+    half_rows = sizes[2]
+    quarter = half_rows // 2
+    z, o, _ = place()
+    share[...] = own[:, pl.ds(pl.multiple_of(o * quarter, quarter), quarter)]
+    theirs = slots_of(sizes, source, z ^ 1, o)
+    for j in range(2):
+        near_out[j] = own[ranked(theirs, 1, j)[1]]
+
+
+def lend_kernel(sizes, source, left, right, left_out, right_out):
+    pairs, secs, half_rows, blk = sizes
+    quarter = half_rows // 2
+    z, o, _ = place()
+    mine = slots_of(sizes, source, z, o)
+    for j in range(2):
+        n = jnp.maximum(ranked(mine, 3, j)[0], 0)
+        k, t = n // secs, n % secs
+        right_out[j] = right[k, t]
+        for part in range(2):
+            first = pl.multiple_of(part * half_rows + (1 - o) * quarter, quarter)
+            left_out[j, :, part * quarter : (part + 1) * quarter] = left[k, t, :, pl.ds(first, quarter)]
+
+
+def pick_kernel(sizes, source, mid, picked):
+    z, o, _ = place()
+    theirs = slots_of(sizes, source, z, 1 - o)
+    for j in range(2):
+        picked[j] = mid[ranked(theirs, 2, j)[1]]
+
+
+def live_columns(sizes, right_dims, src):
+    col = lax.broadcasted_iota(jnp.int32, (1, sizes[3]), 1)
+    return (col < right_dims[src]).astype(F32).astype(BF16)
+
+
+def times_right(sizes, m, rights, row, left_live, out):
+    half_rows = sizes[2]
+    for c, r in enumerate(rights):
+        part = lax.dot_general(m, r, (((1,), (1,)), ((), ())), preferred_element_type=F32)
+        out[:, c * half_rows : (c + 1) * half_rows] = jnp.where(row < left_live, part, 0.0).astype(BF16)
+
+
+def early_kernel(sizes, source, left_dims, right_dims, own, own_far, near, near_far, left, right, right_far, acc, m_buf, rp_buf):
+    pairs, secs, half_rows, blk = sizes
+    z, o, h = place()
+    slots = slots_of(sizes, source, z, o)
+    mine = pl.ds(pl.multiple_of(h * half_rows, half_rows), half_rows)
+    far = pl.ds(pl.multiple_of((1 - h) * half_rows, half_rows), half_rows)
+    acc[...] = jnp.zeros_like(acc)
+    rank = jnp.int32(0)
+    for n, (kind, local, src) in enumerate(slots):
+        k, t = n // secs, n % secs
+        live = live_columns(sizes, right_dims, src)
+
+        @pl.when(kind == 0)
+        def _():
+            m_buf[mine] = own[local] * live
+            m_buf[far] = own_far[local] * live
+
+        @pl.when(kind == 1)
+        def _(rank=rank):
+            m_buf[mine] = near[rank] * live
+            m_buf[far] = near_far[rank] * live
+
+        @pl.when(kind <= 1)
+        def _():
+            row = lax.broadcasted_iota(jnp.int32, (blk, 1), 0)
+            times_right(sizes, m_buf[...], (right[k, t], right_far[k, t]), row, left_dims[src], rp_buf)
+            acc[t] += jnp.dot(left[k, t], rp_buf[...], preferred_element_type=F32)
+
+        rank = rank + (kind == 1).astype(jnp.int32)
+
+
+def late_kernel(
+    sizes, source, left_dims, right_dims, mid, mid_x, mid_far, mid_x_far, end, end_far, inner, inner_far,
+    left, right, right_far, left_x, right_x, right_x_far, early, total, send, keep, m_buf, rp_buf,
+):
+    pairs, secs, half_rows, blk = sizes
+    quarter = half_rows // 2
+    z, o, h = place()
+    is_end = (z == 0) | (z == 3)
+    mine = slots_of(sizes, source, z, o)
+    theirs = slots_of(sizes, source, z, 1 - o)
+
+    def rows(first):
+        return pl.ds(pl.multiple_of(first, quarter), quarter)
+
+    for j in range(2):
+        n, local, src = ranked(mine, 2, j)
+
+        @pl.when(n >= 0)
+        def _():
+            k, t = n // secs, n % secs
+            live = live_columns(sizes, right_dims, src)
+            m_buf[rows(h * half_rows + o * quarter)] = mid[local] * live
+            m_buf[rows(h * half_rows + (1 - o) * quarter)] = mid_x[j] * live
+            m_buf[rows((1 - h) * half_rows + o * quarter)] = mid_far[local] * live
+            m_buf[rows((1 - h) * half_rows + (1 - o) * quarter)] = mid_x_far[j] * live
+            row = lax.broadcasted_iota(jnp.int32, (blk, 1), 0)
+            times_right(sizes, m_buf[...], (right[k, t], right_far[k, t]), row, left_dims[src], rp_buf)
+            total[t] += jnp.dot(left[k, t], rp_buf[...], preferred_element_type=F32)
+
+    at = lax.broadcasted_iota(jnp.int32, (half_rows, 1), 0)
+    row = at + o * quarter + jnp.where(at < quarter, 0, quarter)
+    for i in range(4):
+        j = i % 2
+        n, local, src = ranked(mine if i < 2 else theirs, 3, j)
+
+        @pl.when(n >= 0)
+        def _():
+            k, t = n // secs, n % secs
+            live = live_columns(sizes, right_dims, src)
+
+            @pl.when(is_end)
+            def _():
+                m_buf[rows(h * quarter)] = end[local] * live
+                m_buf[rows((1 - h) * quarter)] = end_far[local] * live
+
+            @pl.when(jnp.logical_not(is_end))
+            def _():
+                m_buf[rows(h * quarter)] = inner[local] * live
+                m_buf[rows((1 - h) * quarter)] = inner_far[local] * live
+
+            if i < 2:
+                rights = (right[k, t], right_far[k, t])
+                l = jnp.concatenate([left[k, t, :, rows(p * half_rows + o * quarter)] for p in range(2)], axis=1)
+            else:
+                rights = (right_x[j], right_x_far[j])
+                l = left_x[j]
+            times_right(sizes, m_buf[:half_rows], rights, row, left_dims[src], rp_buf.at[:half_rows])
+            total[t] += jnp.dot(l, rp_buf[:half_rows], preferred_element_type=F32)
+
+    first = pl.multiple_of((h ^ o) * half_rows, half_rows)
+    other = pl.multiple_of((1 - (h ^ o)) * half_rows, half_rows)
+    keep[...] = total[:, :, pl.ds(first, half_rows)]
+    send[...] = total[:, :, pl.ds(other, half_rows)].astype(BF16)
+
+
+def join_kernel(sizes, left_dims, right_dims, keep, received, out):
+    secs, half_rows, blk = sizes[1:]
+    z, o, h = place()
+    row = h * half_rows + lax.broadcasted_iota(jnp.int32, (half_rows, 1), 0)
+    col = o * half_rows + lax.broadcasted_iota(jnp.int32, (1, half_rows), 1)
+    for t in range(secs):
+        live = (row < left_dims[z * secs + t]) & (col < right_dims[z * secs + t])
+        out[t] = jnp.where(live, keep[t] + received[t].astype(F32), 0.0).astype(BF16)
+
+
+def swap(x, axis):
+    return lax.ppermute(x, axis, [(0, 1), (1, 0)])
+
+
+def swap_on(x, axis, sectors):
+    return lax.ppermute(x, ("sector", axis), [(2 * s + i, 2 * s + 1 - i) for s in sectors for i in range(2)])
+
+
+def four_by_two(wavefunction, left_env, right_env, source, left_dims, right_dims):
+    secs, half_rows, blk = wavefunction.shape
+    pairs = left_env.shape[0]
+    quarter = half_rows // 2
+    sizes = (pairs, secs, half_rows, blk)
+
+    def call(kernel, outs, scalars, arrays, scratch=(), flops=0, **options):
+        shapes = [jax.ShapeDtypeStruct(shape, dtype) for shape, dtype in outs]
+        nbytes = sum(s.size * s.dtype.itemsize for s in [*shapes, *arrays])
+        return pl.pallas_call(
+            functools.partial(kernel, sizes),
+            out_shape=shapes,
+            in_specs=[pl.BlockSpec(memory_space=pltpu.SMEM)] * len(scalars)
+            + [pl.BlockSpec(memory_space=pltpu.VMEM)] * len(arrays),
+            out_specs=[pl.BlockSpec(memory_space=pltpu.VMEM)] * len(shapes),
+            scratch_shapes=scratch,
+            compiler_params=pltpu.CompilerParams(vmem_limit_bytes=VMEM_LIMIT),
+            cost_estimate=pl.CostEstimate(flops=flops, bytes_accessed=nbytes, transcendentals=0),
+            name=kernel.__name__,
+            **options,
+        )(*scalars, *arrays)
+
+    dims = (source, left_dims, right_dims)
+    share, near_out = call(
+        split_kernel,
+        [((secs, quarter, blk), BF16), ((2, half_rows, blk), BF16)],
+        (source,),
+        (wavefunction,),
+    )
+    mid = lax.ppermute(share, "sector", [(i, i ^ 2) for i in range(4)])
+    near = lax.ppermute(near_out, "sector", [(i, i ^ 1) for i in range(4)])
+    left_out, right_out = call(
+        lend_kernel,
+        [((2, half_rows, half_rows), BF16), ((2, half_rows, blk), BF16)],
+        (source,),
+        (left_env, right_env),
+    )
+    right_x = swap(right_out, "op")
+    left_x = swap(left_out, "op")
+    inner = lax.ppermute(share, "sector", [(1, 2), (2, 1)])
+    end = lax.ppermute(mid, "sector", [(1, 0), (2, 3)])
+    own_far = swap(wavefunction, "half")
+    right_far = swap(right_env, "half")
+    near_far = swap(near, "half")
+    (picked,) = call(pick_kernel, [((2, quarter, blk), BF16)], (source,), (mid,))
+    mid_x = swap(picked, "op")
+    buffers = [pltpu.VMEM((blk, blk), BF16), pltpu.VMEM((blk, blk), BF16)]
+    (early,) = call(
+        early_kernel,
+        [((secs, half_rows, blk), F32)],
+        dims,
+        (wavefunction, own_far, near, near_far, left_env, right_env, right_far),
+        buffers,
+        flops=4 * 3 * half_rows * blk * blk * 2,
+    )
+    arrays = (
+        mid, mid_x, swap(mid, "half"), swap(mid_x, "half"),
+        end, swap_on(end, "half", (0, 3)), inner, swap_on(inner, "half", (1, 2)),
+        left_env, right_env, right_far, left_x, right_x, swap(right_x, "half"), early,
+    )
+    _, send, keep = call(
+        late_kernel,
+        [
+            ((secs, half_rows, blk), F32),
+            ((secs, half_rows, half_rows), BF16),
+            ((secs, half_rows, half_rows), F32),
+        ],
+        dims,
+        arrays,
+        buffers,
+        flops=4 * 3 * half_rows * blk * blk * 2,
+        input_output_aliases={len(dims) + len(arrays) - 1: 0},
+    )
+    (out,) = call(
+        join_kernel,
+        [((secs, half_rows, half_rows), BF16)],
+        (left_dims, right_dims),
+        (keep, swap(send, "op")),
+    )
+    return out
 
 
 def solution(mesh):
+    shape = mesh.shape
+    fits = (shape["sector"], shape["op"], shape["half"]) == (4, 2, 2)
     return jax.shard_map(
-        per_device,
+        four_by_two if fits else general,
         mesh=mesh,
         in_specs=(
             P(("group", "sector"), "half", None),

time: 145 us -> 71 us (0.49)
  waiting for transfers between devices: 100 us -> 40.5 us
  between operations: 13.2 us -> 0.18 us
  Pallas kernels: 0 us -> 10.2 us
  starting transfers between devices: 6.4 us -> 15.1 us
  other arithmetic: 7.04 us -> 0 us
  matrix products: 6.96 us -> 0 us
  local copies, waits for them, and re-layouts: 10.6 us -> 4.64 us
    all_to_all x1 -> x0, waiting for transfers between devices: 48 us -> none  [per_device(): lax.all_to_all(outgoing, 'sector', split_axis=0, concat_axis=0, tiled=True)]
    ppermute x0 -> x16, waiting for transfers between devices: none -> 40.5 us  [the longest x10 23.7 us: swap(): return lax.ppermute(x, axis, [(0, 1), (1, 0)])]
    reduce_scatter x1 -> x0, waiting for transfers between devices: 27.3 us -> none  [per_device(): lax.psum_scatter(partial_sum, 'op', scatter_dimension=2, tiled=True)]
    all_gather x2 -> x0, waiting for transfers between devices: 24.7 us -> none  [the longest x1 13.4 us: per_device(): lax.all_gather(right_part, 'half', axis=3, tiled=True)]
    ppermute x0 -> x16, starting transfers between devices: none -> 15.1 us  [the longest x10 4.83 us: swap(): return lax.ppermute(x, axis, [(0, 1), (1, 0)])]
    pallas_call x0 -> x6, Pallas kernels: none -> 10.2 us  [call(): pl.pallas_call(functools.partial(kernel, sizes), out_shape=shapes, in_spe...]
    dot_general x2 -> x0, matrix products: 6.96 us -> none  [the longest x1 4.06 us: per_device(): jnp.einsum('ksrc,kscj->srj', left_env, lax.all_gather(right_part, 'half',...]
    gather x4 -> x0, local copies, waits for them, and re-layouts: 6.81 us -> none  [the longest x1 2.24 us: per_device(): jnp.take(incoming.reshape(sector_count * capacity, half_rows, blk_cols),...]
  transfers between devices with their start and end apart: 4 -> 16, of which waited for: 4 -> 6; matrix products, arithmetic and copies ran while one was open for 0% -> 0% of each run, Pallas kernels for 0% -> 7%
where the time goes in v3:
time: 71 us; the launch traced here: 70.6 us
  waiting for transfers between devices  40.5 us (57%)
  starting transfers between devices  15.1 us (21%)
  Pallas kernels  10.2 us (14%)
  local copies, waits for them, and re-layouts  4.64 us (7%)
    ppermute x10, waiting for transfers between devices, swap(): return lax.ppermute(x, axis, [(0, 1), (1, 0)])  23.7 us
    pallas_call x6, Pallas kernels, call(): pl.pallas_call(functools.partial(kernel, sizes), out_shape=shapes, in_spe...  10.2 us
    ppermute x1, waiting for transfers between devices, four_by_two(): near = lax.ppermute(near_out, 'sector', [(i, i ^ 1) for i in range(4)])  7.15 us
    ppermute x1, waiting for transfers between devices, four_by_two(): mid = lax.ppermute(share, 'sector', [(i, i ^ 2) for i in range(4)])  5.55 us
    ppermute x10, starting transfers between devices, swap(): return lax.ppermute(x, axis, [(0, 1), (1, 0)])  4.83 us
    unnamed x16, local copies, waits for them, and re-layouts  4.64 us
    ppermute x1, waiting for transfers between devices, four_by_two(): end = lax.ppermute(mid, 'sector', [(1, 0), (2, 3)])  4.08 us
    ppermute x1, starting transfers between devices, four_by_two(): mid = lax.ppermute(share, 'sector', [(i, i ^ 2) for i in range(4)])  3.65 us
  transfers between devices with their start and end apart: 16, of which 6 were waited for; matrix products, arithmetic and copies ran while one was open for 0% of the time, Pallas kernels for 7%

profile of v3, /device:TPU:0, one launch (start us, length us, event | category | flops | bytes accessed | tf_op | source)
XLA Modules:
  0.0 70.6 jit_solution(7807586454946810934)
XLA Ops:
  0.0 0.5 collective-permute-start.8
  0.5 1.1 %copy-done.3 = bf16[3,256,512]{2,1,0:T(8,128)(2,1)S(1)} copy-done((bf16[3,256,512]{2,1,0:T(8,128)(2,1)S(1)}, bf16[3,256,512]{2,1,0:T(8,128)(2,1)}, u32[]{:S(2)}) %copy-start.3) | copy-done | bytes 786456
  1.6 0.0 copy-start.5
  1.6 0.7 copy-done.5
  2.3 0.7 split_kernel.1
  2.9 3.7 %collective-permute-start = (bf16[3,128,512]{2,1,0:T(8,128)(2,1)S(1)}, bf16[3,128,512]{2,1,0:T(8,128)(2,1)S(1)}, u32[]{:S(2)}, u32[]{:S(2)}) collective-permute-start(bf16[3,128,512]{2,1,0:T(8,128)(2,1)S(1)} %get-tuple-element.11), channel_id=1, source_target_pairs={{0,8},{4,12},{8,0},{12,4},{1,9},{5,13},{9,1},{13,5},{2,10},{6,14},... | collective-permute-start | bytes 1179656 | tf_op jit(solution)/shard_map/ppermute | solution.py:295
  6.6 0.0 copy-start
  6.6 1.4 %copy-done = bf16[2,3,256,512]{3,2,1,0:T(8,128)(2,1)S(1)} copy-done((bf16[2,3,256,512]{3,2,1,0:T(8,128)(2,1)S(1)}, bf16[2,3,256,512]{3,2,1,0:T(8,128)(2,1)}, u32[]{:S(2)}) %copy-start) | copy-done | bytes 1572888
  8.0 1.4 %copy-done.2 = bf16[2,3,256,512]{3,2,1,0:T(8,128)(2,1)S(1)} copy-done((bf16[2,3,256,512]{3,2,1,0:T(8,128)(2,1)S(1)}, bf16[2,3,256,512]{3,2,1,0:T(8,128)(2,1)}, u32[]{:S(2)}) %copy-start.2) | copy-done | bytes 1572888
  9.4 0.7 %lend_kernel.1 = (bf16[2,256,256]{2,1,0:T(8,128)(2,1)S(1)}, bf16[2,256,512]{2,1,0:T(8,128)(2,1)S(1)}) custom-call(s32[4,12]{1,0:T(4,128)S(1)} %copy-done.5, bf16[2,3,256,512]{3,2,1,0:T(8,128)(2,1)S(1)} %copy-done, bf16[2,3,256,512]{3,2,1,0:T(8,128)(2,1)S(1)} %copy-done.2), custom_call_target="tpu_custom_call" | custom-call | bytes 3932160 | tf_op jit(solution)/shard_map/lend_kernel/pallas_call | solution.py:275
  10.2 1.6 %collective-permute-start.9 = (bf16[2,256,256]{2,1,0:T(8,128)(2,1)S(1)}, bf16[2,256,256]{2,1,0:T(8,128)(2,1)S(1)}, u32[]{:S(2)}, u32[]{:S(2)}) collective-permute-start(bf16[2,256,256]{2,1,0:T(8,128)(2,1)S(1)} %get-tuple-element.12), channel_id=1, source_target_pairs={{0,2},{2,0},{1,3},{3,1},{4,6},{6,4},{5,7},{7,5},{8,10},{10,8},{9,1... | collective-permute-start | bytes 786440 | tf_op jit(solution)/shard_map/ppermute | solution.py:259
  11.7 1.6 %collective-permute-start.13 = (bf16[2,256,512]{2,1,0:T(8,128)(2,1)S(1)}, bf16[2,256,512]{2,1,0:T(8,128)(2,1)S(1)}, u32[]{:S(2)}, u32[]{:S(2)}) collective-permute-start(bf16[2,256,512]{2,1,0:T(8,128)(2,1)S(1)} %get-tuple-element.14), channel_id=1, source_target_pairs={{0,4},{4,0},{8,12},{12,8},{1,5},{5,1},{9,13},{13,9},{2,6},{6,2},{1... | collective-permute-start | bytes 1572872 | tf_op jit(solution)/shard_map/ppermute | solution.py:296
  13.3 0.5 collective-permute-start.10
  13.8 5.5 %collective-permute-done.9.left_x = bf16[2,256,256]{2,1,0:T(8,128)(2,1)S(1)} collective-permute-done((bf16[2,256,256]{2,1,0:T(8,128)(2,1)S(1)}, bf16[2,256,256]{2,1,0:T(8,128)(2,1)S(1)}, u32[]{:S(2)}, u32[]{:S(2)}) %collective-permute-start.9) | collective-permute-done | bytes 262176 | tf_op jit(solution)/shard_map/ppermute | solution.py:259
  19.4 0.0 copy-done.4
  19.4 0.0 collective-permute-start.12
  19.4 5.6 %collective-permute-done.mid = bf16[3,128,512]{2,1,0:T(8,128)(2,1)S(1)} collective-permute-done((bf16[3,128,512]{2,1,0:T(8,128)(2,1)S(1)}, bf16[3,128,512]{2,1,0:T(8,128)(2,1)S(1)}, u32[]{:S(2)}, u32[]{:S(2)}) %collective-permute-start) | collective-permute-done | bytes 393248 | tf_op jit(solution)/shard_map/ppermute | solution.py:295
  24.9 0.7 collective-permute-start.6
  25.6 7.2 %collective-permute-done.13.near = bf16[2,256,512]{2,1,0:T(8,128)(2,1)S(1)} collective-permute-done((bf16[2,256,512]{2,1,0:T(8,128)(2,1)S(1)}, bf16[2,256,512]{2,1,0:T(8,128)(2,1)S(1)}, u32[]{:S(2)}, u32[]{:S(2)}) %collective-permute-start.13) | collective-permute-done | bytes 524320 | tf_op jit(solution)/shard_map/ppermute | solution.py:296
  32.8 0.0 collective-permute-start.14
  32.8 0.7 pick_kernel.1
  33.4 0.0 collective-permute-done.6.inner
  33.4 1.3 %collective-permute-start.4 = (bf16[3,128,512]{2,1,0:T(8,128)(2,1)S(1)}, bf16[3,128,512]{2,1,0:T(8,128)(2,1)S(1)}, u32[]{:S(2)}, u32[]{:S(2)}) collective-permute-start(bf16[3,128,512]{2,1,0:T(8,128)(2,1)S(1)} %collective-permute-done.mid), channel_id=1, source_target_pairs={{4,0},{8,12},{5,1},{9,13},{6,2},{10,14},{7,3},{11,15},{20,16},{24,... | collective-permute-start | bytes 1179656 | tf_op jit(solution)/shard_map/ppermute | solution.py:306
  34.7 0.0 collective-permute-done.10.right_x
  34.7 0.6 collective-permute-start.1
  35.4 8.1 %collective-permute-done.1.mid_x = bf16[2,128,512]{2,1,0:T(8,128)(2,1)S(1)} collective-permute-done((bf16[2,128,512]{2,1,0:T(8,128)(2,1)S(1)}, bf16[2,128,512]{2,1,0:T(8,128)(2,1)S(1)}, u32[]{:S(2)}, u32[]{:S(2)}) %collective-permute-start.1) | collective-permute-done | bytes 262176 | tf_op jit(solution)/shard_map/ppermute | solution.py:259
  43.5 0.0 collective-permute-start.11
  43.5 0.0 collective-permute-done.12.own_far
  43.5 0.7 collective-permute-start.7
  44.2 4.1 %collective-permute-done.4.end = bf16[3,128,512]{2,1,0:T(8,128)(2,1)S(1)} collective-permute-done((bf16[3,128,512]{2,1,0:T(8,128)(2,1)S(1)}, bf16[3,128,512]{2,1,0:T(8,128)(2,1)S(1)}, u32[]{:S(2)}, u32[]{:S(2)}) %collective-permute-start.4) | collective-permute-done | bytes 393248 | tf_op jit(solution)/shard_map/ppermute | solution.py:306
  48.3 0.0 collective-permute-start.2
  48.3 0.0 collective-permute-done.14.near_far
  48.3 2.4 %collective-permute-start.5 = (bf16[3,128,512]{2,1,0:T(8,128)(2,1)S(1)}, bf16[3,128,512]{2,1,0:T(8,128)(2,1)S(1)}, u32[]{:S(2)}, u32[]{:S(2)}) collective-permute-start(bf16[3,128,512]{2,1,0:T(8,128)(2,1)S(1)} %collective-permute-done.4.end), channel_id=1, source_target_pairs={{0,1},{1,0},{12,13},{13,12},{2,3},{3,2},{14,15},{15,14},{16,17},{1... | collective-permute-start | bytes 1179656 | tf_op jit(solution)/shard_map/ppermute | solution.py:263
  50.7 0.0 collective-permute-done.8.right_far
  50.7 0.1 collective-permute-start.3
  50.8 0.0 copy-done.1
  50.8 0.0 copy-done.6
  50.8 0.0 copy-done.7
  50.8 2.9 %early_kernel.1.early = f32[3,256,512]{2,1,0:T(8,128)S(1)} custom-call(s32[4,12]{1,0:T(4,128)S(1)} %copy-done.5, s32[12]{0:T(128)S(1)} %copy-done.6, s32[12]{0:T(128)S(1)} %copy-done.7, bf16[3,256,512]{2,1,0:T(8,128)(2,1)S(1)} %copy-done.4, bf16[3,256,512]{2,1,0:T(8,128)(2,1)S(1)} %collective-permute-done.12.own_far, ...), custom_call_target="tpu_custom_call" | custom-call | flops 1610612736 | bytes 8912896 | tf_op jit(solution)/shard_map/early_kernel/pallas_call | solution.py:275
  53.8 0.0 collective-permute-done.7.inner_far
  53.8 0.0 collective-permute-done.2.mid_far
  53.8 0.0 collective-permute-done.3.mid_x_far
  53.8 0.0 collective-permute-done.11.right_x_far
  53.8 0.0 collective-permute-done.5.end_far
  53.8 3.8 %late_kernel.1 = (f32[3,256,512]{2,1,0:T(8,128)S(1)}, bf16[3,256,256]{2,1,0:T(8,128)(2,1)S(1)}, f32[3,256,256]{2,1,0:T(8,128)S(1)}) custom-call(s32[4,12]{1,0:T(4,128)S(1)} %copy-done.5, s32[12]{0:T(128)S(1)} %copy-done.6, s32[12]{0:T(128)S(1)} %copy-done.7, bf16[3,128,512]{2,1,0:T(8,128)(2,1)S(1)} %collective-permute-done.mid, ...), custom_call_target="tpu_custom_call", output_to_operand_aliasing={{0}: (17, {})} | custom-call | flops 1610612736 | bytes 13238272 | tf_op jit(solution)/shard_map/late_kernel/pallas_call | solution.py:275
  57.7 1.5 %collective-permute-start.15 = (bf16[3,256,256]{2,1,0:T(8,128)(2,1)S(1)}, bf16[3,256,256]{2,1,0:T(8,128)(2,1)S(1)}, u32[]{:S(2)}, u32[]{:S(2)}) collective-permute-start(bf16[3,256,256]{2,1,0:T(8,128)(2,1)S(1)} %get-tuple-element.16), channel_id=1, source_target_pairs={{0,2},{2,0},{1,3},{3,1},{4,6},{6,4},{5,7},{7,5},{8,10},{10,8},{9,1... | collective-permute-start | bytes 1179656 | tf_op jit(solution)/shard_map/ppermute | solution.py:259
  59.2 10.0 %collective-permute-done.15.received = bf16[3,256,256]{2,1,0:T(8,128)(2,1)S(1)} collective-permute-done((bf16[3,256,256]{2,1,0:T(8,128)(2,1)S(1)}, bf16[3,256,256]{2,1,0:T(8,128)(2,1)S(1)}, u32[]{:S(2)}, u32[]{:S(2)}) %collective-permute-start.15) | collective-permute-done | bytes 393248 | tf_op jit(solution)/shard_map/ppermute | solution.py:259
  69.2 1.4 %join_kernel.1 = bf16[3,256,256]{2,1,0:T(8,128)(2,1)} custom-call(s32[12]{0:T(128)S(1)} %copy-done.6, s32[12]{0:T(128)S(1)} %copy-done.7, f32[3,256,256]{2,1,0:T(8,128)S(1)} %get-tuple-element.15.keep, bf16[3,256,256]{2,1,0:T(8,128)(2,1)S(1)} %collective-permute-done.15.received), custom_call_target="tpu_custom_call" | custom-call | bytes 1572864 | tf_op jit(solution)/shard_map/join_kernel/pallas_call | solution.py:275
  (6 shorter events, 0.0 us)
Async XLA Ops:
  0.0 50.7 %collective-permute-start.8 = (bf16[2,3,256,512]{3,2,1,0:T(8,128)(2,1)}, bf16[2,3,256,512]{3,2,1,0:T(8,128)(2,1)S(1)}, u32[]{:S(2)}, u32[]{:S(2)}) collective-permute-start(bf16[2,3,256,512]{3,2,1,0:T(8,128)(2,1)} %right.5), channel_id=1, source_target_pairs={{0,1},{1,0},{2,3},{3,2},{4,5},{5,4},{6,7},{7,6},{8,9},{9,8},{10,11... | collective-permute-start | bytes 4718600 | tf_op jit(solution)/shard_map/ppermute | solution.py:259
  0.5 1.1 %copy-start.3 = (bf16[3,256,512]{2,1,0:T(8,128)(2,1)S(1)}, bf16[3,256,512]{2,1,0:T(8,128)(2,1)}, u32[]{:S(2)}) copy-start(bf16[3,256,512]{2,1,0:T(8,128)(2,1)} %own.3) | copy-start | bytes 2359300
  1.6 0.7 copy-start.5
  2.9 22.0 %collective-permute-start = (bf16[3,128,512]{2,1,0:T(8,128)(2,1)S(1)}, bf16[3,128,512]{2,1,0:T(8,128)(2,1)S(1)}, u32[]{:S(2)}, u32[]{:S(2)}) collective-permute-start(bf16[3,128,512]{2,1,0:T(8,128)(2,1)S(1)} %get-tuple-element.11), channel_id=1, source_target_pairs={{0,8},{4,12},{8,0},{12,4},{1,9},{5,13},{9,1},{13,5},{2,10},{6,14},... | collective-permute-start | bytes 1179656 | tf_op jit(solution)/shard_map/ppermute | solution.py:295
  6.6 1.4 %copy-start = (bf16[2,3,256,512]{3,2,1,0:T(8,128)(2,1)S(1)}, bf16[2,3,256,512]{3,2,1,0:T(8,128)(2,1)}, u32[]{:S(2)}) copy-start(bf16[2,3,256,512]{3,2,1,0:T(8,128)(2,1)} %left.5) | copy-start | bytes 4718596
  8.0 1.4 %copy-start.2 = (bf16[2,3,256,512]{3,2,1,0:T(8,128)(2,1)S(1)}, bf16[2,3,256,512]{3,2,1,0:T(8,128)(2,1)}, u32[]{:S(2)}) copy-start(bf16[2,3,256,512]{3,2,1,0:T(8,128)(2,1)} %right.5) | copy-start | bytes 4718596
  9.4 9.9 %copy-start.4 = (bf16[3,256,512]{2,1,0:T(8,128)(2,1)S(1)}, bf16[3,256,512]{2,1,0:T(8,128)(2,1)}, u32[]{:S(2)}) copy-start(bf16[3,256,512]{2,1,0:T(8,128)(2,1)} %own.3) | copy-start | bytes 2359300
  9.4 41.4 %copy-start.1 = (bf16[2,3,256,512]{3,2,1,0:T(8,128)(2,1)S(1)}, bf16[2,3,256,512]{3,2,1,0:T(8,128)(2,1)}, u32[]{:S(2)}) copy-start(bf16[2,3,256,512]{3,2,1,0:T(8,128)(2,1)} %left.5) | copy-start | bytes 4718596
  9.4 41.4 %copy-start.6 = (s32[12]{0:T(128)S(1)}, s32[12]{0:T(128)}, u32[]{:S(2)}) copy-start(s32[12]{0:T(128)} %left_dims.5) | copy-start | bytes 148
  9.4 41.4 %copy-start.7 = (s32[12]{0:T(128)S(1)}, s32[12]{0:T(128)}, u32[]{:S(2)}) copy-start(s32[12]{0:T(128)} %right_dims.5) | copy-start | bytes 148
  10.2 9.2 %collective-permute-start.9 = (bf16[2,256,256]{2,1,0:T(8,128)(2,1)S(1)}, bf16[2,256,256]{2,1,0:T(8,128)(2,1)S(1)}, u32[]{:S(2)}, u32[]{:S(2)}) collective-permute-start(bf16[2,256,256]{2,1,0:T(8,128)(2,1)S(1)} %get-tuple-element.12), channel_id=1, source_target_pairs={{0,2},{2,0},{1,3},{3,1},{4,6},{6,4},{5,7},{7,5},{8,10},{10,8},{9,1... | collective-permute-start | bytes 786440 | tf_op jit(solution)/shard_map/ppermute | solution.py:259
  11.7 21.0 %collective-permute-start.13 = (bf16[2,256,512]{2,1,0:T(8,128)(2,1)S(1)}, bf16[2,256,512]{2,1,0:T(8,128)(2,1)S(1)}, u32[]{:S(2)}, u32[]{:S(2)}) collective-permute-start(bf16[2,256,512]{2,1,0:T(8,128)(2,1)S(1)} %get-tuple-element.14), channel_id=1, source_target_pairs={{0,4},{4,0},{8,12},{12,8},{1,5},{5,1},{9,13},{13,9},{2,6},{6,2},{1... | collective-permute-start | bytes 1572872 | tf_op jit(solution)/shard_map/ppermute | solution.py:296
  13.3 21.4 %collective-permute-start.10 = (bf16[2,256,512]{2,1,0:T(8,128)(2,1)S(1)}, bf16[2,256,512]{2,1,0:T(8,128)(2,1)S(1)}, u32[]{:S(2)}, u32[]{:S(2)}) collective-permute-start(bf16[2,256,512]{2,1,0:T(8,128)(2,1)S(1)} %get-tuple-element.13), channel_id=1, source_target_pairs={{0,2},{2,0},{1,3},{3,1},{4,6},{6,4},{5,7},{7,5},{8,10},{10,8},{9,1... | collective-permute-start | bytes 1572872 | tf_op jit(solution)/shard_map/ppermute | solution.py:259
  19.4 24.2 %collective-permute-start.12 = (bf16[3,256,512]{2,1,0:T(8,128)(2,1)S(1)}, bf16[3,256,512]{2,1,0:T(8,128)(2,1)S(1)}, u32[]{:S(2)}, u32[]{:S(2)}) collective-permute-start(bf16[3,256,512]{2,1,0:T(8,128)(2,1)S(1)} %copy-done.4), channel_id=1, source_target_pairs={{0,1},{1,0},{2,3},{3,2},{4,5},{5,4},{6,7},{7,6},{8,9},{9,8},{10,11... | collective-permute-start | bytes 2359304 | tf_op jit(solution)/shard_map/ppermute | solution.py:259
  24.9 8.5 %collective-permute-start.6 = (bf16[3,128,512]{2,1,0:T(8,128)(2,1)S(1)}, bf16[3,128,512]{2,1,0:T(8,128)(2,1)S(1)}, u32[]{:S(2)}, u32[]{:S(2)}) collective-permute-start(bf16[3,128,512]{2,1,0:T(8,128)(2,1)S(1)} %get-tuple-element.11), channel_id=1, source_target_pairs={{4,8},{8,4},{5,9},{9,5},{6,10},{10,6},{7,11},{11,7},{20,24},{24,20... | collective-permute-start | bytes 1179656 | tf_op jit(solution)/shard_map/ppermute | solution.py:305
  32.8 15.5 %collective-permute-start.14 = (bf16[2,256,512]{2,1,0:T(8,128)(2,1)S(1)}, bf16[2,256,512]{2,1,0:T(8,128)(2,1)S(1)}, u32[]{:S(2)}, u32[]{:S(2)}) collective-permute-start(bf16[2,256,512]{2,1,0:T(8,128)(2,1)S(1)} %collective-permute-done.13.near), channel_id=1, source_target_pairs={{0,1},{1,0},{2,3},{3,2},{4,5},{5,4},{6,7},{7,6},{8,9},{9,8},{10,11... | collective-permute-start | bytes 1572872 | tf_op jit(solution)/shard_map/ppermute | solution.py:259
  33.4 14.9 %collective-permute-start.4 = (bf16[3,128,512]{2,1,0:T(8,128)(2,1)S(1)}, bf16[3,128,512]{2,1,0:T(8,128)(2,1)S(1)}, u32[]{:S(2)}, u32[]{:S(2)}) collective-permute-start(bf16[3,128,512]{2,1,0:T(8,128)(2,1)S(1)} %collective-permute-done.mid), channel_id=1, source_target_pairs={{4,0},{8,12},{5,1},{9,13},{6,2},{10,14},{7,3},{11,15},{20,16},{24,... | collective-permute-start | bytes 1179656 | tf_op jit(solution)/shard_map/ppermute | solution.py:306
  34.7 8.8 %collective-permute-start.1 = (bf16[2,128,512]{2,1,0:T(8,128)(2,1)S(1)}, bf16[2,128,512]{2,1,0:T(8,128)(2,1)S(1)}, u32[]{:S(2)}, u32[]{:S(2)}) collective-permute-start(bf16[2,128,512]{2,1,0:T(8,128)(2,1)S(1)} %pick_kernel.1), channel_id=1, source_target_pairs={{0,2},{2,0},{1,3},{3,1},{4,6},{6,4},{5,7},{7,5},{8,10},{10,8},{9,1... | collective-permute-start | bytes 786440 | tf_op jit(solution)/shard_map/ppermute | solution.py:259
  43.5 10.3 %collective-permute-start.11 = (bf16[2,256,512]{2,1,0:T(8,128)(2,1)S(1)}, bf16[2,256,512]{2,1,0:T(8,128)(2,1)S(1)}, u32[]{:S(2)}, u32[]{:S(2)}) collective-permute-start(bf16[2,256,512]{2,1,0:T(8,128)(2,1)S(1)} %collective-permute-done.10.right_x), channel_id=1, source_target_pairs={{0,1},{1,0},{2,3},{3,2},{4,5},{5,4},{6,7},{7,6},{8,9},{9,8},{10,11... | collective-permute-start | bytes 1572872 | tf_op jit(solution)/shard_map/ppermute | solution.py:259
  43.5 10.2 %collective-permute-start.7 = (bf16[3,128,512]{2,1,0:T(8,128)(2,1)S(1)}, bf16[3,128,512]{2,1,0:T(8,128)(2,1)S(1)}, u32[]{:S(2)}, u32[]{:S(2)}) collective-permute-start(bf16[3,128,512]{2,1,0:T(8,128)(2,1)S(1)} %collective-permute-done.6.inner), channel_id=1, source_target_pairs={{4,5},{5,4},{8,9},{9,8},{6,7},{7,6},{10,11},{11,10},{20,21},{21,20... | collective-permute-start | bytes 1179656 | tf_op jit(solution)/shard_map/ppermute | solution.py:263
  48.3 5.5 %collective-permute-start.2 = (bf16[3,128,512]{2,1,0:T(8,128)(2,1)S(1)}, bf16[3,128,512]{2,1,0:T(8,128)(2,1)S(1)}, u32[]{:S(2)}, u32[]{:S(2)}) collective-permute-start(bf16[3,128,512]{2,1,0:T(8,128)(2,1)S(1)} %collective-permute-done.mid), channel_id=1, source_target_pairs={{0,1},{1,0},{2,3},{3,2},{4,5},{5,4},{6,7},{7,6},{8,9},{9,8},{10,11... | collective-permute-start | bytes 1179656 | tf_op jit(solution)/shard_map/ppermute | solution.py:259
  48.3 5.5 %collective-permute-start.5 = (bf16[3,128,512]{2,1,0:T(8,128)(2,1)S(1)}, bf16[3,128,512]{2,1,0:T(8,128)(2,1)S(1)}, u32[]{:S(2)}, u32[]{:S(2)}) collective-permute-start(bf16[3,128,512]{2,1,0:T(8,128)(2,1)S(1)} %collective-permute-done.4.end), channel_id=1, source_target_pairs={{0,1},{1,0},{12,13},{13,12},{2,3},{3,2},{14,15},{15,14},{16,17},{1... | collective-permute-start | bytes 1179656 | tf_op jit(solution)/shard_map/ppermute | solution.py:263
  50.7 3.1 %collective-permute-start.3 = (bf16[2,128,512]{2,1,0:T(8,128)(2,1)S(1)}, bf16[2,128,512]{2,1,0:T(8,128)(2,1)S(1)}, u32[]{:S(2)}, u32[]{:S(2)}) collective-permute-start(bf16[2,128,512]{2,1,0:T(8,128)(2,1)S(1)} %collective-permute-done.1.mid_x), channel_id=1, source_target_pairs={{0,1},{1,0},{2,3},{3,2},{4,5},{5,4},{6,7},{7,6},{8,9},{9,8},{10,11... | collective-permute-start | bytes 786440 | tf_op jit(solution)/shard_map/ppermute | solution.py:259
  57.7 11.6 %collective-permute-start.15 = (bf16[3,256,256]{2,1,0:T(8,128)(2,1)S(1)}, bf16[3,256,256]{2,1,0:T(8,128)(2,1)S(1)}, u32[]{:S(2)}, u32[]{:S(2)}) collective-permute-start(bf16[3,256,256]{2,1,0:T(8,128)(2,1)S(1)} %get-tuple-element.16), channel_id=1, source_target_pairs={{0,2},{2,0},{1,3},{3,1},{4,6},{6,4},{5,7},{7,5},{8,10},{10,8},{9,1... | collective-permute-start | bytes 1179656 | tf_op jit(solution)/shard_map/ppermute | solution.py:259

commit v4 on v0

--- a/solution.py
+++ b/solution.py
@@ -1,10 +1,21 @@
+import functools
+
 import jax
 import jax.numpy as jnp
 from jax import lax
+from jax.experimental import pallas as pl
+from jax.experimental.pallas import tpu as pltpu
 from jax.sharding import PartitionSpec as P
 
-
-def per_device(wavefunction, left_env, right_env, source, left_dims, right_dims):
+BF16 = jnp.bfloat16
+F32 = jnp.float32
+FILL = 30 * 10**9
+VMEM_MOST = 61 * 1024 * 1024
+VMEM_MUCH = 48 * 1024 * 1024
+VMEM_LIMIT = 16 * 1024 * 1024
+
+
+def general(wavefunction, left_env, right_env, source, left_dims, right_dims):
     sec_local, half_rows, blk_cols = wavefunction.shape
     pair_local = left_env.shape[0]
     needed = pair_local * sec_local
@@ -54,14 +65,14 @@
         "nab,ncb->nac",
         lax.all_gather(fetched, "half", axis=1, tiled=True),
         right_rows,
-        preferred_element_type=jnp.float32,
-    ).astype(jnp.bfloat16)
+        preferred_element_type=F32,
+    ).astype(BF16)
     right_part = right_part.reshape(pair_local, sec_local, right_part.shape[1], right_part.shape[2])
     partial_sum = jnp.einsum(
         "ksrc,kscj->srj",
         left_env,
         lax.all_gather(right_part, "half", axis=3, tiled=True),
-        preferred_element_type=jnp.float32,
+        preferred_element_type=F32,
     )
     summed = lax.psum_scatter(partial_sum, "op", scatter_dimension=2, tiled=True)
     col_width = summed.shape[2]
@@ -69,12 +80,284 @@
     out_mask = (row_ids[None, :, None] < left_live[:, None, None]) & (
         out_cols[None, None, :] < right_live[:, None, None]
     )
-    return jnp.where(out_mask, summed, jnp.zeros((), jnp.float32)).astype(jnp.bfloat16)
+    return jnp.where(out_mask, summed, jnp.zeros((), F32)).astype(BF16)
+
+
+def place():
+    return lax.axis_index("sector"), lax.axis_index("op"), lax.axis_index("half")
+
+
+def slots_of(sizes, source, z, op):
+    pairs, secs = sizes[:2]
+    found = []
+    for n in range(pairs * secs):
+        src = source[op * pairs + n // secs, z * secs + n % secs]
+        holder = src // secs
+        found.append((holder ^ z, src - holder * secs, src))
+    return found
+
+
+def ranked(slots, kind, rank):
+    slot, local, source = jnp.int32(-1), jnp.int32(0), jnp.int32(0)
+    seen = jnp.int32(0)
+    for n, (k, b, s) in enumerate(slots):
+        hit = (k == kind) & (seen == rank)
+        slot = jnp.where(hit, n, slot)
+        local = jnp.where(hit, b, local)
+        source = jnp.where(hit, s, source)
+        seen = seen + (k == kind).astype(jnp.int32)
+    return slot, local, source
+
+
+def first_kernel(sizes, source, own, left, right, share, near_out, env_out, l_buf, sem):
+    pairs, secs, half_rows, blk = sizes
+    quarter = half_rows // 2
+    z, o, _ = place()
+    theirs = slots_of(sizes, source, z ^ 1, o)
+    mine = slots_of(sizes, source, z, o)
+    moves = [(own.at[:, pl.ds(pl.multiple_of(o * quarter, quarter), quarter)], share)]
+    for j in range(2):
+        moves.append((own.at[ranked(theirs, 1, j)[1]], near_out.at[j]))
+    for j in range(2):
+        n = jnp.maximum(ranked(mine, 3, j)[0], 0)
+        moves.append((left.at[n // secs, n % secs], l_buf.at[j]))
+        moves.append((right.at[n // secs, n % secs], env_out.at[j, :, :blk]))
+    copies = [pltpu.make_async_copy(src, dst, sem.at[i]) for i, (src, dst) in enumerate(moves)]
+    for copy in copies:
+        copy.start()
+    for copy in copies:
+        copy.wait()
+    for part in range(2):
+        first = pl.multiple_of(part * half_rows + (1 - o) * quarter, quarter)
+        env_out[:, :, blk + part * quarter : blk + (part + 1) * quarter] = l_buf[:, :, pl.ds(first, quarter)]
+
+
+def load_kernel(sizes, *refs):
+    count = len(refs) // 2
+    copies = [pltpu.make_async_copy(refs[i], refs[count + i], refs[-1].at[i]) for i in range(count)]
+    for copy in copies:
+        copy.start()
+    for copy in copies:
+        copy.wait()
+
+
+def pick_kernel(sizes, source, mid, picked):
+    z, o, _ = place()
+    theirs = slots_of(sizes, source, z, 1 - o)
+    for j in range(2):
+        picked[j] = mid[ranked(theirs, 2, j)[1]]
+
+
+def live_columns(sizes, right_dims, src):
+    col = lax.broadcasted_iota(jnp.int32, (1, sizes[3]), 1)
+    return (col < right_dims[src]).astype(F32).astype(BF16)
+
+
+def times_right(m, r, row, left_live):
+    part = lax.dot_general(m, r, (((1,), (1,)), ((), ())), preferred_element_type=F32)
+    return jnp.where(row < left_live, part, 0.0).astype(BF16)
+
+
+def early_kernel(kind, sizes, source, left_dims, right_dims, near, near_far, left, right, right_far, *rest):
+    pairs, secs, half_rows, blk = sizes
+    acc, m_buf = rest[-2:]
+    z, o, h = place()
+    slots = slots_of(sizes, source, z, o)
+    mine = pl.ds(pl.multiple_of(h * half_rows, half_rows), half_rows)
+    far = pl.ds(pl.multiple_of((1 - h) * half_rows, half_rows), half_rows)
+    acc[...] = rest[0][...] if kind == 1 else jnp.zeros_like(acc)
+    row = lax.broadcasted_iota(jnp.int32, (blk, 1), 0)
+    for j in range(2):
+        n, local, src = ranked(slots, kind, j)
+
+        @pl.when(n >= 0)
+        def _():
+            k, t = n // secs, n % secs
+            live = live_columns(sizes, right_dims, src)
+            at = j if kind == 1 else local
+            m_buf[mine] = near[at] * live
+            m_buf[far] = near_far[at] * live
+            r = jnp.concatenate(
+                [jnp.where(h == 0, right[k, t], right_far[k, t]), jnp.where(h == 0, right_far[k, t], right[k, t])],
+                axis=0,
+            )
+            part = times_right(m_buf[...], r, row, left_dims[src])
+            acc[t] += jnp.dot(left[k, t], part, preferred_element_type=F32)
+
+
+def late_kernel(
+    kept, sizes, source, left_dims, right_dims, mid, mid_x, mid_far, mid_x_far, far, far_far,
+    left, right, right_far, env_x, env_x_far, early, out, total,
+):
+    pairs, secs, half_rows, blk = sizes
+    quarter = half_rows // 2
+    z, o, h = place()
+    mine = slots_of(sizes, source, z, o)
+    theirs = slots_of(sizes, source, z, 1 - o)
+    side = o if kept else 1 - o
+    total[...] = early[:, :, pl.ds(pl.multiple_of(side * half_rows, half_rows), half_rows)]
+    at = lax.broadcasted_iota(jnp.int32, (quarter, 1), 0)
+
+    def product(m_pieces, firsts, left_pieces, r, n, src):
+        live = live_columns(sizes, right_dims, src)
+        row = jnp.concatenate([at + first for first in firsts], axis=0)
+        left_live = jnp.where(n >= 0, left_dims[src], 0)
+        part = times_right(jnp.concatenate(m_pieces, axis=0), r * live, row, left_live)
+        return jnp.dot(jnp.concatenate(left_pieces, axis=1), part, preferred_element_type=F32)
+
+    def columns(ref, k, t, first):
+        return ref[k, t, :, pl.ds(pl.multiple_of(first, quarter), quarter)]
+
+    found = []
+    for j in range(2):
+        n, local, src = ranked(mine, 2, j)
+        k, t = jnp.maximum(n, 0) // secs, jnp.maximum(n, 0) % secs
+        firsts = [half * half_rows + op * quarter for half, op in ((h, o), (h, 1 - o), (1 - h, o), (1 - h, 1 - o))]
+        pieces = [mid[local], mid_x[j], mid_far[local], mid_x_far[j]]
+        lefts = [columns(left, k, t, first) for first in firsts]
+        r = jnp.where(side == h, right[k, t], right_far[k, t])
+        found.append((t, product(pieces, firsts, lefts, r, n, src)))
+
+    firsts = [h * half_rows + o * quarter, (1 - h) * half_rows + o * quarter]
+    for i in range(4):
+        j = i % 2
+        n, local, src = ranked(mine if i < 2 else theirs, 3, j)
+        k, t = jnp.maximum(n, 0) // secs, jnp.maximum(n, 0) % secs
+        pieces = [far[local], far_far[local]]
+        if i < 2:
+            r = jnp.where(side == h, right[k, t], right_far[k, t])
+            lefts = [columns(left, k, t, first) for first in firsts]
+        else:
+            r = jnp.where(side == h, env_x[j, :, :blk], env_x_far[j, :, :blk])
+            lefts = [
+                env_x[j, :, pl.ds(pl.multiple_of(blk + first, quarter), quarter)]
+                for first in (h * quarter, (1 - h) * quarter)
+            ]
+        found.append((t, product(pieces, firsts, lefts, r, n, src)))
+
+    for t, term in found:
+        total[t] += term
+    out[...] = total[...].astype(out.dtype)
+
+
+def join_kernel(sizes, left_dims, right_dims, keep, received, out):
+    secs, half_rows, blk = sizes[1:]
+    z, o, h = place()
+    row = h * half_rows + lax.broadcasted_iota(jnp.int32, (half_rows, 1), 0)
+    col = o * half_rows + lax.broadcasted_iota(jnp.int32, (1, half_rows), 1)
+    for t in range(secs):
+        live = (row < left_dims[z * secs + t]) & (col < right_dims[z * secs + t])
+        out[t] = jnp.where(live, keep[t] + received[t].astype(F32), 0.0).astype(BF16)
+
+
+def swap(x, axis):
+    return lax.ppermute(x, axis, [(0, 1), (1, 0)])
+
+
+def after(x, *earlier):
+    return lax.optimization_barrier((x, *earlier))[0]
+
+
+def exchange(x, kind):
+    return lax.ppermute(x, "sector", [(i, i ^ kind) for i in range(4)])
+
+
+def four_by_two(wavefunction, left_env, right_env, source, left_dims, right_dims):
+    secs, half_rows, blk = wavefunction.shape
+    pairs = left_env.shape[0]
+    quarter = half_rows // 2
+    sizes = (pairs, secs, half_rows, blk)
+
+    def call(kernel, name, outs, scalars, arrays, scratch=(), flops=0, space=pltpu.VMEM, limit=VMEM_LIMIT):
+        shapes = [jax.ShapeDtypeStruct(shape, dtype) for shape, dtype in outs]
+        nbytes = sum(s.size * s.dtype.itemsize for s in [*shapes, *arrays])
+        return pl.pallas_call(
+            functools.partial(kernel, sizes),
+            out_shape=shapes,
+            in_specs=[pl.BlockSpec(memory_space=pltpu.SMEM)] * len(scalars)
+            + [pl.BlockSpec(memory_space=space)] * len(arrays),
+            out_specs=[pl.BlockSpec(memory_space=pltpu.VMEM)] * len(shapes),
+            scratch_shapes=scratch,
+            compiler_params=pltpu.CompilerParams(vmem_limit_bytes=limit),
+            cost_estimate=pl.CostEstimate(flops=flops, bytes_accessed=nbytes, transcendentals=0),
+            name=name,
+        )(*scalars, *arrays)
+
+    dims = (source, left_dims, right_dims)
+    share, near_out, env_out = call(
+        first_kernel,
+        "first",
+        [
+            ((secs, quarter, blk), BF16),
+            ((2, half_rows, blk), BF16),
+            ((2, half_rows, blk + half_rows), BF16),
+        ],
+        (source,),
+        (wavefunction, left_env, right_env),
+        [pltpu.VMEM((2, half_rows, blk), BF16), pltpu.SemaphoreType.DMA((7,))],
+        space=pltpu.HBM,
+        limit=VMEM_MOST,
+    )
+    mid = exchange(share, 2)
+    near = exchange(near_out, 1)
+    env_x = swap(env_out, "op")
+    own_far = swap(wavefunction, "half")
+    right_far = swap(right_env, "half")
+    loaded = (after(wavefunction, share), left_env, right_env)
+    own, left, right = call(
+        load_kernel,
+        "load",
+        [(x.shape, x.dtype) for x in loaded],
+        (),
+        loaded,
+        [pltpu.SemaphoreType.DMA((3,))],
+        flops=FILL,
+        space=pltpu.HBM,
+        limit=VMEM_MUCH,
+    )
+    mid, near, env_x, own_far, right_far = (after(x, own) for x in (mid, near, env_x, own_far, right_far))
+    far = exchange(mid, 1)
+    envs = (left, right, right_far)
+    total = [((secs, half_rows, blk), F32)]
+    block = [pltpu.VMEM((blk, blk), BF16)]
+    (picked,) = call(pick_kernel, "pick", [((2, quarter, blk), BF16)], (source,), (after(mid, env_x),))
+    mid_x = swap(picked, "op")
+    near_far = swap(near, "half")
+    mid_far = swap(mid, "half")
+    env_x_far = swap(env_x, "half")
+    (early,) = call(functools.partial(early_kernel, 0), "own_slots", total, dims, (own, own_far, *envs), block)
+    (early,) = call(
+        functools.partial(early_kernel, 1),
+        "near_slots",
+        total,
+        dims,
+        (near, after(near_far, mid_far, env_x_far), *envs, early),
+        block,
+        flops=FILL,
+    )
+    mid_x, far = after(mid_x, early), after(far, early)
+    mid_x_far = swap(mid_x, "half")
+    far_far = swap(far, "half")
+    arrays = (mid, mid_x, mid_far, mid_x_far, far, far_far, *envs, env_x, env_x_far, early)
+    buffers = [pltpu.VMEM((secs, half_rows, half_rows), F32)]
+    flops = 2 * 3 * half_rows * blk * blk * 2
+    columns = (secs, half_rows, half_rows)
+    (send,) = call(
+        functools.partial(late_kernel, False), "late_sent", [(columns, BF16)], dims, arrays, buffers, flops
+    )
+    received = swap(send, "op")
+    (keep,) = call(
+        functools.partial(late_kernel, True), "late_kept", [(columns, F32)], dims, arrays, buffers, flops
+    )
+    (out,) = call(join_kernel, "join", [(columns, BF16)], (left_dims, right_dims), (keep, received))
+    return out
 
 
 def solution(mesh):
+    shape = mesh.shape
+    fits = (shape["sector"], shape["op"], shape["half"]) == (4, 2, 2)
     return jax.shard_map(
-        per_device,
+        four_by_two if fits else general,
         mesh=mesh,
         in_specs=(
             P(("group", "sector"), "half", None),

time: 145 us -> 60 us (0.41)
  waiting for transfers between devices: 100 us -> 30.9 us
  Pallas kernels: 0 us -> 17.6 us
  between operations: 13.2 us -> 0.1 us
  local copies, waits for them, and re-layouts: 10.6 us -> 0.01 us
  other arithmetic: 7.04 us -> 0 us
  matrix products: 6.96 us -> 0 us
  starting transfers between devices: 6.4 us -> 11.2 us
    all_to_all x1 -> x0, waiting for transfers between devices: 48 us -> none  [per_device(): lax.all_to_all(outgoing, 'sector', split_axis=0, concat_axis=0, tiled=True)]
    ppermute x0 -> x13, waiting for transfers between devices: none -> 30.9 us  [the longest x10 23.5 us: swap(): return lax.ppermute(x, axis, [(0, 1), (1, 0)])]
    reduce_scatter x1 -> x0, waiting for transfers between devices: 27.3 us -> none  [per_device(): lax.psum_scatter(partial_sum, 'op', scatter_dimension=2, tiled=True)]
    all_gather x2 -> x0, waiting for transfers between devices: 24.7 us -> none  [the longest x1 13.4 us: per_device(): lax.all_gather(right_part, 'half', axis=3, tiled=True)]
    pallas_call x0 -> x8, Pallas kernels: none -> 17.6 us  [call(): pl.pallas_call(functools.partial(kernel, sizes), out_shape=shapes, in_spe...]
    ppermute x0 -> x13, starting transfers between devices: none -> 11.2 us  [the longest x3 5.94 us: exchange(): return lax.ppermute(x, 'sector', [(i, i ^ kind) for i in range(4)])]
    dot_general x2 -> x0, matrix products: 6.96 us -> none  [the longest x1 4.06 us: per_device(): jnp.einsum('ksrc,kscj->srj', left_env, lax.all_gather(right_part, 'half',...]
    gather x4 -> x0, local copies, waits for them, and re-layouts: 6.81 us -> none  [the longest x1 2.24 us: per_device(): jnp.take(incoming.reshape(sector_count * capacity, half_rows, blk_cols),...]
  transfers between devices with their start and end apart: 4 -> 13, of which waited for: 4 -> 5; matrix products, arithmetic and copies ran while one was open for 0% -> 0% of each run, Pallas kernels for 0% -> 22%
where the time goes in v4:
time: 60 us; the launch traced here: 59.8 us
  waiting for transfers between devices  30.9 us (52%)
  Pallas kernels  17.6 us (29%)
  starting transfers between devices  11.2 us (19%)
    ppermute x10, waiting for transfers between devices, swap(): return lax.ppermute(x, axis, [(0, 1), (1, 0)])  23.5 us
    pallas_call x8, Pallas kernels, call(): pl.pallas_call(functools.partial(kernel, sizes), out_shape=shapes, in_spe...  17.6 us
    ppermute x3, waiting for transfers between devices, exchange(): return lax.ppermute(x, 'sector', [(i, i ^ kind) for i in range(4)])  7.35 us
    ppermute x3, starting transfers between devices, exchange(): return lax.ppermute(x, 'sector', [(i, i ^ kind) for i in range(4)])  5.94 us
    ppermute x10, starting transfers between devices, swap(): return lax.ppermute(x, axis, [(0, 1), (1, 0)])  5.25 us
  transfers between devices with their start and end apart: 13, of which 5 were waited for; matrix products, arithmetic and copies ran while one was open for 0% of the time, Pallas kernels for 22%

profile of v4, /device:TPU:0, one launch (start us, length us, event | category | flops | bytes accessed | tf_op | source)
XLA Modules:
  0.0 59.8 jit_solution(949098985833980078)
XLA Ops:
  0.0 0.0 copy-start
  0.0 0.5 collective-permute-start.7
  0.5 0.1 collective-permute-start.8
  0.5 3.5 %first.1 = (bf16[3,128,512]{2,1,0:T(8,128)(2,1)}, bf16[2,256,512]{2,1,0:T(8,128)(2,1)}, bf16[2,256,768]{2,1,0:T(8,128)(2,1)}) custom-call(s32[4,12]{1,0:T(4,128)} %source.11, bf16[3,256,512]{2,1,0:T(8,128)(2,1)} %refs_0_, bf16[2,3,256,512]{3,2,1,0:T(8,128)(2,1)} %refs_1_.1, bf16[2,3,256,512]{3,2,1,0:T(8,128)(2,1)} %refs_2_.1), custom_call_target="tpu_custom_call" | custom-call | bytes 5636096 | tf_op jit(solution)/shard_map/first/pallas_call | solution.py:274
  4.0 4.1 %collective-permute-start = (bf16[3,128,512]{2,1,0:T(8,128)(2,1)}, bf16[3,128,512]{2,1,0:T(8,128)(2,1)S(1)}, u32[]{:S(2)}, u32[]{:S(2)}) collective-permute-start(bf16[3,128,512]{2,1,0:T(8,128)(2,1)} %get-tuple-element.21), channel_id=1, source_target_pairs={{0,8},{4,12},{8,0},{12,4},{1,9},{5,13},{9,1},{13,5},{2,10},{6,14},... | collective-permute-start | bytes 1179656 | tf_op jit(solution)/shard_map/ppermute | solution.py:262
  8.1 1.5 %collective-permute-start.1 = (bf16[2,256,768]{2,1,0:T(8,128)(2,1)}, bf16[2,256,768]{2,1,0:T(8,128)(2,1)S(1)}, u32[]{:S(2)}, u32[]{:S(2)}) collective-permute-start(bf16[2,256,768]{2,1,0:T(8,128)(2,1)} %get-tuple-element.25), channel_id=1, source_target_pairs={{0,2},{2,0},{1,3},{3,1},{4,6},{6,4},{5,7},{7,5},{8,10},{10,8},{9,1... | collective-permute-start | bytes 2359304 | tf_op jit(solution)/shard_map/ppermute | solution.py:254
  9.6 0.0 copy-start.1
  9.6 0.0 copy-start.2
  9.6 0.0 copy-start.3
  9.6 1.6 %collective-permute-start.3 = (bf16[2,256,512]{2,1,0:T(8,128)(2,1)}, bf16[2,256,512]{2,1,0:T(8,128)(2,1)S(1)}, u32[]{:S(2)}, u32[]{:S(2)}) collective-permute-start(bf16[2,256,512]{2,1,0:T(8,128)(2,1)} %get-tuple-element.28), channel_id=1, source_target_pairs={{0,4},{4,0},{8,12},{12,8},{1,5},{5,1},{9,13},{13,9},{2,6},{6,2},{1... | collective-permute-start | bytes 1572872 | tf_op jit(solution)/shard_map/ppermute | solution.py:262
  11.2 0.0 copy-done
  11.2 2.0 %load.1 = (bf16[3,256,512]{2,1,0:T(8,128)(2,1)S(1)}, bf16[2,3,256,512]{3,2,1,0:T(8,128)(2,1)S(1)}, bf16[2,3,256,512]{3,2,1,0:T(8,128)(2,1)S(1)}) custom-call(bf16[3,256,512]{2,1,0:T(8,128)(2,1)S(1)} %copy-done, bf16[2,3,256,512]{3,2,1,0:T(8,128)(2,1)} %refs_1_.1, bf16[2,3,256,512]{3,2,1,0:T(8,128)(2,1)} %refs_2_.1), custom_call_target="tpu_custom_call" | custom-call | flops 30000001024 | bytes 7864320 | tf_op jit(solution)/shard_map/load/pallas_call | solution.py:274
  13.1 14.4 %collective-permute-done.1.env_x = bf16[2,256,768]{2,1,0:T(8,128)(2,1)S(1)} collective-permute-done((bf16[2,256,768]{2,1,0:T(8,128)(2,1)}, bf16[2,256,768]{2,1,0:T(8,128)(2,1)S(1)}, u32[]{:S(2)}, u32[]{:S(2)}) %collective-permute-start.1) | collective-permute-done | bytes 786464 | tf_op jit(solution)/shard_map/ppermute | solution.py:254
  27.5 0.0 collective-permute-start.6
  27.5 2.9 %collective-permute-done.3.near = bf16[2,256,512]{2,1,0:T(8,128)(2,1)S(1)} collective-permute-done((bf16[2,256,512]{2,1,0:T(8,128)(2,1)}, bf16[2,256,512]{2,1,0:T(8,128)(2,1)S(1)}, u32[]{:S(2)}, u32[]{:S(2)}) %collective-permute-start.3) | collective-permute-done | bytes 524320 | tf_op jit(solution)/shard_map/ppermute | solution.py:262
  30.4 0.0 collective-permute-start.4
  30.4 0.0 collective-permute-done.mid
  30.4 0.5 collective-permute-start.5
  30.9 0.0 collective-permute-done.8.near_far
  30.9 0.3 collective-permute-start.10
  31.2 0.0 copy-done.1
  31.2 0.7 %pick.1 = bf16[2,128,512]{2,1,0:T(8,128)(2,1)S(1)} custom-call(s32[4,12]{1,0:T(4,128)S(1)} %copy-done.1, bf16[3,128,512]{2,1,0:T(8,128)(2,1)S(1)} %collective-permute-done.mid), custom_call_target="tpu_custom_call" | custom-call | bytes 655360 | tf_op jit(solution)/shard_map/pick/pallas_call | solution.py:274
  31.8 0.0 collective-permute-done.7.right_far
  31.9 1.6 %collective-permute-start.2 = (bf16[2,128,512]{2,1,0:T(8,128)(2,1)S(1)}, bf16[2,128,512]{2,1,0:T(8,128)(2,1)S(1)}, u32[]{:S(2)}, u32[]{:S(2)}) collective-permute-start(bf16[2,128,512]{2,1,0:T(8,128)(2,1)S(1)} %pick.1), channel_id=1, source_target_pairs={{0,2},{2,0},{1,3},{3,1},{4,6},{6,4},{5,7},{7,5},{8,10},{10,8},{9,1... | collective-permute-start | bytes 786440 | tf_op jit(solution)/shard_map/ppermute | solution.py:254
  33.4 0.0 collective-permute-done.5.mid_far
  33.4 0.0 collective-permute-done.4.near_far
  33.4 0.0 collective-permute-done.6.env_x_far
  33.4 0.0 copy-done.2
  33.4 0.0 copy-done.3
  33.4 2.0 %own_slots.1.rest_0_ = f32[3,256,512]{2,1,0:T(8,128)S(1)} custom-call(s32[4,12]{1,0:T(4,128)S(1)} %copy-done.1, s32[12]{0:T(128)S(1)} %copy-done.2, s32[12]{0:T(128)S(1)} %copy-done.3, bf16[3,256,512]{2,1,0:T(8,128)(2,1)S(1)} %get-tuple-element.23.near, bf16[3,256,512]{2,1,0:T(8,128)(2,1)} %collective-permute-done.8.near_far, ...), custom_call_target="tpu_custom_call" | custom-call | bytes 7864320 | tf_op jit(solution)/shard_map/own_slots/pallas_call | solution.py:274
  35.4 2.1 %near_slots.1.early = f32[3,256,512]{2,1,0:T(8,128)S(1)} custom-call(s32[4,12]{1,0:T(4,128)S(1)} %copy-done.1, s32[12]{0:T(128)S(1)} %copy-done.2, s32[12]{0:T(128)S(1)} %copy-done.3, bf16[2,256,512]{2,1,0:T(8,128)(2,1)S(1)} %collective-permute-done.3.near, bf16[2,256,512]{2,1,0:T(8,128)(2,1)S(1)} %collective-permute-done.4.near_far, ...), custom_call_target="tpu_custom_call" | custom-call | flops 30000001024 | bytes 8912896 | tf_op jit(solution)/shard_map/near_slots/pallas_call | solution.py:274
  37.5 4.5 %collective-permute-done.10.far = bf16[3,128,512]{2,1,0:T(8,128)(2,1)S(1)} collective-permute-done((bf16[3,128,512]{2,1,0:T(8,128)(2,1)S(1)}, bf16[3,128,512]{2,1,0:T(8,128)(2,1)S(1)}, u32[]{:S(2)}, u32[]{:S(2)}) %collective-permute-start.10) | collective-permute-done | bytes 393248 | tf_op jit(solution)/shard_map/ppermute | solution.py:262
  42.0 0.0 collective-permute-start.11
  42.0 0.0 collective-permute-done.2.mid_x
  42.0 0.5 collective-permute-start.9
  42.5 1.6 %collective-permute-done.9.mid_x_far = bf16[2,128,512]{2,1,0:T(8,128)(2,1)S(1)} collective-permute-done((bf16[2,128,512]{2,1,0:T(8,128)(2,1)S(1)}, bf16[2,128,512]{2,1,0:T(8,128)(2,1)S(1)}, u32[]{:S(2)}, u32[]{:S(2)}) %collective-permute-start.9) | collective-permute-done | bytes 262176 | tf_op jit(solution)/shard_map/ppermute | solution.py:254
  44.1 0.0 collective-permute-done.11.far_far
  44.1 3.0 %late_sent.1 = bf16[3,256,256]{2,1,0:T(8,128)(2,1)S(1)} custom-call(s32[4,12]{1,0:T(4,128)S(1)} %copy-done.1, s32[12]{0:T(128)S(1)} %copy-done.2, s32[12]{0:T(128)S(1)} %copy-done.3, bf16[3,128,512]{2,1,0:T(8,128)(2,1)S(1)} %collective-permute-done.mid, bf16[2,128,512]{2,1,0:T(8,128)(2,1)S(1)} %collective-permute-done.2.mid_x, ...), custom_call_target="tpu_custom_call" | custom-call | flops 805306368 | bytes 10354688 | tf_op jit(solution)/shard_map/late_sent/pallas_call | solution.py:274
  47.1 0.7 %collective-permute-start.12 = (bf16[3,256,256]{2,1,0:T(8,128)(2,1)S(1)}, bf16[3,256,256]{2,1,0:T(8,128)(2,1)S(1)}, u32[]{:S(2)}, u32[]{:S(2)}) collective-permute-start(bf16[3,256,256]{2,1,0:T(8,128)(2,1)S(1)} %late_sent.1), channel_id=1, source_target_pairs={{0,2},{2,0},{1,3},{3,1},{4,6},{6,4},{5,7},{7,5},{8,10},{10,8},{9,1... | collective-permute-start | bytes 1179656 | tf_op jit(solution)/shard_map/ppermute | solution.py:254
  47.8 3.0 %late_kept.1.keep = f32[3,256,256]{2,1,0:T(8,128)S(1)} custom-call(s32[4,12]{1,0:T(4,128)S(1)} %copy-done.1, s32[12]{0:T(128)S(1)} %copy-done.2, s32[12]{0:T(128)S(1)} %copy-done.3, bf16[3,128,512]{2,1,0:T(8,128)(2,1)S(1)} %collective-permute-done.mid, bf16[2,128,512]{2,1,0:T(8,128)(2,1)S(1)} %collective-permute-done.2.mid_x, ...), custom_call_target="tpu_custom_call" | custom-call | flops 805306368 | bytes 10747904 | tf_op jit(solution)/shard_map/late_kept/pallas_call | solution.py:274
  50.8 7.5 %collective-permute-done.12.received = bf16[3,256,256]{2,1,0:T(8,128)(2,1)S(1)} collective-permute-done((bf16[3,256,256]{2,1,0:T(8,128)(2,1)S(1)}, bf16[3,256,256]{2,1,0:T(8,128)(2,1)S(1)}, u32[]{:S(2)}, u32[]{:S(2)}) %collective-permute-start.12) | collective-permute-done | bytes 393248 | tf_op jit(solution)/shard_map/ppermute | solution.py:254
  58.4 1.4 %join.1 = bf16[3,256,256]{2,1,0:T(8,128)(2,1)} custom-call(s32[12]{0:T(128)S(1)} %copy-done.2, s32[12]{0:T(128)S(1)} %copy-done.3, f32[3,256,256]{2,1,0:T(8,128)S(1)} %late_kept.1.keep, bf16[3,256,256]{2,1,0:T(8,128)(2,1)S(1)} %collective-permute-done.12.received), custom_call_target="tpu_custom_call" | custom-call | bytes 1572864 | tf_op jit(solution)/shard_map/join/pallas_call | solution.py:274
Async XLA Ops:
  0.0 11.2 %copy-start = (bf16[3,256,512]{2,1,0:T(8,128)(2,1)S(1)}, bf16[3,256,512]{2,1,0:T(8,128)(2,1)}, u32[]{:S(2)}) copy-start(bf16[3,256,512]{2,1,0:T(8,128)(2,1)} %refs_0_) | copy-start | bytes 2359300
  0.0 31.8 %collective-permute-start.7 = (bf16[2,3,256,512]{3,2,1,0:T(8,128)(2,1)}, bf16[2,3,256,512]{3,2,1,0:T(8,128)(2,1)S(1)}, u32[]{:S(2)}, u32[]{:S(2)}) collective-permute-start(bf16[2,3,256,512]{3,2,1,0:T(8,128)(2,1)} %refs_2_.1), channel_id=1, source_target_pairs={{0,1},{1,0},{2,3},{3,2},{4,5},{5,4},{6,7},{7,6},{8,9},{9,8},{10,11... | collective-permute-start | bytes 4718600 | tf_op jit(solution)/shard_map/ppermute | solution.py:254
  0.5 30.5 %collective-permute-start.8 = (bf16[3,256,512]{2,1,0:T(8,128)(2,1)}, bf16[3,256,512]{2,1,0:T(8,128)(2,1)}, u32[]{:S(2)}, u32[]{:S(2)}) collective-permute-start(bf16[3,256,512]{2,1,0:T(8,128)(2,1)} %refs_0_), channel_id=1, source_target_pairs={{0,1},{1,0},{2,3},{3,2},{4,5},{5,4},{6,7},{7,6},{8,9},{9,8},{10,11... | collective-permute-start | bytes 2359304 | tf_op jit(solution)/shard_map/ppermute | solution.py:254
  4.0 26.4 %collective-permute-start = (bf16[3,128,512]{2,1,0:T(8,128)(2,1)}, bf16[3,128,512]{2,1,0:T(8,128)(2,1)S(1)}, u32[]{:S(2)}, u32[]{:S(2)}) collective-permute-start(bf16[3,128,512]{2,1,0:T(8,128)(2,1)} %get-tuple-element.21), channel_id=1, source_target_pairs={{0,8},{4,12},{8,0},{12,4},{1,9},{5,13},{9,1},{13,5},{2,10},{6,14},... | collective-permute-start | bytes 1179656 | tf_op jit(solution)/shard_map/ppermute | solution.py:262
  8.1 19.4 %collective-permute-start.1 = (bf16[2,256,768]{2,1,0:T(8,128)(2,1)}, bf16[2,256,768]{2,1,0:T(8,128)(2,1)S(1)}, u32[]{:S(2)}, u32[]{:S(2)}) collective-permute-start(bf16[2,256,768]{2,1,0:T(8,128)(2,1)} %get-tuple-element.25), channel_id=1, source_target_pairs={{0,2},{2,0},{1,3},{3,1},{4,6},{6,4},{5,7},{7,5},{8,10},{10,8},{9,1... | collective-permute-start | bytes 2359304 | tf_op jit(solution)/shard_map/ppermute | solution.py:254
  9.6 21.6 %copy-start.1 = (s32[4,12]{1,0:T(4,128)S(1)}, s32[4,12]{1,0:T(4,128)}, u32[]{:S(2)}) copy-start(s32[4,12]{1,0:T(4,128)} %source.11) | copy-start | bytes 580
  9.6 23.8 %copy-start.2 = (s32[12]{0:T(128)S(1)}, s32[12]{0:T(128)}, u32[]{:S(2)}) copy-start(s32[12]{0:T(128)} %left_dims.9) | copy-start | bytes 148
  9.6 23.8 %copy-start.3 = (s32[12]{0:T(128)S(1)}, s32[12]{0:T(128)}, u32[]{:S(2)}) copy-start(s32[12]{0:T(128)} %right_dims.9) | copy-start | bytes 148
  9.6 20.8 %collective-permute-start.3 = (bf16[2,256,512]{2,1,0:T(8,128)(2,1)}, bf16[2,256,512]{2,1,0:T(8,128)(2,1)S(1)}, u32[]{:S(2)}, u32[]{:S(2)}) collective-permute-start(bf16[2,256,512]{2,1,0:T(8,128)(2,1)} %get-tuple-element.28), channel_id=1, source_target_pairs={{0,4},{4,0},{8,12},{12,8},{1,5},{5,1},{9,13},{13,9},{2,6},{6,2},{1... | collective-permute-start | bytes 1572872 | tf_op jit(solution)/shard_map/ppermute | solution.py:262
  27.5 5.9 %collective-permute-start.6 = (bf16[2,256,768]{2,1,0:T(8,128)(2,1)S(1)}, bf16[2,256,768]{2,1,0:T(8,128)(2,1)S(1)}, u32[]{:S(2)}, u32[]{:S(2)}) collective-permute-start(bf16[2,256,768]{2,1,0:T(8,128)(2,1)S(1)} %collective-permute-done.1.env_x), channel_id=1, source_target_pairs={{0,1},{1,0},{2,3},{3,2},{4,5},{5,4},{6,7},{7,6},{8,9},{9,8},{10,11... | collective-permute-start | bytes 2359304 | tf_op jit(solution)/shard_map/ppermute | solution.py:254
  30.4 3.0 %collective-permute-start.4 = (bf16[2,256,512]{2,1,0:T(8,128)(2,1)S(1)}, bf16[2,256,512]{2,1,0:T(8,128)(2,1)S(1)}, u32[]{:S(2)}, u32[]{:S(2)}) collective-permute-start(bf16[2,256,512]{2,1,0:T(8,128)(2,1)S(1)} %collective-permute-done.3.near), channel_id=1, source_target_pairs={{0,1},{1,0},{2,3},{3,2},{4,5},{5,4},{6,7},{7,6},{8,9},{9,8},{10,11... | collective-permute-start | bytes 1572872 | tf_op jit(solution)/shard_map/ppermute | solution.py:254
  30.4 3.0 %collective-permute-start.5 = (bf16[3,128,512]{2,1,0:T(8,128)(2,1)S(1)}, bf16[3,128,512]{2,1,0:T(8,128)(2,1)S(1)}, u32[]{:S(2)}, u32[]{:S(2)}) collective-permute-start(bf16[3,128,512]{2,1,0:T(8,128)(2,1)S(1)} %collective-permute-done.mid), channel_id=1, source_target_pairs={{0,1},{1,0},{2,3},{3,2},{4,5},{5,4},{6,7},{7,6},{8,9},{9,8},{10,11... | collective-permute-start | bytes 1179656 | tf_op jit(solution)/shard_map/ppermute | solution.py:254
  30.9 11.1 %collective-permute-start.10 = (bf16[3,128,512]{2,1,0:T(8,128)(2,1)S(1)}, bf16[3,128,512]{2,1,0:T(8,128)(2,1)S(1)}, u32[]{:S(2)}, u32[]{:S(2)}) collective-permute-start(bf16[3,128,512]{2,1,0:T(8,128)(2,1)S(1)} %collective-permute-done.mid), channel_id=1, source_target_pairs={{0,4},{4,0},{8,12},{12,8},{1,5},{5,1},{9,13},{13,9},{2,6},{6,2},{1... | collective-permute-start | bytes 1179656 | tf_op jit(solution)/shard_map/ppermute | solution.py:262
  31.9 10.2 %collective-permute-start.2 = (bf16[2,128,512]{2,1,0:T(8,128)(2,1)S(1)}, bf16[2,128,512]{2,1,0:T(8,128)(2,1)S(1)}, u32[]{:S(2)}, u32[]{:S(2)}) collective-permute-start(bf16[2,128,512]{2,1,0:T(8,128)(2,1)S(1)} %pick.1), channel_id=1, source_target_pairs={{0,2},{2,0},{1,3},{3,1},{4,6},{6,4},{5,7},{7,5},{8,10},{10,8},{9,1... | collective-permute-start | bytes 786440 | tf_op jit(solution)/shard_map/ppermute | solution.py:254
  42.0 2.1 %collective-permute-start.11 = (bf16[3,128,512]{2,1,0:T(8,128)(2,1)S(1)}, bf16[3,128,512]{2,1,0:T(8,128)(2,1)S(1)}, u32[]{:S(2)}, u32[]{:S(2)}) collective-permute-start(bf16[3,128,512]{2,1,0:T(8,128)(2,1)S(1)} %collective-permute-done.10.far), channel_id=1, source_target_pairs={{0,1},{1,0},{2,3},{3,2},{4,5},{5,4},{6,7},{7,6},{8,9},{9,8},{10,11... | collective-permute-start | bytes 1179656 | tf_op jit(solution)/shard_map/ppermute | solution.py:254
  42.0 2.1 %collective-permute-start.9 = (bf16[2,128,512]{2,1,0:T(8,128)(2,1)S(1)}, bf16[2,128,512]{2,1,0:T(8,128)(2,1)S(1)}, u32[]{:S(2)}, u32[]{:S(2)}) collective-permute-start(bf16[2,128,512]{2,1,0:T(8,128)(2,1)S(1)} %collective-permute-done.2.mid_x), channel_id=1, source_target_pairs={{0,1},{1,0},{2,3},{3,2},{4,5},{5,4},{6,7},{7,6},{8,9},{9,8},{10,11... | collective-permute-start | bytes 786440 | tf_op jit(solution)/shard_map/ppermute | solution.py:254
  47.1 11.2 %collective-permute-start.12 = (bf16[3,256,256]{2,1,0:T(8,128)(2,1)S(1)}, bf16[3,256,256]{2,1,0:T(8,128)(2,1)S(1)}, u32[]{:S(2)}, u32[]{:S(2)}) collective-permute-start(bf16[3,256,256]{2,1,0:T(8,128)(2,1)S(1)} %late_sent.1), channel_id=1, source_target_pairs={{0,2},{2,0},{1,3},{3,1},{4,6},{6,4},{5,7},{7,5},{8,10},{10,8},{9,1... | collective-permute-start | bytes 1179656 | tf_op jit(solution)/shard_map/ppermute | solution.py:254

commit v5 on v4

--- a/solution.py
+++ b/solution.py
@@ -109,21 +109,27 @@
     return slot, local, source
 
 
-def first_kernel(sizes, source, own, left, right, share, near_out, env_out, l_buf, sem):
+def first_kernel(sizes, source_hbm, own, left, right, share, near_out, env_out, source, l_buf, sem):
     pairs, secs, half_rows, blk = sizes
     quarter = half_rows // 2
     z, o, _ = place()
+    rows = pl.ds(pl.multiple_of(o * quarter, quarter), quarter)
+    copies = [
+        pltpu.make_async_copy(source_hbm, source, sem.at[0]),
+        pltpu.make_async_copy(own.at[:, rows], share, sem.at[1]),
+    ]
+    copies[0].start()
+    copies[1].start()
+    copies[0].wait()
     theirs = slots_of(sizes, source, z ^ 1, o)
     mine = slots_of(sizes, source, z, o)
-    moves = [(own.at[:, pl.ds(pl.multiple_of(o * quarter, quarter), quarter)], share)]
-    for j in range(2):
-        moves.append((own.at[ranked(theirs, 1, j)[1]], near_out.at[j]))
+    moves = [(own.at[ranked(theirs, 1, j)[1]], near_out.at[j]) for j in range(2)]
     for j in range(2):
         n = jnp.maximum(ranked(mine, 3, j)[0], 0)
         moves.append((left.at[n // secs, n % secs], l_buf.at[j]))
         moves.append((right.at[n // secs, n % secs], env_out.at[j, :, :blk]))
-    copies = [pltpu.make_async_copy(src, dst, sem.at[i]) for i, (src, dst) in enumerate(moves)]
-    for copy in copies:
+    copies = copies[1:] + [pltpu.make_async_copy(src, dst, sem.at[2 + i]) for i, (src, dst) in enumerate(moves)]
+    for copy in copies[1:]:
         copy.start()
     for copy in copies:
         copy.wait()
@@ -158,25 +164,21 @@
     return jnp.where(row < left_live, part, 0.0).astype(BF16)
 
 
-def early_kernel(kind, sizes, source, left_dims, right_dims, near, near_far, left, right, right_far, *rest):
+def own_kernel(sizes, source, left_dims, right_dims, own, own_far, left, right, right_far, acc, m_buf):
     pairs, secs, half_rows, blk = sizes
-    acc, m_buf = rest[-2:]
     z, o, h = place()
     slots = slots_of(sizes, source, z, o)
-    mine = pl.ds(pl.multiple_of(h * half_rows, half_rows), half_rows)
-    far = pl.ds(pl.multiple_of((1 - h) * half_rows, half_rows), half_rows)
-    acc[...] = rest[0][...] if kind == 1 else jnp.zeros_like(acc)
+    acc[...] = jnp.zeros_like(acc)
     row = lax.broadcasted_iota(jnp.int32, (blk, 1), 0)
     for j in range(2):
-        n, local, src = ranked(slots, kind, j)
+        n, local, src = ranked(slots, 0, j)
 
         @pl.when(n >= 0)
         def _():
             k, t = n // secs, n % secs
             live = live_columns(sizes, right_dims, src)
-            at = j if kind == 1 else local
-            m_buf[mine] = near[at] * live
-            m_buf[far] = near_far[at] * live
+            for half, ref in ((h, own), (1 - h, own_far)):
+                m_buf[pl.ds(pl.multiple_of(half * half_rows, half_rows), half_rows)] = ref[local] * live
             r = jnp.concatenate(
                 [jnp.where(h == 0, right[k, t], right_far[k, t]), jnp.where(h == 0, right_far[k, t], right[k, t])],
                 axis=0,
@@ -186,7 +188,7 @@
 
 
 def late_kernel(
-    kept, sizes, source, left_dims, right_dims, mid, mid_x, mid_far, mid_x_far, far, far_far,
+    kept, sizes, source, left_dims, right_dims, near, near_far, mid, mid_x, mid_far, mid_x_far, far, far_far,
     left, right, right_far, env_x, env_x_far, early, out, total,
 ):
     pairs, secs, half_rows, blk = sizes
@@ -196,47 +198,36 @@
     theirs = slots_of(sizes, source, z, 1 - o)
     side = o if kept else 1 - o
     total[...] = early[:, :, pl.ds(pl.multiple_of(side * half_rows, half_rows), half_rows)]
-    at = lax.broadcasted_iota(jnp.int32, (quarter, 1), 0)
-
-    def product(m_pieces, firsts, left_pieces, r, n, src):
+    parts = []
+
+    def add(slot, pieces, firsts, env=None):
+        n, _, src = slot
+        k, t = jnp.maximum(n, 0) // secs, jnp.maximum(n, 0) % secs
+        size = pieces[0].shape[0]
+        if env is None:
+            r = jnp.where(side == h, right[k, t], right_far[k, t])
+            lefts = [left[k, t, :, pl.ds(pl.multiple_of(first, size), size)] for first in firsts]
+        else:
+            r = jnp.where(side == h, env_x[env, :, :blk], env_x_far[env, :, :blk])
+            lefts = [env_x[env, :, pl.ds(pl.multiple_of(blk + half * quarter, quarter), quarter)] for half in (h, 1 - h)]
+        at = lax.broadcasted_iota(jnp.int32, (size, 1), 0)
+        row = jnp.concatenate([at + first for first in firsts], axis=0)
         live = live_columns(sizes, right_dims, src)
-        row = jnp.concatenate([at + first for first in firsts], axis=0)
         left_live = jnp.where(n >= 0, left_dims[src], 0)
-        part = times_right(jnp.concatenate(m_pieces, axis=0), r * live, row, left_live)
-        return jnp.dot(jnp.concatenate(left_pieces, axis=1), part, preferred_element_type=F32)
-
-    def columns(ref, k, t, first):
-        return ref[k, t, :, pl.ds(pl.multiple_of(first, quarter), quarter)]
-
-    found = []
+        part = times_right(jnp.concatenate(pieces, axis=0), r * live, row, left_live)
+        parts.append((t, jnp.concatenate(lefts, axis=1), part))
+
+    halves = [h * half_rows, (1 - h) * half_rows]
+    ops = [o * quarter, (1 - o) * quarter]
     for j in range(2):
-        n, local, src = ranked(mine, 2, j)
-        k, t = jnp.maximum(n, 0) // secs, jnp.maximum(n, 0) % secs
-        firsts = [half * half_rows + op * quarter for half, op in ((h, o), (h, 1 - o), (1 - h, o), (1 - h, 1 - o))]
-        pieces = [mid[local], mid_x[j], mid_far[local], mid_x_far[j]]
-        lefts = [columns(left, k, t, first) for first in firsts]
-        r = jnp.where(side == h, right[k, t], right_far[k, t])
-        found.append((t, product(pieces, firsts, lefts, r, n, src)))
-
-    firsts = [h * half_rows + o * quarter, (1 - h) * half_rows + o * quarter]
-    for i in range(4):
-        j = i % 2
-        n, local, src = ranked(mine if i < 2 else theirs, 3, j)
-        k, t = jnp.maximum(n, 0) // secs, jnp.maximum(n, 0) % secs
-        pieces = [far[local], far_far[local]]
-        if i < 2:
-            r = jnp.where(side == h, right[k, t], right_far[k, t])
-            lefts = [columns(left, k, t, first) for first in firsts]
-        else:
-            r = jnp.where(side == h, env_x[j, :, :blk], env_x_far[j, :, :blk])
-            lefts = [
-                env_x[j, :, pl.ds(pl.multiple_of(blk + first, quarter), quarter)]
-                for first in (h * quarter, (1 - h) * quarter)
-            ]
-        found.append((t, product(pieces, firsts, lefts, r, n, src)))
-
-    for t, term in found:
-        total[t] += term
+        add(ranked(mine, 1, j), [near[j], near_far[j]], halves)
+        slot = ranked(mine, 2, j)
+        pieces = [mid[slot[1]], mid_x[j], mid_far[slot[1]], mid_x_far[j]]
+        add(slot, pieces, [half + op for half in halves for op in ops])
+        for slot, env in ((ranked(mine, 3, j), None), (ranked(theirs, 3, j), j)):
+            add(slot, [far[slot[1]], far_far[slot[1]]], [half + ops[0] for half in halves], env)
+    for t, l, part in parts:
+        total[t] += jnp.dot(l, part, preferred_element_type=F32)
     out[...] = total[...].astype(out.dtype)
 
 
@@ -287,14 +278,14 @@
     share, near_out, env_out = call(
         first_kernel,
         "first",
+        [((secs, quarter, blk), BF16), ((2, half_rows, blk), BF16), ((2, half_rows, blk + half_rows), BF16)],
+        (),
+        (source, wavefunction, left_env, right_env),
         [
-            ((secs, quarter, blk), BF16),
-            ((2, half_rows, blk), BF16),
-            ((2, half_rows, blk + half_rows), BF16),
+            pltpu.SMEM(source.shape, source.dtype),
+            pltpu.VMEM((2, half_rows, blk), BF16),
+            pltpu.SemaphoreType.DMA((8,)),
         ],
-        (source,),
-        (wavefunction, left_env, right_env),
-        [pltpu.VMEM((2, half_rows, blk), BF16), pltpu.SemaphoreType.DMA((7,))],
         space=pltpu.HBM,
         limit=VMEM_MOST,
     )
@@ -303,7 +294,7 @@
     env_x = swap(env_out, "op")
     own_far = swap(wavefunction, "half")
     right_far = swap(right_env, "half")
-    loaded = (after(wavefunction, share), left_env, right_env)
+    loaded = (after(wavefunction, env_out), left_env, right_env)
     own, left, right = call(
         load_kernel,
         "load",
@@ -316,29 +307,30 @@
         limit=VMEM_MUCH,
     )
     mid, near, env_x, own_far, right_far = (after(x, own) for x in (mid, near, env_x, own_far, right_far))
+    envs = (left, right, right_far)
+
     far = exchange(mid, 1)
-    envs = (left, right, right_far)
-    total = [((secs, half_rows, blk), F32)]
-    block = [pltpu.VMEM((blk, blk), BF16)]
-    (picked,) = call(pick_kernel, "pick", [((2, quarter, blk), BF16)], (source,), (after(mid, env_x),))
+    (picked,) = call(pick_kernel, "pick", [((2, quarter, blk), BF16)], (source,), (mid,))
     mid_x = swap(picked, "op")
-    near_far = swap(near, "half")
-    mid_far = swap(mid, "half")
-    env_x_far = swap(env_x, "half")
-    (early,) = call(functools.partial(early_kernel, 0), "own_slots", total, dims, (own, own_far, *envs), block)
     (early,) = call(
-        functools.partial(early_kernel, 1),
-        "near_slots",
-        total,
+        own_kernel,
+        "own_slots",
+        [((secs, half_rows, blk), F32)],
         dims,
-        (near, after(near_far, mid_far, env_x_far), *envs, early),
-        block,
+        (own, after(own_far, picked), *envs),
+        [pltpu.VMEM((blk, blk), BF16)],
         flops=FILL,
     )
-    mid_x, far = after(mid_x, early), after(far, early)
+    mid_x, env_x = after(mid_x, early), after(env_x, early)
     mid_x_far = swap(mid_x, "half")
-    far_far = swap(far, "half")
-    arrays = (mid, mid_x, mid_far, mid_x_far, far, far_far, *envs, env_x, env_x_far, early)
+    mid_far = swap(after(mid, mid_x), "half")
+    env_x_far = swap(after(env_x, mid_x), "half")
+    far = after(far, early, mid_x_far)
+    near = after(near, mid_x)
+    arrays = (
+        near, swap(near, "half"), mid, mid_x, mid_far, mid_x_far, far, swap(far, "half"),
+        *envs, env_x, env_x_far, early,
+    )
     buffers = [pltpu.VMEM((secs, half_rows, half_rows), F32)]
     flops = 2 * 3 * half_rows * blk * blk * 2
     columns = (secs, half_rows, half_rows)

time: 60 us -> 55.4 us (0.923)
  Pallas kernels: 17.6 us -> 14.2 us
  waiting for transfers between devices: 30.9 us -> 28.2 us
  starting transfers between devices: 11.2 us -> 12.7 us
    ppermute x10, waiting for transfers between devices: 23.5 us -> 14.2 us  [swap(): return lax.ppermute(x, axis, [(0, 1), (1, 0)])]
    ppermute x3, waiting for transfers between devices: 7.35 us -> 14 us  [exchange(): return lax.ppermute(x, 'sector', [(i, i ^ kind) for i in range(4)])]
    pallas_call x8 -> x7, Pallas kernels: 17.6 us -> 14.2 us  [call(): pl.pallas_call(functools.partial(kernel, sizes), out_shape=shapes, in_spe...]
    ppermute x10, starting transfers between devices: 5.25 us -> 6.21 us  [swap(): return lax.ppermute(x, axis, [(0, 1), (1, 0)])]
  transfers between devices with their start and end apart: 13 -> 13, of which waited for: 5 -> 8; matrix products, arithmetic and copies ran while one was open for 0% -> 0% of each run, Pallas kernels for 22% -> 19%
where the time goes in v5:
time: 55.4 us; the launch traced here: 55.2 us
  waiting for transfers between devices  28.2 us (51%)
  Pallas kernels  14.2 us (26%)
  starting transfers between devices  12.7 us (23%)
    pallas_call x7, Pallas kernels, call(): pl.pallas_call(functools.partial(kernel, sizes), out_shape=shapes, in_spe...  14.2 us
    ppermute x10, waiting for transfers between devices, swap(): return lax.ppermute(x, axis, [(0, 1), (1, 0)])  14.2 us
    ppermute x3, waiting for transfers between devices, exchange(): return lax.ppermute(x, 'sector', [(i, i ^ kind) for i in range(4)])  14 us
    ppermute x3, starting transfers between devices, exchange(): return lax.ppermute(x, 'sector', [(i, i ^ kind) for i in range(4)])  6.5 us
    ppermute x10, starting transfers between devices, swap(): return lax.ppermute(x, axis, [(0, 1), (1, 0)])  6.21 us
  transfers between devices with their start and end apart: 13, of which 8 were waited for; matrix products, arithmetic and copies ran while one was open for 0% of the time, Pallas kernels for 19%

profile of v5, /device:TPU:0, one launch (start us, length us, event | category | flops | bytes accessed | tf_op | source)
XLA Modules:
  0.0 55.2 jit_solution(11947516749658916280)
XLA Ops:
  0.0 0.0 copy-start
  0.0 0.5 collective-permute-start.3
  0.5 0.1 collective-permute-start.4
  0.5 3.4 %first.1 = (bf16[3,128,512]{2,1,0:T(8,128)(2,1)}, bf16[2,256,512]{2,1,0:T(8,128)(2,1)}, bf16[2,256,768]{2,1,0:T(8,128)(2,1)}) custom-call(s32[4,12]{1,0:T(4,128)} %source.7, bf16[3,256,512]{2,1,0:T(8,128)(2,1)} %refs_0_, bf16[2,3,256,512]{3,2,1,0:T(8,128)(2,1)} %refs_1_.1, bf16[2,3,256,512]{3,2,1,0:T(8,128)(2,1)} %refs_2_.1), custom_call_target="tpu_custom_call" | custom-call | bytes 5636288 | tf_op jit(solution)/shard_map/first/pallas_call | solution.py:265
  3.9 4.1 %collective-permute-start.1 = (bf16[3,128,512]{2,1,0:T(8,128)(2,1)}, bf16[3,128,512]{2,1,0:T(8,128)(2,1)S(1)}, u32[]{:S(2)}, u32[]{:S(2)}) collective-permute-start(bf16[3,128,512]{2,1,0:T(8,128)(2,1)} %get-tuple-element.29), channel_id=1, source_target_pairs={{0,8},{4,12},{8,0},{12,4},{1,9},{5,13},{9,1},{13,5},{2,10},{6,14},... | collective-permute-start | bytes 1179656 | tf_op jit(solution)/shard_map/ppermute | solution.py:253
  8.0 1.6 %collective-permute-start = (bf16[2,256,512]{2,1,0:T(8,128)(2,1)}, bf16[2,256,512]{2,1,0:T(8,128)(2,1)S(1)}, u32[]{:S(2)}, u32[]{:S(2)}) collective-permute-start(bf16[2,256,512]{2,1,0:T(8,128)(2,1)} %get-tuple-element.24), channel_id=1, source_target_pairs={{0,4},{4,0},{8,12},{12,8},{1,5},{5,1},{9,13},{13,9},{2,6},{6,2},{1... | collective-permute-start | bytes 1572872 | tf_op jit(solution)/shard_map/ppermute | solution.py:253
  9.6 0.0 copy-start.1
  9.6 0.0 copy-start.2
  9.6 0.0 copy-start.3
  9.6 1.5 %collective-permute-start.10 = (bf16[2,256,768]{2,1,0:T(8,128)(2,1)}, bf16[2,256,768]{2,1,0:T(8,128)(2,1)S(1)}, u32[]{:S(2)}, u32[]{:S(2)}) collective-permute-start(bf16[2,256,768]{2,1,0:T(8,128)(2,1)} %get-tuple-element.25), channel_id=1, source_target_pairs={{0,2},{2,0},{1,3},{3,1},{4,6},{6,4},{5,7},{7,5},{8,10},{10,8},{9,1... | collective-permute-start | bytes 2359304 | tf_op jit(solution)/shard_map/ppermute | solution.py:245
  11.1 0.0 copy-done
  11.1 2.0 %load.1 = (bf16[3,256,512]{2,1,0:T(8,128)(2,1)S(1)}, bf16[2,3,256,512]{3,2,1,0:T(8,128)(2,1)S(1)}, bf16[2,3,256,512]{3,2,1,0:T(8,128)(2,1)S(1)}) custom-call(bf16[3,256,512]{2,1,0:T(8,128)(2,1)S(1)} %copy-done, bf16[2,3,256,512]{3,2,1,0:T(8,128)(2,1)} %refs_1_.1, bf16[2,3,256,512]{3,2,1,0:T(8,128)(2,1)} %refs_2_.1), custom_call_target="tpu_custom_call" | custom-call | flops 30000001024 | bytes 7864320 | tf_op jit(solution)/shard_map/load/pallas_call | solution.py:265
  13.1 13.0 %collective-permute-done.1.mid = bf16[3,128,512]{2,1,0:T(8,128)(2,1)S(1)} collective-permute-done((bf16[3,128,512]{2,1,0:T(8,128)(2,1)}, bf16[3,128,512]{2,1,0:T(8,128)(2,1)S(1)}, u32[]{:S(2)}, u32[]{:S(2)}) %collective-permute-start.1) | collective-permute-done | bytes 393248 | tf_op jit(solution)/shard_map/ppermute | solution.py:253
  26.1 0.0 copy-done.1
  26.1 0.7 %pick.1 = bf16[2,128,512]{2,1,0:T(8,128)(2,1)S(1)} custom-call(s32[4,12]{1,0:T(4,128)S(1)} %copy-done.1, bf16[3,128,512]{2,1,0:T(8,128)(2,1)S(1)} %collective-permute-done.1.mid), custom_call_target="tpu_custom_call" | custom-call | bytes 655360 | tf_op jit(solution)/shard_map/pick/pallas_call | solution.py:265
  26.8 0.8 %collective-permute-start.8 = (bf16[3,128,512]{2,1,0:T(8,128)(2,1)S(1)}, bf16[3,128,512]{2,1,0:T(8,128)(2,1)S(1)}, u32[]{:S(2)}, u32[]{:S(2)}) collective-permute-start(bf16[3,128,512]{2,1,0:T(8,128)(2,1)S(1)} %collective-permute-done.1.mid), channel_id=1, source_target_pairs={{0,4},{4,0},{8,12},{12,8},{1,5},{5,1},{9,13},{13,9},{2,6},{6,2},{1... | collective-permute-start | bytes 1179656 | tf_op jit(solution)/shard_map/ppermute | solution.py:253
  27.6 1.2 %collective-permute-done.10.env_x = bf16[2,256,768]{2,1,0:T(8,128)(2,1)S(1)} collective-permute-done((bf16[2,256,768]{2,1,0:T(8,128)(2,1)}, bf16[2,256,768]{2,1,0:T(8,128)(2,1)S(1)}, u32[]{:S(2)}, u32[]{:S(2)}) %collective-permute-start.10) | collective-permute-done | bytes 786464 | tf_op jit(solution)/shard_map/ppermute | solution.py:245
  28.8 1.5 %collective-permute-start.2 = (bf16[2,128,512]{2,1,0:T(8,128)(2,1)S(1)}, bf16[2,128,512]{2,1,0:T(8,128)(2,1)S(1)}, u32[]{:S(2)}, u32[]{:S(2)}) collective-permute-start(bf16[2,128,512]{2,1,0:T(8,128)(2,1)S(1)} %pick.1), channel_id=1, source_target_pairs={{0,2},{2,0},{1,3},{3,1},{4,6},{6,4},{5,7},{7,5},{8,10},{10,8},{9,1... | collective-permute-start | bytes 786440 | tf_op jit(solution)/shard_map/ppermute | solution.py:245
  30.3 0.0 collective-permute-done.3.own_far
  30.3 0.0 collective-permute-done.4.right_far
  30.3 0.0 copy-done.2
  30.3 0.0 copy-done.3
  30.3 2.0 %own_slots.1.early = f32[3,256,512]{2,1,0:T(8,128)S(1)} custom-call(s32[4,12]{1,0:T(4,128)S(1)} %copy-done.1, s32[12]{0:T(128)S(1)} %copy-done.2, s32[12]{0:T(128)S(1)} %copy-done.3, bf16[3,256,512]{2,1,0:T(8,128)(2,1)S(1)} %get-tuple-element.27.own, bf16[3,256,512]{2,1,0:T(8,128)(2,1)} %collective-permute-done.3.own_far, ...), custom_call_target="tpu_custom_call" | custom-call | flops 30000001024 | bytes 7864320 | tf_op jit(solution)/shard_map/own_slots/pallas_call | solution.py:265
  32.3 3.3 %collective-permute-done.2.mid_x = bf16[2,128,512]{2,1,0:T(8,128)(2,1)S(1)} collective-permute-done((bf16[2,128,512]{2,1,0:T(8,128)(2,1)S(1)}, bf16[2,128,512]{2,1,0:T(8,128)(2,1)S(1)}, u32[]{:S(2)}, u32[]{:S(2)}) %collective-permute-start.2) | collective-permute-done | bytes 262176 | tf_op jit(solution)/shard_map/ppermute | solution.py:245
  35.6 0.0 collective-permute-start.11
  35.6 0.5 collective-permute-start.7
  36.1 0.0 collective-permute-done.near
  36.1 0.0 collective-permute-start.5
  36.1 0.5 collective-permute-start.6
  36.6 0.9 %collective-permute-done.8.far = bf16[3,128,512]{2,1,0:T(8,128)(2,1)S(1)} collective-permute-done((bf16[3,128,512]{2,1,0:T(8,128)(2,1)S(1)}, bf16[3,128,512]{2,1,0:T(8,128)(2,1)S(1)}, u32[]{:S(2)}, u32[]{:S(2)}) %collective-permute-start.8) | collective-permute-done | bytes 393248 | tf_op jit(solution)/shard_map/ppermute | solution.py:253
  37.6 0.7 %collective-permute-done.7.mid_x_far = bf16[2,128,512]{2,1,0:T(8,128)(2,1)S(1)} collective-permute-done((bf16[2,128,512]{2,1,0:T(8,128)(2,1)S(1)}, bf16[2,128,512]{2,1,0:T(8,128)(2,1)S(1)}, u32[]{:S(2)}, u32[]{:S(2)}) %collective-permute-start.7) | collective-permute-done | bytes 262176 | tf_op jit(solution)/shard_map/ppermute | solution.py:245
  38.2 0.1 collective-permute-start.9
  38.4 1.2 %collective-permute-done.6.mid_far = bf16[3,128,512]{2,1,0:T(8,128)(2,1)S(1)} collective-permute-done((bf16[3,128,512]{2,1,0:T(8,128)(2,1)S(1)}, bf16[3,128,512]{2,1,0:T(8,128)(2,1)S(1)}, u32[]{:S(2)}, u32[]{:S(2)}) %collective-permute-start.6) | collective-permute-done | bytes 393248 | tf_op jit(solution)/shard_map/ppermute | solution.py:245
  39.6 0.0 collective-permute-done.5.near_far
  39.6 0.6 %collective-permute-done.9.far_far = bf16[3,128,512]{2,1,0:T(8,128)(2,1)S(1)} collective-permute-done((bf16[3,128,512]{2,1,0:T(8,128)(2,1)S(1)}, bf16[3,128,512]{2,1,0:T(8,128)(2,1)S(1)}, u32[]{:S(2)}, u32[]{:S(2)}) %collective-permute-start.9) | collective-permute-done | bytes 393248 | tf_op jit(solution)/shard_map/ppermute | solution.py:245
  40.1 0.0 collective-permute-done.11.env_x_far
  40.1 2.4 %late_sent.1 = bf16[3,256,256]{2,1,0:T(8,128)(2,1)S(1)} custom-call(s32[4,12]{1,0:T(4,128)S(1)} %copy-done.1, s32[12]{0:T(128)S(1)} %copy-done.2, s32[12]{0:T(128)S(1)} %copy-done.3, bf16[2,256,512]{2,1,0:T(8,128)(2,1)S(1)} %collective-permute-done.near, bf16[2,256,512]{2,1,0:T(8,128)(2,1)S(1)} %collective-permute-done.5.near_far, ...), custom_call_target="tpu_custom_call" | custom-call | flops 805306368 | bytes 11403264 | tf_op jit(solution)/shard_map/late_sent/pallas_call | solution.py:265
  42.5 1.6 %collective-permute-start.12 = (bf16[3,256,256]{2,1,0:T(8,128)(2,1)S(1)}, bf16[3,256,256]{2,1,0:T(8,128)(2,1)S(1)}, u32[]{:S(2)}, u32[]{:S(2)}) collective-permute-start(bf16[3,256,256]{2,1,0:T(8,128)(2,1)S(1)} %late_sent.1), channel_id=1, source_target_pairs={{0,2},{2,0},{1,3},{3,1},{4,6},{6,4},{5,7},{7,5},{8,10},{10,8},{9,1... | collective-permute-start | bytes 1179656 | tf_op jit(solution)/shard_map/ppermute | solution.py:245
  44.1 2.4 %late_kept.1.keep = f32[3,256,256]{2,1,0:T(8,128)S(1)} custom-call(s32[4,12]{1,0:T(4,128)S(1)} %copy-done.1, s32[12]{0:T(128)S(1)} %copy-done.2, s32[12]{0:T(128)S(1)} %copy-done.3, bf16[2,256,512]{2,1,0:T(8,128)(2,1)S(1)} %collective-permute-done.near, bf16[2,256,512]{2,1,0:T(8,128)(2,1)S(1)} %collective-permute-done.5.near_far, ...), custom_call_target="tpu_custom_call" | custom-call | flops 805306368 | bytes 11796480 | tf_op jit(solution)/shard_map/late_kept/pallas_call | solution.py:265
  46.5 7.3 %collective-permute-done.12.received = bf16[3,256,256]{2,1,0:T(8,128)(2,1)S(1)} collective-permute-done((bf16[3,256,256]{2,1,0:T(8,128)(2,1)S(1)}, bf16[3,256,256]{2,1,0:T(8,128)(2,1)S(1)}, u32[]{:S(2)}, u32[]{:S(2)}) %collective-permute-start.12) | collective-permute-done | bytes 393248 | tf_op jit(solution)/shard_map/ppermute | solution.py:245
  53.7 1.4 %join.1 = bf16[3,256,256]{2,1,0:T(8,128)(2,1)} custom-call(s32[12]{0:T(128)S(1)} %copy-done.2, s32[12]{0:T(128)S(1)} %copy-done.3, f32[3,256,256]{2,1,0:T(8,128)S(1)} %late_kept.1.keep, bf16[3,256,256]{2,1,0:T(8,128)(2,1)S(1)} %collective-permute-done.12.received), custom_call_target="tpu_custom_call" | custom-call | bytes 1572864 | tf_op jit(solution)/shard_map/join/pallas_call | solution.py:265
Async XLA Ops:
  0.0 11.1 %copy-start = (bf16[3,256,512]{2,1,0:T(8,128)(2,1)S(1)}, bf16[3,256,512]{2,1,0:T(8,128)(2,1)}, u32[]{:S(2)}) copy-start(bf16[3,256,512]{2,1,0:T(8,128)(2,1)} %refs_0_) | copy-start | bytes 2359300
  0.0 30.3 %collective-permute-start.3 = (bf16[3,256,512]{2,1,0:T(8,128)(2,1)}, bf16[3,256,512]{2,1,0:T(8,128)(2,1)}, u32[]{:S(2)}, u32[]{:S(2)}) collective-permute-start(bf16[3,256,512]{2,1,0:T(8,128)(2,1)} %refs_0_), channel_id=1, source_target_pairs={{0,1},{1,0},{2,3},{3,2},{4,5},{5,4},{6,7},{7,6},{8,9},{9,8},{10,11... | collective-permute-start | bytes 2359304 | tf_op jit(solution)/shard_map/ppermute | solution.py:245
  0.5 29.8 %collective-permute-start.4 = (bf16[2,3,256,512]{3,2,1,0:T(8,128)(2,1)}, bf16[2,3,256,512]{3,2,1,0:T(8,128)(2,1)S(1)}, u32[]{:S(2)}, u32[]{:S(2)}) collective-permute-start(bf16[2,3,256,512]{3,2,1,0:T(8,128)(2,1)} %refs_2_.1), channel_id=1, source_target_pairs={{0,1},{1,0},{2,3},{3,2},{4,5},{5,4},{6,7},{7,6},{8,9},{9,8},{10,11... | collective-permute-start | bytes 4718600 | tf_op jit(solution)/shard_map/ppermute | solution.py:245
  3.9 22.2 %collective-permute-start.1 = (bf16[3,128,512]{2,1,0:T(8,128)(2,1)}, bf16[3,128,512]{2,1,0:T(8,128)(2,1)S(1)}, u32[]{:S(2)}, u32[]{:S(2)}) collective-permute-start(bf16[3,128,512]{2,1,0:T(8,128)(2,1)} %get-tuple-element.29), channel_id=1, source_target_pairs={{0,8},{4,12},{8,0},{12,4},{1,9},{5,13},{9,1},{13,5},{2,10},{6,14},... | collective-permute-start | bytes 1179656 | tf_op jit(solution)/shard_map/ppermute | solution.py:253
  8.0 28.1 %collective-permute-start = (bf16[2,256,512]{2,1,0:T(8,128)(2,1)}, bf16[2,256,512]{2,1,0:T(8,128)(2,1)S(1)}, u32[]{:S(2)}, u32[]{:S(2)}) collective-permute-start(bf16[2,256,512]{2,1,0:T(8,128)(2,1)} %get-tuple-element.24), channel_id=1, source_target_pairs={{0,4},{4,0},{8,12},{12,8},{1,5},{5,1},{9,13},{13,9},{2,6},{6,2},{1... | collective-permute-start | bytes 1572872 | tf_op jit(solution)/shard_map/ppermute | solution.py:253
  9.6 16.5 %copy-start.1 = (s32[4,12]{1,0:T(4,128)S(1)}, s32[4,12]{1,0:T(4,128)}, u32[]{:S(2)}) copy-start(s32[4,12]{1,0:T(4,128)} %source.7) | copy-start | bytes 580
  9.6 20.7 %copy-start.2 = (s32[12]{0:T(128)S(1)}, s32[12]{0:T(128)}, u32[]{:S(2)}) copy-start(s32[12]{0:T(128)} %left_dims.7) | copy-start | bytes 148
  9.6 20.7 %copy-start.3 = (s32[12]{0:T(128)S(1)}, s32[12]{0:T(128)}, u32[]{:S(2)}) copy-start(s32[12]{0:T(128)} %right_dims.7) | copy-start | bytes 148
  9.6 19.2 %collective-permute-start.10 = (bf16[2,256,768]{2,1,0:T(8,128)(2,1)}, bf16[2,256,768]{2,1,0:T(8,128)(2,1)S(1)}, u32[]{:S(2)}, u32[]{:S(2)}) collective-permute-start(bf16[2,256,768]{2,1,0:T(8,128)(2,1)} %get-tuple-element.25), channel_id=1, source_target_pairs={{0,2},{2,0},{1,3},{3,1},{4,6},{6,4},{5,7},{7,5},{8,10},{10,8},{9,1... | collective-permute-start | bytes 2359304 | tf_op jit(solution)/shard_map/ppermute | solution.py:245
  26.8 10.8 %collective-permute-start.8 = (bf16[3,128,512]{2,1,0:T(8,128)(2,1)S(1)}, bf16[3,128,512]{2,1,0:T(8,128)(2,1)S(1)}, u32[]{:S(2)}, u32[]{:S(2)}) collective-permute-start(bf16[3,128,512]{2,1,0:T(8,128)(2,1)S(1)} %collective-permute-done.1.mid), channel_id=1, source_target_pairs={{0,4},{4,0},{8,12},{12,8},{1,5},{5,1},{9,13},{13,9},{2,6},{6,2},{1... | collective-permute-start | bytes 1179656 | tf_op jit(solution)/shard_map/ppermute | solution.py:253
  28.8 6.8 %collective-permute-start.2 = (bf16[2,128,512]{2,1,0:T(8,128)(2,1)S(1)}, bf16[2,128,512]{2,1,0:T(8,128)(2,1)S(1)}, u32[]{:S(2)}, u32[]{:S(2)}) collective-permute-start(bf16[2,128,512]{2,1,0:T(8,128)(2,1)S(1)} %pick.1), channel_id=1, source_target_pairs={{0,2},{2,0},{1,3},{3,1},{4,6},{6,4},{5,7},{7,5},{8,10},{10,8},{9,1... | collective-permute-start | bytes 786440 | tf_op jit(solution)/shard_map/ppermute | solution.py:245
  35.6 4.5 %collective-permute-start.11 = (bf16[2,256,768]{2,1,0:T(8,128)(2,1)S(1)}, bf16[2,256,768]{2,1,0:T(8,128)(2,1)S(1)}, u32[]{:S(2)}, u32[]{:S(2)}) collective-permute-start(bf16[2,256,768]{2,1,0:T(8,128)(2,1)S(1)} %collective-permute-done.10.env_x), channel_id=1, source_target_pairs={{0,1},{1,0},{2,3},{3,2},{4,5},{5,4},{6,7},{7,6},{8,9},{9,8},{10,11... | collective-permute-start | bytes 2359304 | tf_op jit(solution)/shard_map/ppermute | solution.py:245
  35.6 2.7 %collective-permute-start.7 = (bf16[2,128,512]{2,1,0:T(8,128)(2,1)S(1)}, bf16[2,128,512]{2,1,0:T(8,128)(2,1)S(1)}, u32[]{:S(2)}, u32[]{:S(2)}) collective-permute-start(bf16[2,128,512]{2,1,0:T(8,128)(2,1)S(1)} %collective-permute-done.2.mid_x), channel_id=1, source_target_pairs={{0,1},{1,0},{2,3},{3,2},{4,5},{5,4},{6,7},{7,6},{8,9},{9,8},{10,11... | collective-permute-start | bytes 786440 | tf_op jit(solution)/shard_map/ppermute | solution.py:245
  36.1 3.5 %collective-permute-start.5 = (bf16[2,256,512]{2,1,0:T(8,128)(2,1)S(1)}, bf16[2,256,512]{2,1,0:T(8,128)(2,1)S(1)}, u32[]{:S(2)}, u32[]{:S(2)}) collective-permute-start(bf16[2,256,512]{2,1,0:T(8,128)(2,1)S(1)} %collective-permute-done.near), channel_id=1, source_target_pairs={{0,1},{1,0},{2,3},{3,2},{4,5},{5,4},{6,7},{7,6},{8,9},{9,8},{10,11... | collective-permute-start | bytes 1572872 | tf_op jit(solution)/shard_map/ppermute | solution.py:245
  36.1 3.5 %collective-permute-start.6 = (bf16[3,128,512]{2,1,0:T(8,128)(2,1)S(1)}, bf16[3,128,512]{2,1,0:T(8,128)(2,1)S(1)}, u32[]{:S(2)}, u32[]{:S(2)}) collective-permute-start(bf16[3,128,512]{2,1,0:T(8,128)(2,1)S(1)} %collective-permute-done.1.mid), channel_id=1, source_target_pairs={{0,1},{1,0},{2,3},{3,2},{4,5},{5,4},{6,7},{7,6},{8,9},{9,8},{10,11... | collective-permute-start | bytes 1179656 | tf_op jit(solution)/shard_map/ppermute | solution.py:245
  38.2 1.9 %collective-permute-start.9 = (bf16[3,128,512]{2,1,0:T(8,128)(2,1)S(1)}, bf16[3,128,512]{2,1,0:T(8,128)(2,1)S(1)}, u32[]{:S(2)}, u32[]{:S(2)}) collective-permute-start(bf16[3,128,512]{2,1,0:T(8,128)(2,1)S(1)} %collective-permute-done.8.far), channel_id=1, source_target_pairs={{0,1},{1,0},{2,3},{3,2},{4,5},{5,4},{6,7},{7,6},{8,9},{9,8},{10,11... | collective-permute-start | bytes 1179656 | tf_op jit(solution)/shard_map/ppermute | solution.py:245
  42.5 11.2 %collective-permute-start.12 = (bf16[3,256,256]{2,1,0:T(8,128)(2,1)S(1)}, bf16[3,256,256]{2,1,0:T(8,128)(2,1)S(1)}, u32[]{:S(2)}, u32[]{:S(2)}) collective-permute-start(bf16[3,256,256]{2,1,0:T(8,128)(2,1)S(1)} %late_sent.1), channel_id=1, source_target_pairs={{0,2},{2,0},{1,3},{3,1},{4,6},{6,4},{5,7},{7,5},{8,10},{10,8},{9,1... | collective-permute-start | bytes 1179656 | tf_op jit(solution)/shard_map/ppermute | solution.py:245

commit v6 on v5

--- a/solution.py
+++ b/solution.py
@@ -109,33 +109,33 @@
     return slot, local, source
 
 
-def first_kernel(sizes, source_hbm, own, left, right, share, near_out, env_out, source, l_buf, sem):
+def first_kernel(sizes, source_hbm, own, left, right, share, near_out, env_out, source, own_buf, left_buf, sem):
     pairs, secs, half_rows, blk = sizes
     quarter = half_rows // 2
     z, o, _ = place()
-    rows = pl.ds(pl.multiple_of(o * quarter, quarter), quarter)
-    copies = [
-        pltpu.make_async_copy(source_hbm, source, sem.at[0]),
-        pltpu.make_async_copy(own.at[:, rows], share, sem.at[1]),
-    ]
-    copies[0].start()
-    copies[1].start()
+    copies = [pltpu.make_async_copy(source_hbm, source, sem.at[0]), pltpu.make_async_copy(own, own_buf, sem.at[1])]
+    for copy in copies:
+        copy.start()
     copies[0].wait()
+    mine = slots_of(sizes, source, z, o)
+    for j in range(2):
+        n = jnp.maximum(ranked(mine, 3, j)[0], 0)
+        for src, dst in ((right, env_out.at[j]), (left, left_buf.at[j])):
+            copy = pltpu.make_async_copy(src.at[n // secs, n % secs], dst, sem.at[len(copies)])
+            copy.start()
+            copies.append(copy)
     theirs = slots_of(sizes, source, z ^ 1, o)
-    mine = slots_of(sizes, source, z, o)
-    moves = [(own.at[ranked(theirs, 1, j)[1]], near_out.at[j]) for j in range(2)]
-    for j in range(2):
-        n = jnp.maximum(ranked(mine, 3, j)[0], 0)
-        moves.append((left.at[n // secs, n % secs], l_buf.at[j]))
-        moves.append((right.at[n // secs, n % secs], env_out.at[j, :, :blk]))
-    copies = copies[1:] + [pltpu.make_async_copy(src, dst, sem.at[2 + i]) for i, (src, dst) in enumerate(moves)]
-    for copy in copies[1:]:
-        copy.start()
-    for copy in copies:
+    copies[1].wait()
+    share[...] = own_buf[:, pl.ds(pl.multiple_of(o * quarter, quarter), quarter)]
+    for j in range(2):
+        near_out[j] = own_buf[ranked(theirs, 1, j)[1]]
+    for copy in copies[2:]:
         copy.wait()
-    for part in range(2):
-        first = pl.multiple_of(part * half_rows + (1 - o) * quarter, quarter)
-        env_out[:, :, blk + part * quarter : blk + (part + 1) * quarter] = l_buf[:, :, pl.ds(first, quarter)]
+    for j in range(2):
+        for part in range(2):
+            first = pl.multiple_of(part * half_rows + (1 - o) * quarter, quarter)
+            to = j * half_rows + part * quarter
+            env_out[2, :, to : to + quarter] = left_buf[j, :, pl.ds(first, quarter)]
 
 
 def load_kernel(sizes, *refs):
@@ -208,8 +208,11 @@
             r = jnp.where(side == h, right[k, t], right_far[k, t])
             lefts = [left[k, t, :, pl.ds(pl.multiple_of(first, size), size)] for first in firsts]
         else:
-            r = jnp.where(side == h, env_x[env, :, :blk], env_x_far[env, :, :blk])
-            lefts = [env_x[env, :, pl.ds(pl.multiple_of(blk + half * quarter, quarter), quarter)] for half in (h, 1 - h)]
+            r = jnp.where(side == h, env_x[env], env_x_far[env])
+            lefts = [
+                env_x[2, :, pl.ds(pl.multiple_of(env * half_rows + half * quarter, quarter), quarter)]
+                for half in (h, 1 - h)
+            ]
         at = lax.broadcasted_iota(jnp.int32, (size, 1), 0)
         row = jnp.concatenate([at + first for first in firsts], axis=0)
         live = live_columns(sizes, right_dims, src)
@@ -231,14 +234,18 @@
     out[...] = total[...].astype(out.dtype)
 
 
-def join_kernel(sizes, left_dims, right_dims, keep, received, out):
+def join_kernel(sizes, left_dims, right_dims, keep, received, out, held, sem):
     secs, half_rows, blk = sizes[1:]
     z, o, h = place()
     row = h * half_rows + lax.broadcasted_iota(jnp.int32, (half_rows, 1), 0)
     col = o * half_rows + lax.broadcasted_iota(jnp.int32, (1, half_rows), 1)
+    copies = [pltpu.make_async_copy(held.at[t], out.at[t], sem.at[t]) for t in range(secs)]
     for t in range(secs):
         live = (row < left_dims[z * secs + t]) & (col < right_dims[z * secs + t])
-        out[t] = jnp.where(live, keep[t] + received[t].astype(F32), 0.0).astype(BF16)
+        held[t] = jnp.where(live, keep[t] + received[t].astype(F32), 0.0).astype(BF16)
+        copies[t].start()
+    for copy in copies:
+        copy.wait()
 
 
 def swap(x, axis):
@@ -259,7 +266,9 @@
     quarter = half_rows // 2
     sizes = (pairs, secs, half_rows, blk)
 
-    def call(kernel, name, outs, scalars, arrays, scratch=(), flops=0, space=pltpu.VMEM, limit=VMEM_LIMIT):
+    def call(
+        kernel, name, outs, scalars, arrays, scratch=(), flops=0, space=pltpu.VMEM, limit=VMEM_LIMIT, to=pltpu.VMEM
+    ):
         shapes = [jax.ShapeDtypeStruct(shape, dtype) for shape, dtype in outs]
         nbytes = sum(s.size * s.dtype.itemsize for s in [*shapes, *arrays])
         return pl.pallas_call(
@@ -267,7 +276,7 @@
             out_shape=shapes,
             in_specs=[pl.BlockSpec(memory_space=pltpu.SMEM)] * len(scalars)
             + [pl.BlockSpec(memory_space=space)] * len(arrays),
-            out_specs=[pl.BlockSpec(memory_space=pltpu.VMEM)] * len(shapes),
+            out_specs=[pl.BlockSpec(memory_space=to)] * len(shapes),
             scratch_shapes=scratch,
             compiler_params=pltpu.CompilerParams(vmem_limit_bytes=limit),
             cost_estimate=pl.CostEstimate(flops=flops, bytes_accessed=nbytes, transcendentals=0),
@@ -278,13 +287,14 @@
     share, near_out, env_out = call(
         first_kernel,
         "first",
-        [((secs, quarter, blk), BF16), ((2, half_rows, blk), BF16), ((2, half_rows, blk + half_rows), BF16)],
+        [((secs, quarter, blk), BF16), ((2, half_rows, blk), BF16), ((3, half_rows, blk), BF16)],
         (),
         (source, wavefunction, left_env, right_env),
         [
             pltpu.SMEM(source.shape, source.dtype),
+            pltpu.VMEM((secs, half_rows, blk), BF16),
             pltpu.VMEM((2, half_rows, blk), BF16),
-            pltpu.SemaphoreType.DMA((8,)),
+            pltpu.SemaphoreType.DMA((6,)),
         ],
         space=pltpu.HBM,
         limit=VMEM_MOST,
@@ -321,11 +331,11 @@
         [pltpu.VMEM((blk, blk), BF16)],
         flops=FILL,
     )
+    mid_far = swap(mid, "half")
     mid_x, env_x = after(mid_x, early), after(env_x, early)
     mid_x_far = swap(mid_x, "half")
-    mid_far = swap(after(mid, mid_x), "half")
-    env_x_far = swap(after(env_x, mid_x), "half")
-    far = after(far, early, mid_x_far)
+    env_x_far = swap(after(env_x[:2], early), "half")
+    far = after(far, early, mid_x_far, mid_far)
     near = after(near, mid_x)
     arrays = (
         near, swap(near, "half"), mid, mid_x, mid_far, mid_x_far, far, swap(far, "half"),
@@ -341,7 +351,15 @@
     (keep,) = call(
         functools.partial(late_kernel, True), "late_kept", [(columns, F32)], dims, arrays, buffers, flops
     )
-    (out,) = call(join_kernel, "join", [(columns, BF16)], (left_dims, right_dims), (keep, received))
+    (out,) = call(
+        join_kernel,
+        "join",
+        [(columns, BF16)],
+        (left_dims, right_dims),
+        (keep, received),
+        [pltpu.VMEM(columns, BF16), pltpu.SemaphoreType.DMA((secs,))],
+        to=pltpu.HBM,
+    )
     return out
 
 

time: 55.4 us -> 54.3 us (0.980)
  waiting for transfers between devices: 28.2 us -> 27.1 us
    ppermute x10, waiting for transfers between devices: 14.2 us -> 12.8 us  [swap(): return lax.ppermute(x, axis, [(0, 1), (1, 0)])]
  transfers between devices with their start and end apart: 13 -> 13, of which waited for: 8 -> 7; matrix products, arithmetic and copies ran while one was open for 0% -> 0% of each run, Pallas kernels for 19% -> 20%
where the time goes in v6:
time: 54.3 us; the launch traced here: 54.1 us
  waiting for transfers between devices  27.1 us (50%)
  Pallas kernels  14.6 us (27%)
  starting transfers between devices  12.3 us (23%)
    pallas_call x7, Pallas kernels, call(): pl.pallas_call(functools.partial(kernel, sizes), out_shape=shapes, in_spe...  14.6 us
    ppermute x3, waiting for transfers between devices, exchange(): return lax.ppermute(x, 'sector', [(i, i ^ kind) for i in range(4)])  14.3 us
    ppermute x10, waiting for transfers between devices, swap(): return lax.ppermute(x, axis, [(0, 1), (1, 0)])  12.8 us
    ppermute x3, starting transfers between devices, exchange(): return lax.ppermute(x, 'sector', [(i, i ^ kind) for i in range(4)])  6.5 us
    ppermute x10, starting transfers between devices, swap(): return lax.ppermute(x, axis, [(0, 1), (1, 0)])  5.75 us
  transfers between devices with their start and end apart: 13, of which 7 were waited for; matrix products, arithmetic and copies ran while one was open for 0% of the time, Pallas kernels for 20%

profile of v6, /device:TPU:0, one launch (start us, length us, event | category | flops | bytes accessed | tf_op | source)
XLA Modules:
  0.0 54.1 jit_solution(1693077702601177977)
XLA Ops:
  0.0 0.0 copy-start
  0.0 0.5 collective-permute-start.3
  0.5 0.1 collective-permute-start.4
  0.5 3.3 %first.1 = (bf16[3,128,512]{2,1,0:T(8,128)(2,1)}, bf16[2,256,512]{2,1,0:T(8,128)(2,1)}, bf16[3,256,512]{2,1,0:T(8,128)(2,1)}) custom-call(s32[4,12]{1,0:T(4,128)} %source.7, bf16[3,256,512]{2,1,0:T(8,128)(2,1)} %refs_0_, bf16[2,3,256,512]{3,2,1,0:T(8,128)(2,1)} %refs_1_.1, bf16[2,3,256,512]{3,2,1,0:T(8,128)(2,1)} %refs_2_.1), custom_call_target="tpu_custom_call" | custom-call | bytes 5636288 | tf_op jit(solution)/shard_map/first/pallas_call | solution.py:274
  3.8 4.1 %collective-permute-start.1 = (bf16[3,128,512]{2,1,0:T(8,128)(2,1)}, bf16[3,128,512]{2,1,0:T(8,128)(2,1)S(1)}, u32[]{:S(2)}, u32[]{:S(2)}) collective-permute-start(bf16[3,128,512]{2,1,0:T(8,128)(2,1)} %get-tuple-element.28), channel_id=1, source_target_pairs={{0,8},{4,12},{8,0},{12,4},{1,9},{5,13},{9,1},{13,5},{2,10},{6,14},... | collective-permute-start | bytes 1179656 | tf_op jit(solution)/shard_map/ppermute | solution.py:260
  7.9 1.6 %collective-permute-start = (bf16[2,256,512]{2,1,0:T(8,128)(2,1)}, bf16[2,256,512]{2,1,0:T(8,128)(2,1)S(1)}, u32[]{:S(2)}, u32[]{:S(2)}) collective-permute-start(bf16[2,256,512]{2,1,0:T(8,128)(2,1)} %get-tuple-element.23), channel_id=1, source_target_pairs={{0,4},{4,0},{8,12},{12,8},{1,5},{5,1},{9,13},{13,9},{2,6},{6,2},{1... | collective-permute-start | bytes 1572872 | tf_op jit(solution)/shard_map/ppermute | solution.py:260
  9.5 0.0 copy-start.1
  9.5 0.0 copy-start.2
  9.5 0.0 copy-start.3
  9.5 1.5 %collective-permute-start.10 = (bf16[3,256,512]{2,1,0:T(8,128)(2,1)}, bf16[3,256,512]{2,1,0:T(8,128)(2,1)S(1)}, u32[]{:S(2)}, u32[]{:S(2)}) collective-permute-start(bf16[3,256,512]{2,1,0:T(8,128)(2,1)} %get-tuple-element.24), channel_id=1, source_target_pairs={{0,2},{2,0},{1,3},{3,1},{4,6},{6,4},{5,7},{7,5},{8,10},{10,8},{9,1... | collective-permute-start | bytes 2359304 | tf_op jit(solution)/shard_map/ppermute | solution.py:252
  11.0 0.0 copy-done
  11.0 2.0 %load.1 = (bf16[3,256,512]{2,1,0:T(8,128)(2,1)S(1)}, bf16[2,3,256,512]{3,2,1,0:T(8,128)(2,1)S(1)}, bf16[2,3,256,512]{3,2,1,0:T(8,128)(2,1)S(1)}) custom-call(bf16[3,256,512]{2,1,0:T(8,128)(2,1)S(1)} %copy-done, bf16[2,3,256,512]{3,2,1,0:T(8,128)(2,1)} %refs_1_.1, bf16[2,3,256,512]{3,2,1,0:T(8,128)(2,1)} %refs_2_.1), custom_call_target="tpu_custom_call" | custom-call | flops 30000001024 | bytes 7864320 | tf_op jit(solution)/shard_map/load/pallas_call | solution.py:274
  13.0 13.0 %collective-permute-done.1.mid = bf16[3,128,512]{2,1,0:T(8,128)(2,1)S(1)} collective-permute-done((bf16[3,128,512]{2,1,0:T(8,128)(2,1)}, bf16[3,128,512]{2,1,0:T(8,128)(2,1)S(1)}, u32[]{:S(2)}, u32[]{:S(2)}) %collective-permute-start.1) | collective-permute-done | bytes 393248 | tf_op jit(solution)/shard_map/ppermute | solution.py:260
  26.0 0.0 copy-done.1
  26.0 0.7 %pick.1 = bf16[2,128,512]{2,1,0:T(8,128)(2,1)S(1)} custom-call(s32[4,12]{1,0:T(4,128)S(1)} %copy-done.1, bf16[3,128,512]{2,1,0:T(8,128)(2,1)S(1)} %collective-permute-done.1.mid), custom_call_target="tpu_custom_call" | custom-call | bytes 655360 | tf_op jit(solution)/shard_map/pick/pallas_call | solution.py:274
  26.7 0.8 %collective-permute-start.8 = (bf16[3,128,512]{2,1,0:T(8,128)(2,1)S(1)}, bf16[3,128,512]{2,1,0:T(8,128)(2,1)S(1)}, u32[]{:S(2)}, u32[]{:S(2)}) collective-permute-start(bf16[3,128,512]{2,1,0:T(8,128)(2,1)S(1)} %collective-permute-done.1.mid), channel_id=1, source_target_pairs={{0,4},{4,0},{8,12},{12,8},{1,5},{5,1},{9,13},{13,9},{2,6},{6,2},{1... | collective-permute-start | bytes 1179656 | tf_op jit(solution)/shard_map/ppermute | solution.py:260
  27.5 0.0 collective-permute-done.3.own_far
  27.5 1.5 %collective-permute-start.2 = (bf16[2,128,512]{2,1,0:T(8,128)(2,1)S(1)}, bf16[2,128,512]{2,1,0:T(8,128)(2,1)S(1)}, u32[]{:S(2)}, u32[]{:S(2)}) collective-permute-start(bf16[2,128,512]{2,1,0:T(8,128)(2,1)S(1)} %pick.1), channel_id=1, source_target_pairs={{0,2},{2,0},{1,3},{3,1},{4,6},{6,4},{5,7},{7,5},{8,10},{10,8},{9,1... | collective-permute-start | bytes 786440 | tf_op jit(solution)/shard_map/ppermute | solution.py:252
  29.0 0.0 collective-permute-done.4.right_far
  29.0 0.0 collective-permute-start.6
  29.0 0.0 copy-done.2
  29.0 0.0 copy-done.3
  29.0 2.6 %own_slots.1.early = f32[3,256,512]{2,1,0:T(8,128)S(1)} custom-call(s32[4,12]{1,0:T(4,128)S(1)} %copy-done.1, s32[12]{0:T(128)S(1)} %copy-done.2, s32[12]{0:T(128)S(1)} %copy-done.3, bf16[3,256,512]{2,1,0:T(8,128)(2,1)S(1)} %get-tuple-element.26.own, bf16[3,256,512]{2,1,0:T(8,128)(2,1)} %collective-permute-done.3.own_far, ...), custom_call_target="tpu_custom_call" | custom-call | flops 30000001024 | bytes 7864320 | tf_op jit(solution)/shard_map/own_slots/pallas_call | solution.py:274
  31.7 3.8 %collective-permute-done.2.mid_x = bf16[2,128,512]{2,1,0:T(8,128)(2,1)S(1)} collective-permute-done((bf16[2,128,512]{2,1,0:T(8,128)(2,1)S(1)}, bf16[2,128,512]{2,1,0:T(8,128)(2,1)S(1)}, u32[]{:S(2)}, u32[]{:S(2)}) %collective-permute-start.2) | collective-permute-done | bytes 262176 | tf_op jit(solution)/shard_map/ppermute | solution.py:252
  35.5 0.0 collective-permute-start.7
  35.5 0.0 collective-permute-done.near
  35.5 0.0 collective-permute-done.10.env_x
  35.5 0.6 %collective-permute-start.11 = (bf16[2,256,512]{2,1,0:T(8,128)(2,1)S(1)}, bf16[2,256,512]{2,1,0:T(8,128)(2,1)S(1)}, u32[]{:S(2)}, u32[]{:S(2)}) collective-permute-start(bf16[2,256,512]{2,1,0:T(8,128)(2,1)S(1)} %slice.3), channel_id=1, source_target_pairs={{0,1},{1,0},{2,3},{3,2},{4,5},{5,4},{6,7},{7,6},{8,9},{9,8},{10,11... | collective-permute-start | bytes 1572872 | tf_op jit(solution)/shard_map/ppermute | solution.py:252
  36.1 0.1 collective-permute-start.5
  36.2 1.3 %collective-permute-done.8.far = bf16[3,128,512]{2,1,0:T(8,128)(2,1)S(1)} collective-permute-done((bf16[3,128,512]{2,1,0:T(8,128)(2,1)S(1)}, bf16[3,128,512]{2,1,0:T(8,128)(2,1)S(1)}, u32[]{:S(2)}, u32[]{:S(2)}) %collective-permute-start.8) | collective-permute-done | bytes 393248 | tf_op jit(solution)/shard_map/ppermute | solution.py:260
  37.4 0.0 collective-permute-done.6.mid_far
  37.4 0.0 collective-permute-done.7.mid_x_far
  37.4 0.0 collective-permute-start.9
  37.4 0.3 collective-permute-done.11.env_x_far
  37.7 0.7 %collective-permute-done.5.near_far = bf16[2,256,512]{2,1,0:T(8,128)(2,1)S(1)} collective-permute-done((bf16[2,256,512]{2,1,0:T(8,128)(2,1)S(1)}, bf16[2,256,512]{2,1,0:T(8,128)(2,1)S(1)}, u32[]{:S(2)}, u32[]{:S(2)}) %collective-permute-start.5) | collective-permute-done | bytes 524320 | tf_op jit(solution)/shard_map/ppermute | solution.py:252
  38.5 0.7 %collective-permute-done.9.far_far = bf16[3,128,512]{2,1,0:T(8,128)(2,1)S(1)} collective-permute-done((bf16[3,128,512]{2,1,0:T(8,128)(2,1)S(1)}, bf16[3,128,512]{2,1,0:T(8,128)(2,1)S(1)}, u32[]{:S(2)}, u32[]{:S(2)}) %collective-permute-start.9) | collective-permute-done | bytes 393248 | tf_op jit(solution)/shard_map/ppermute | solution.py:252
  39.2 2.4 %late_sent.1 = bf16[3,256,256]{2,1,0:T(8,128)(2,1)S(1)} custom-call(s32[4,12]{1,0:T(4,128)S(1)} %copy-done.1, s32[12]{0:T(128)S(1)} %copy-done.2, s32[12]{0:T(128)S(1)} %copy-done.3, bf16[2,256,512]{2,1,0:T(8,128)(2,1)S(1)} %collective-permute-done.near, bf16[2,256,512]{2,1,0:T(8,128)(2,1)S(1)} %collective-permute-done.5.near_far, ...), custom_call_target="tpu_custom_call" | custom-call | flops 805306368 | bytes 11141120 | tf_op jit(solution)/shard_map/late_sent/pallas_call | solution.py:274
  41.5 1.6 %collective-permute-start.12 = (bf16[3,256,256]{2,1,0:T(8,128)(2,1)S(1)}, bf16[3,256,256]{2,1,0:T(8,128)(2,1)S(1)}, u32[]{:S(2)}, u32[]{:S(2)}) collective-permute-start(bf16[3,256,256]{2,1,0:T(8,128)(2,1)S(1)} %late_sent.1), channel_id=1, source_target_pairs={{0,2},{2,0},{1,3},{3,1},{4,6},{6,4},{5,7},{7,5},{8,10},{10,8},{9,1... | collective-permute-start | bytes 1179656 | tf_op jit(solution)/shard_map/ppermute | solution.py:252
  43.1 2.4 %late_kept.1.keep = f32[3,256,256]{2,1,0:T(8,128)S(1)} custom-call(s32[4,12]{1,0:T(4,128)S(1)} %copy-done.1, s32[12]{0:T(128)S(1)} %copy-done.2, s32[12]{0:T(128)S(1)} %copy-done.3, bf16[2,256,512]{2,1,0:T(8,128)(2,1)S(1)} %collective-permute-done.near, bf16[2,256,512]{2,1,0:T(8,128)(2,1)S(1)} %collective-permute-done.5.near_far, ...), custom_call_target="tpu_custom_call" | custom-call | flops 805306368 | bytes 11534336 | tf_op jit(solution)/shard_map/late_kept/pallas_call | solution.py:274
  45.5 7.3 %collective-permute-done.12.received = bf16[3,256,256]{2,1,0:T(8,128)(2,1)S(1)} collective-permute-done((bf16[3,256,256]{2,1,0:T(8,128)(2,1)S(1)}, bf16[3,256,256]{2,1,0:T(8,128)(2,1)S(1)}, u32[]{:S(2)}, u32[]{:S(2)}) %collective-permute-start.12) | collective-permute-done | bytes 393248 | tf_op jit(solution)/shard_map/ppermute | solution.py:252
  52.8 1.4 %join.1 = bf16[3,256,256]{2,1,0:T(8,128)(2,1)} custom-call(s32[12]{0:T(128)S(1)} %copy-done.2, s32[12]{0:T(128)S(1)} %copy-done.3, f32[3,256,256]{2,1,0:T(8,128)S(1)} %late_kept.1.keep, bf16[3,256,256]{2,1,0:T(8,128)(2,1)S(1)} %collective-permute-done.12.received), custom_call_target="tpu_custom_call" | custom-call | bytes 1572864 | tf_op jit(solution)/shard_map/join/pallas_call | solution.py:274
  (1 shorter events, 0.0 us)
Async XLA Ops:
  0.0 11.0 %copy-start = (bf16[3,256,512]{2,1,0:T(8,128)(2,1)S(1)}, bf16[3,256,512]{2,1,0:T(8,128)(2,1)}, u32[]{:S(2)}) copy-start(bf16[3,256,512]{2,1,0:T(8,128)(2,1)} %refs_0_) | copy-start | bytes 2359300
  0.0 27.5 %collective-permute-start.3 = (bf16[3,256,512]{2,1,0:T(8,128)(2,1)}, bf16[3,256,512]{2,1,0:T(8,128)(2,1)}, u32[]{:S(2)}, u32[]{:S(2)}) collective-permute-start(bf16[3,256,512]{2,1,0:T(8,128)(2,1)} %refs_0_), channel_id=1, source_target_pairs={{0,1},{1,0},{2,3},{3,2},{4,5},{5,4},{6,7},{7,6},{8,9},{9,8},{10,11... | collective-permute-start | bytes 2359304 | tf_op jit(solution)/shard_map/ppermute | solution.py:252
  0.5 28.5 %collective-permute-start.4 = (bf16[2,3,256,512]{3,2,1,0:T(8,128)(2,1)}, bf16[2,3,256,512]{3,2,1,0:T(8,128)(2,1)S(1)}, u32[]{:S(2)}, u32[]{:S(2)}) collective-permute-start(bf16[2,3,256,512]{3,2,1,0:T(8,128)(2,1)} %refs_2_.1), channel_id=1, source_target_pairs={{0,1},{1,0},{2,3},{3,2},{4,5},{5,4},{6,7},{7,6},{8,9},{9,8},{10,11... | collective-permute-start | bytes 4718600 | tf_op jit(solution)/shard_map/ppermute | solution.py:252
  3.8 22.2 %collective-permute-start.1 = (bf16[3,128,512]{2,1,0:T(8,128)(2,1)}, bf16[3,128,512]{2,1,0:T(8,128)(2,1)S(1)}, u32[]{:S(2)}, u32[]{:S(2)}) collective-permute-start(bf16[3,128,512]{2,1,0:T(8,128)(2,1)} %get-tuple-element.28), channel_id=1, source_target_pairs={{0,8},{4,12},{8,0},{12,4},{1,9},{5,13},{9,1},{13,5},{2,10},{6,14},... | collective-permute-start | bytes 1179656 | tf_op jit(solution)/shard_map/ppermute | solution.py:260
  7.9 27.5 %collective-permute-start = (bf16[2,256,512]{2,1,0:T(8,128)(2,1)}, bf16[2,256,512]{2,1,0:T(8,128)(2,1)S(1)}, u32[]{:S(2)}, u32[]{:S(2)}) collective-permute-start(bf16[2,256,512]{2,1,0:T(8,128)(2,1)} %get-tuple-element.23), channel_id=1, source_target_pairs={{0,4},{4,0},{8,12},{12,8},{1,5},{5,1},{9,13},{13,9},{2,6},{6,2},{1... | collective-permute-start | bytes 1572872 | tf_op jit(solution)/shard_map/ppermute | solution.py:260
  9.5 16.5 %copy-start.1 = (s32[4,12]{1,0:T(4,128)S(1)}, s32[4,12]{1,0:T(4,128)}, u32[]{:S(2)}) copy-start(s32[4,12]{1,0:T(4,128)} %source.7) | copy-start | bytes 580
  9.5 19.5 %copy-start.2 = (s32[12]{0:T(128)S(1)}, s32[12]{0:T(128)}, u32[]{:S(2)}) copy-start(s32[12]{0:T(128)} %left_dims.7) | copy-start | bytes 148
  9.5 19.5 %copy-start.3 = (s32[12]{0:T(128)S(1)}, s32[12]{0:T(128)}, u32[]{:S(2)}) copy-start(s32[12]{0:T(128)} %right_dims.7) | copy-start | bytes 148
  9.5 26.0 %collective-permute-start.10 = (bf16[3,256,512]{2,1,0:T(8,128)(2,1)}, bf16[3,256,512]{2,1,0:T(8,128)(2,1)S(1)}, u32[]{:S(2)}, u32[]{:S(2)}) collective-permute-start(bf16[3,256,512]{2,1,0:T(8,128)(2,1)} %get-tuple-element.24), channel_id=1, source_target_pairs={{0,2},{2,0},{1,3},{3,1},{4,6},{6,4},{5,7},{7,5},{8,10},{10,8},{9,1... | collective-permute-start | bytes 2359304 | tf_op jit(solution)/shard_map/ppermute | solution.py:252
  26.7 10.8 %collective-permute-start.8 = (bf16[3,128,512]{2,1,0:T(8,128)(2,1)S(1)}, bf16[3,128,512]{2,1,0:T(8,128)(2,1)S(1)}, u32[]{:S(2)}, u32[]{:S(2)}) collective-permute-start(bf16[3,128,512]{2,1,0:T(8,128)(2,1)S(1)} %collective-permute-done.1.mid), channel_id=1, source_target_pairs={{0,4},{4,0},{8,12},{12,8},{1,5},{5,1},{9,13},{13,9},{2,6},{6,2},{1... | collective-permute-start | bytes 1179656 | tf_op jit(solution)/shard_map/ppermute | solution.py:260
  27.5 8.0 %collective-permute-start.2 = (bf16[2,128,512]{2,1,0:T(8,128)(2,1)S(1)}, bf16[2,128,512]{2,1,0:T(8,128)(2,1)S(1)}, u32[]{:S(2)}, u32[]{:S(2)}) collective-permute-start(bf16[2,128,512]{2,1,0:T(8,128)(2,1)S(1)} %pick.1), channel_id=1, source_target_pairs={{0,2},{2,0},{1,3},{3,1},{4,6},{6,4},{5,7},{7,5},{8,10},{10,8},{9,1... | collective-permute-start | bytes 786440 | tf_op jit(solution)/shard_map/ppermute | solution.py:252
  29.0 8.4 %collective-permute-start.6 = (bf16[3,128,512]{2,1,0:T(8,128)(2,1)S(1)}, bf16[3,128,512]{2,1,0:T(8,128)(2,1)S(1)}, u32[]{:S(2)}, u32[]{:S(2)}) collective-permute-start(bf16[3,128,512]{2,1,0:T(8,128)(2,1)S(1)} %collective-permute-done.1.mid), channel_id=1, source_target_pairs={{0,1},{1,0},{2,3},{3,2},{4,5},{5,4},{6,7},{7,6},{8,9},{9,8},{10,11... | collective-permute-start | bytes 1179656 | tf_op jit(solution)/shard_map/ppermute | solution.py:252
  35.5 2.0 %collective-permute-start.7 = (bf16[2,128,512]{2,1,0:T(8,128)(2,1)S(1)}, bf16[2,128,512]{2,1,0:T(8,128)(2,1)S(1)}, u32[]{:S(2)}, u32[]{:S(2)}) collective-permute-start(bf16[2,128,512]{2,1,0:T(8,128)(2,1)S(1)} %collective-permute-done.2.mid_x), channel_id=1, source_target_pairs={{0,1},{1,0},{2,3},{3,2},{4,5},{5,4},{6,7},{7,6},{8,9},{9,8},{10,11... | collective-permute-start | bytes 786440 | tf_op jit(solution)/shard_map/ppermute | solution.py:252
  35.5 2.2 %collective-permute-start.11 = (bf16[2,256,512]{2,1,0:T(8,128)(2,1)S(1)}, bf16[2,256,512]{2,1,0:T(8,128)(2,1)S(1)}, u32[]{:S(2)}, u32[]{:S(2)}) collective-permute-start(bf16[2,256,512]{2,1,0:T(8,128)(2,1)S(1)} %slice.3), channel_id=1, source_target_pairs={{0,1},{1,0},{2,3},{3,2},{4,5},{5,4},{6,7},{7,6},{8,9},{9,8},{10,11... | collective-permute-start | bytes 1572872 | tf_op jit(solution)/shard_map/ppermute | solution.py:252
  36.1 2.4 %collective-permute-start.5 = (bf16[2,256,512]{2,1,0:T(8,128)(2,1)S(1)}, bf16[2,256,512]{2,1,0:T(8,128)(2,1)S(1)}, u32[]{:S(2)}, u32[]{:S(2)}) collective-permute-start(bf16[2,256,512]{2,1,0:T(8,128)(2,1)S(1)} %collective-permute-done.near), channel_id=1, source_target_pairs={{0,1},{1,0},{2,3},{3,2},{4,5},{5,4},{6,7},{7,6},{8,9},{9,8},{10,11... | collective-permute-start | bytes 1572872 | tf_op jit(solution)/shard_map/ppermute | solution.py:252
  37.4 1.7 %collective-permute-start.9 = (bf16[3,128,512]{2,1,0:T(8,128)(2,1)S(1)}, bf16[3,128,512]{2,1,0:T(8,128)(2,1)S(1)}, u32[]{:S(2)}, u32[]{:S(2)}) collective-permute-start(bf16[3,128,512]{2,1,0:T(8,128)(2,1)S(1)} %collective-permute-done.8.far), channel_id=1, source_target_pairs={{0,1},{1,0},{2,3},{3,2},{4,5},{5,4},{6,7},{7,6},{8,9},{9,8},{10,11... | collective-permute-start | bytes 1179656 | tf_op jit(solution)/shard_map/ppermute | solution.py:252
  41.5 11.2 %collective-permute-start.12 = (bf16[3,256,256]{2,1,0:T(8,128)(2,1)S(1)}, bf16[3,256,256]{2,1,0:T(8,128)(2,1)S(1)}, u32[]{:S(2)}, u32[]{:S(2)}) collective-permute-start(bf16[3,256,256]{2,1,0:T(8,128)(2,1)S(1)} %late_sent.1), channel_id=1, source_target_pairs={{0,2},{2,0},{1,3},{3,1},{4,6},{6,4},{5,7},{7,5},{8,10},{10,8},{9,1... | collective-permute-start | bytes 1179656 | tf_op jit(solution)/shard_map/ppermute | solution.py:252

commit v7 on v6

--- a/solution.py
+++ b/solution.py
@@ -302,8 +302,8 @@
     mid = exchange(share, 2)
     near = exchange(near_out, 1)
     env_x = swap(env_out, "op")
-    own_far = swap(wavefunction, "half")
-    right_far = swap(right_env, "half")
+    own_far = swap(after(wavefunction, share), "half")
+    right_far = swap(after(right_env, share), "half")
     loaded = (after(wavefunction, env_out), left_env, right_env)
     own, left, right = call(
         load_kernel,

time: 54.3 us -> 53.8 us (level)
    ppermute x10, waiting for transfers between devices: 12.8 us -> 13.5 us  [swap(): return lax.ppermute(x, axis, [(0, 1), (1, 0)])]
    ppermute x3, waiting for transfers between devices: 14.3 us -> 13.8 us  [exchange(): return lax.ppermute(x, 'sector', [(i, i ^ kind) for i in range(4)])]
  transfers between devices with their start and end apart: 13 -> 13, of which waited for: 7 -> 7; matrix products, arithmetic and copies ran while one was open for 0% -> 0% of each run, Pallas kernels for 20% -> 13%
where the time goes in v7:
time: 53.8 us; the launch traced here: 53.6 us
  waiting for transfers between devices  27.2 us (51%)
  Pallas kernels  14.3 us (27%)
  starting transfers between devices  12 us (22%)
    pallas_call x7, Pallas kernels, call(): pl.pallas_call(functools.partial(kernel, sizes), out_shape=shapes, in_spe...  14.3 us
    ppermute x3, waiting for transfers between devices, exchange(): return lax.ppermute(x, 'sector', [(i, i ^ kind) for i in range(4)])  13.8 us
    ppermute x10, waiting for transfers between devices, swap(): return lax.ppermute(x, axis, [(0, 1), (1, 0)])  13.5 us
    ppermute x3, starting transfers between devices, exchange(): return lax.ppermute(x, 'sector', [(i, i ^ kind) for i in range(4)])  6.51 us
    ppermute x10, starting transfers between devices, swap(): return lax.ppermute(x, axis, [(0, 1), (1, 0)])  5.47 us
  transfers between devices with their start and end apart: 13, of which 7 were waited for; matrix products, arithmetic and copies ran while one was open for 0% of the time, Pallas kernels for 13%

profile of v7, /device:TPU:0, one launch (start us, length us, event | category | flops | bytes accessed | tf_op | source)
XLA Modules:
  0.0 53.6 jit_solution(4241784462757020604)
XLA Ops:
  0.0 0.0 copy-start.4
  0.0 0.0 copy-start
  0.0 3.5 %first.1 = (bf16[3,128,512]{2,1,0:T(8,128)(2,1)}, bf16[2,256,512]{2,1,0:T(8,128)(2,1)}, bf16[3,256,512]{2,1,0:T(8,128)(2,1)}) custom-call(s32[4,12]{1,0:T(4,128)} %source.7, bf16[3,256,512]{2,1,0:T(8,128)(2,1)} %refs_0_, bf16[2,3,256,512]{3,2,1,0:T(8,128)(2,1)} %refs_1_.1, bf16[2,3,256,512]{3,2,1,0:T(8,128)(2,1)} %refs_2_.1), custom_call_target="tpu_custom_call" | custom-call | bytes 5636288 | tf_op jit(solution)/shard_map/first/pallas_call | solution.py:274
  3.5 4.1 %collective-permute-start.1 = (bf16[3,128,512]{2,1,0:T(8,128)(2,1)}, bf16[3,128,512]{2,1,0:T(8,128)(2,1)S(1)}, u32[]{:S(2)}, u32[]{:S(2)}) collective-permute-start(bf16[3,128,512]{2,1,0:T(8,128)(2,1)} %get-tuple-element.30), channel_id=1, source_target_pairs={{0,8},{4,12},{8,0},{12,4},{1,9},{5,13},{9,1},{13,5},{2,10},{6,14},... | collective-permute-start | bytes 1179656 | tf_op jit(solution)/shard_map/ppermute | solution.py:260
  7.6 1.6 %collective-permute-start = (bf16[2,256,512]{2,1,0:T(8,128)(2,1)}, bf16[2,256,512]{2,1,0:T(8,128)(2,1)S(1)}, u32[]{:S(2)}, u32[]{:S(2)}) collective-permute-start(bf16[2,256,512]{2,1,0:T(8,128)(2,1)} %get-tuple-element.25), channel_id=1, source_target_pairs={{0,4},{4,0},{8,12},{12,8},{1,5},{5,1},{9,13},{13,9},{2,6},{6,2},{1... | collective-permute-start | bytes 1572872 | tf_op jit(solution)/shard_map/ppermute | solution.py:260
  9.1 0.0 copy-done
  9.1 0.0 collective-permute-start.3
  9.2 0.0 copy-start.1
  9.2 0.0 copy-start.2
  9.2 0.0 copy-start.3
  9.2 1.6 %collective-permute-start.10 = (bf16[3,256,512]{2,1,0:T(8,128)(2,1)}, bf16[3,256,512]{2,1,0:T(8,128)(2,1)S(1)}, u32[]{:S(2)}, u32[]{:S(2)}) collective-permute-start(bf16[3,256,512]{2,1,0:T(8,128)(2,1)} %get-tuple-element.26), channel_id=1, source_target_pairs={{0,2},{2,0},{1,3},{3,1},{4,6},{6,4},{5,7},{7,5},{8,10},{10,8},{9,1... | collective-permute-start | bytes 2359304 | tf_op jit(solution)/shard_map/ppermute | solution.py:252
  10.7 0.0 copy-done.4
  10.7 0.2 collective-permute-start.4
  10.9 2.0 %load.1 = (bf16[3,256,512]{2,1,0:T(8,128)(2,1)S(1)}, bf16[2,3,256,512]{3,2,1,0:T(8,128)(2,1)S(1)}, bf16[2,3,256,512]{3,2,1,0:T(8,128)(2,1)S(1)}) custom-call(bf16[3,256,512]{2,1,0:T(8,128)(2,1)S(1)} %copy-done, bf16[2,3,256,512]{3,2,1,0:T(8,128)(2,1)} %refs_1_.1, bf16[2,3,256,512]{3,2,1,0:T(8,128)(2,1)} %refs_2_.1), custom_call_target="tpu_custom_call" | custom-call | flops 30000001024 | bytes 7864320 | tf_op jit(solution)/shard_map/load/pallas_call | solution.py:274
  12.9 12.6 %collective-permute-done.1.mid = bf16[3,128,512]{2,1,0:T(8,128)(2,1)S(1)} collective-permute-done((bf16[3,128,512]{2,1,0:T(8,128)(2,1)}, bf16[3,128,512]{2,1,0:T(8,128)(2,1)S(1)}, u32[]{:S(2)}, u32[]{:S(2)}) %collective-permute-start.1) | collective-permute-done | bytes 393248 | tf_op jit(solution)/shard_map/ppermute | solution.py:260
  25.4 0.0 copy-done.1
  25.4 0.7 %pick.1 = bf16[2,128,512]{2,1,0:T(8,128)(2,1)S(1)} custom-call(s32[4,12]{1,0:T(4,128)S(1)} %copy-done.1, bf16[3,128,512]{2,1,0:T(8,128)(2,1)S(1)} %collective-permute-done.1.mid), custom_call_target="tpu_custom_call" | custom-call | bytes 655360 | tf_op jit(solution)/shard_map/pick/pallas_call | solution.py:274
  26.1 0.8 %collective-permute-start.8 = (bf16[3,128,512]{2,1,0:T(8,128)(2,1)S(1)}, bf16[3,128,512]{2,1,0:T(8,128)(2,1)S(1)}, u32[]{:S(2)}, u32[]{:S(2)}) collective-permute-start(bf16[3,128,512]{2,1,0:T(8,128)(2,1)S(1)} %collective-permute-done.1.mid), channel_id=1, source_target_pairs={{0,4},{4,0},{8,12},{12,8},{1,5},{5,1},{9,13},{13,9},{2,6},{6,2},{1... | collective-permute-start | bytes 1179656 | tf_op jit(solution)/shard_map/ppermute | solution.py:260
  26.9 0.0 collective-permute-done.3.own_far
  26.9 1.5 %collective-permute-start.2 = (bf16[2,128,512]{2,1,0:T(8,128)(2,1)S(1)}, bf16[2,128,512]{2,1,0:T(8,128)(2,1)S(1)}, u32[]{:S(2)}, u32[]{:S(2)}) collective-permute-start(bf16[2,128,512]{2,1,0:T(8,128)(2,1)S(1)} %pick.1), channel_id=1, source_target_pairs={{0,2},{2,0},{1,3},{3,1},{4,6},{6,4},{5,7},{7,5},{8,10},{10,8},{9,1... | collective-permute-start | bytes 786440 | tf_op jit(solution)/shard_map/ppermute | solution.py:252
  28.4 0.0 collective-permute-done.4.right_far
  28.4 0.0 collective-permute-start.6
  28.4 0.0 copy-done.2
  28.4 0.0 copy-done.3
  28.4 2.1 %own_slots.1.early = f32[3,256,512]{2,1,0:T(8,128)S(1)} custom-call(s32[4,12]{1,0:T(4,128)S(1)} %copy-done.1, s32[12]{0:T(128)S(1)} %copy-done.2, s32[12]{0:T(128)S(1)} %copy-done.3, bf16[3,256,512]{2,1,0:T(8,128)(2,1)S(1)} %get-tuple-element.28.own, bf16[3,256,512]{2,1,0:T(8,128)(2,1)S(1)} %collective-permute-done.3.own_far, ...), custom_call_target="tpu_custom_call" | custom-call | flops 30000001024 | bytes 7864320 | tf_op jit(solution)/shard_map/own_slots/pallas_call | solution.py:274
  30.6 4.4 %collective-permute-done.2.mid_x = bf16[2,128,512]{2,1,0:T(8,128)(2,1)S(1)} collective-permute-done((bf16[2,128,512]{2,1,0:T(8,128)(2,1)S(1)}, bf16[2,128,512]{2,1,0:T(8,128)(2,1)S(1)}, u32[]{:S(2)}, u32[]{:S(2)}) %collective-permute-start.2) | collective-permute-done | bytes 262176 | tf_op jit(solution)/shard_map/ppermute | solution.py:252
  35.0 0.0 collective-permute-start.7
  35.0 0.0 collective-permute-done.near
  35.0 0.0 collective-permute-done.10.env_x
  35.0 0.6 %collective-permute-start.11 = (bf16[2,256,512]{2,1,0:T(8,128)(2,1)S(1)}, bf16[2,256,512]{2,1,0:T(8,128)(2,1)S(1)}, u32[]{:S(2)}, u32[]{:S(2)}) collective-permute-start(bf16[2,256,512]{2,1,0:T(8,128)(2,1)S(1)} %slice.3), channel_id=1, source_target_pairs={{0,1},{1,0},{2,3},{3,2},{4,5},{5,4},{6,7},{7,6},{8,9},{9,8},{10,11... | collective-permute-start | bytes 1572872 | tf_op jit(solution)/shard_map/ppermute | solution.py:252
  35.6 0.1 collective-permute-start.5
  35.7 1.2 %collective-permute-done.8.far = bf16[3,128,512]{2,1,0:T(8,128)(2,1)S(1)} collective-permute-done((bf16[3,128,512]{2,1,0:T(8,128)(2,1)S(1)}, bf16[3,128,512]{2,1,0:T(8,128)(2,1)S(1)}, u32[]{:S(2)}, u32[]{:S(2)}) %collective-permute-start.8) | collective-permute-done | bytes 393248 | tf_op jit(solution)/shard_map/ppermute | solution.py:260
  36.9 0.0 collective-permute-done.6.mid_far
  36.9 0.0 collective-permute-done.7.mid_x_far
  36.9 0.0 collective-permute-start.9
  36.9 0.4 collective-permute-done.11.env_x_far
  37.2 0.7 %collective-permute-done.5.near_far = bf16[2,256,512]{2,1,0:T(8,128)(2,1)S(1)} collective-permute-done((bf16[2,256,512]{2,1,0:T(8,128)(2,1)S(1)}, bf16[2,256,512]{2,1,0:T(8,128)(2,1)S(1)}, u32[]{:S(2)}, u32[]{:S(2)}) %collective-permute-start.5) | collective-permute-done | bytes 524320 | tf_op jit(solution)/shard_map/ppermute | solution.py:252
  38.0 0.6 %collective-permute-done.9.far_far = bf16[3,128,512]{2,1,0:T(8,128)(2,1)S(1)} collective-permute-done((bf16[3,128,512]{2,1,0:T(8,128)(2,1)S(1)}, bf16[3,128,512]{2,1,0:T(8,128)(2,1)S(1)}, u32[]{:S(2)}, u32[]{:S(2)}) %collective-permute-start.9) | collective-permute-done | bytes 393248 | tf_op jit(solution)/shard_map/ppermute | solution.py:252
  38.6 2.4 %late_sent.1 = bf16[3,256,256]{2,1,0:T(8,128)(2,1)S(1)} custom-call(s32[4,12]{1,0:T(4,128)S(1)} %copy-done.1, s32[12]{0:T(128)S(1)} %copy-done.2, s32[12]{0:T(128)S(1)} %copy-done.3, bf16[2,256,512]{2,1,0:T(8,128)(2,1)S(1)} %collective-permute-done.near, bf16[2,256,512]{2,1,0:T(8,128)(2,1)S(1)} %collective-permute-done.5.near_far, ...), custom_call_target="tpu_custom_call" | custom-call | flops 805306368 | bytes 11141120 | tf_op jit(solution)/shard_map/late_sent/pallas_call | solution.py:274
  41.0 1.6 %collective-permute-start.12 = (bf16[3,256,256]{2,1,0:T(8,128)(2,1)S(1)}, bf16[3,256,256]{2,1,0:T(8,128)(2,1)S(1)}, u32[]{:S(2)}, u32[]{:S(2)}) collective-permute-start(bf16[3,256,256]{2,1,0:T(8,128)(2,1)S(1)} %late_sent.1), channel_id=1, source_target_pairs={{0,2},{2,0},{1,3},{3,1},{4,6},{6,4},{5,7},{7,5},{8,10},{10,8},{9,1... | collective-permute-start | bytes 1179656 | tf_op jit(solution)/shard_map/ppermute | solution.py:252
  42.6 2.4 %late_kept.1.keep = f32[3,256,256]{2,1,0:T(8,128)S(1)} custom-call(s32[4,12]{1,0:T(4,128)S(1)} %copy-done.1, s32[12]{0:T(128)S(1)} %copy-done.2, s32[12]{0:T(128)S(1)} %copy-done.3, bf16[2,256,512]{2,1,0:T(8,128)(2,1)S(1)} %collective-permute-done.near, bf16[2,256,512]{2,1,0:T(8,128)(2,1)S(1)} %collective-permute-done.5.near_far, ...), custom_call_target="tpu_custom_call" | custom-call | flops 805306368 | bytes 11534336 | tf_op jit(solution)/shard_map/late_kept/pallas_call | solution.py:274
  44.9 7.3 %collective-permute-done.12.received = bf16[3,256,256]{2,1,0:T(8,128)(2,1)S(1)} collective-permute-done((bf16[3,256,256]{2,1,0:T(8,128)(2,1)S(1)}, bf16[3,256,256]{2,1,0:T(8,128)(2,1)S(1)}, u32[]{:S(2)}, u32[]{:S(2)}) %collective-permute-start.12) | collective-permute-done | bytes 393248 | tf_op jit(solution)/shard_map/ppermute | solution.py:252
  52.3 1.4 %join.1 = bf16[3,256,256]{2,1,0:T(8,128)(2,1)} custom-call(s32[12]{0:T(128)S(1)} %copy-done.2, s32[12]{0:T(128)S(1)} %copy-done.3, f32[3,256,256]{2,1,0:T(8,128)S(1)} %late_kept.1.keep, bf16[3,256,256]{2,1,0:T(8,128)(2,1)S(1)} %collective-permute-done.12.received), custom_call_target="tpu_custom_call" | custom-call | bytes 1572864 | tf_op jit(solution)/shard_map/join/pallas_call | solution.py:274
  (1 shorter events, 0.0 us)
Async XLA Ops:
  0.0 10.7 %copy-start.4 = (bf16[2,3,256,512]{3,2,1,0:T(8,128)(2,1)S(1)}, bf16[2,3,256,512]{3,2,1,0:T(8,128)(2,1)}, u32[]{:S(2)}) copy-start(bf16[2,3,256,512]{3,2,1,0:T(8,128)(2,1)} %refs_2_.1) | copy-start | bytes 4718596
  0.0 9.1 %copy-start = (bf16[3,256,512]{2,1,0:T(8,128)(2,1)S(1)}, bf16[3,256,512]{2,1,0:T(8,128)(2,1)}, u32[]{:S(2)}) copy-start(bf16[3,256,512]{2,1,0:T(8,128)(2,1)} %refs_0_) | copy-start | bytes 2359300
  3.5 22.0 %collective-permute-start.1 = (bf16[3,128,512]{2,1,0:T(8,128)(2,1)}, bf16[3,128,512]{2,1,0:T(8,128)(2,1)S(1)}, u32[]{:S(2)}, u32[]{:S(2)}) collective-permute-start(bf16[3,128,512]{2,1,0:T(8,128)(2,1)} %get-tuple-element.30), channel_id=1, source_target_pairs={{0,8},{4,12},{8,0},{12,4},{1,9},{5,13},{9,1},{13,5},{2,10},{6,14},... | collective-permute-start | bytes 1179656 | tf_op jit(solution)/shard_map/ppermute | solution.py:260
  7.6 27.4 %collective-permute-start = (bf16[2,256,512]{2,1,0:T(8,128)(2,1)}, bf16[2,256,512]{2,1,0:T(8,128)(2,1)S(1)}, u32[]{:S(2)}, u32[]{:S(2)}) collective-permute-start(bf16[2,256,512]{2,1,0:T(8,128)(2,1)} %get-tuple-element.25), channel_id=1, source_target_pairs={{0,4},{4,0},{8,12},{12,8},{1,5},{5,1},{9,13},{13,9},{2,6},{6,2},{1... | collective-permute-start | bytes 1572872 | tf_op jit(solution)/shard_map/ppermute | solution.py:260
  9.1 17.8 %collective-permute-start.3 = (bf16[3,256,512]{2,1,0:T(8,128)(2,1)S(1)}, bf16[3,256,512]{2,1,0:T(8,128)(2,1)S(1)}, u32[]{:S(2)}, u32[]{:S(2)}) collective-permute-start(bf16[3,256,512]{2,1,0:T(8,128)(2,1)S(1)} %copy-done), channel_id=1, source_target_pairs={{0,1},{1,0},{2,3},{3,2},{4,5},{5,4},{6,7},{7,6},{8,9},{9,8},{10,11... | collective-permute-start | bytes 2359304 | tf_op jit(solution)/shard_map/ppermute | solution.py:252
  9.2 16.3 %copy-start.1 = (s32[4,12]{1,0:T(4,128)S(1)}, s32[4,12]{1,0:T(4,128)}, u32[]{:S(2)}) copy-start(s32[4,12]{1,0:T(4,128)} %source.7) | copy-start | bytes 580
  9.2 19.3 %copy-start.2 = (s32[12]{0:T(128)S(1)}, s32[12]{0:T(128)}, u32[]{:S(2)}) copy-start(s32[12]{0:T(128)} %left_dims.7) | copy-start | bytes 148
  9.2 19.3 %copy-start.3 = (s32[12]{0:T(128)S(1)}, s32[12]{0:T(128)}, u32[]{:S(2)}) copy-start(s32[12]{0:T(128)} %right_dims.7) | copy-start | bytes 148
  9.2 25.8 %collective-permute-start.10 = (bf16[3,256,512]{2,1,0:T(8,128)(2,1)}, bf16[3,256,512]{2,1,0:T(8,128)(2,1)S(1)}, u32[]{:S(2)}, u32[]{:S(2)}) collective-permute-start(bf16[3,256,512]{2,1,0:T(8,128)(2,1)} %get-tuple-element.26), channel_id=1, source_target_pairs={{0,2},{2,0},{1,3},{3,1},{4,6},{6,4},{5,7},{7,5},{8,10},{10,8},{9,1... | collective-permute-start | bytes 2359304 | tf_op jit(solution)/shard_map/ppermute | solution.py:252
  10.7 17.7 %collective-permute-start.4 = (bf16[2,3,256,512]{3,2,1,0:T(8,128)(2,1)S(1)}, bf16[2,3,256,512]{3,2,1,0:T(8,128)(2,1)S(1)}, u32[]{:S(2)}, u32[]{:S(2)}) collective-permute-start(bf16[2,3,256,512]{3,2,1,0:T(8,128)(2,1)S(1)} %copy-done.4), channel_id=1, source_target_pairs={{0,1},{1,0},{2,3},{3,2},{4,5},{5,4},{6,7},{7,6},{8,9},{9,8},{10,11... | collective-permute-start | bytes 4718600 | tf_op jit(solution)/shard_map/ppermute | solution.py:252
  26.1 10.8 %collective-permute-start.8 = (bf16[3,128,512]{2,1,0:T(8,128)(2,1)S(1)}, bf16[3,128,512]{2,1,0:T(8,128)(2,1)S(1)}, u32[]{:S(2)}, u32[]{:S(2)}) collective-permute-start(bf16[3,128,512]{2,1,0:T(8,128)(2,1)S(1)} %collective-permute-done.1.mid), channel_id=1, source_target_pairs={{0,4},{4,0},{8,12},{12,8},{1,5},{5,1},{9,13},{13,9},{2,6},{6,2},{1... | collective-permute-start | bytes 1179656 | tf_op jit(solution)/shard_map/ppermute | solution.py:260
  26.9 8.0 %collective-permute-start.2 = (bf16[2,128,512]{2,1,0:T(8,128)(2,1)S(1)}, bf16[2,128,512]{2,1,0:T(8,128)(2,1)S(1)}, u32[]{:S(2)}, u32[]{:S(2)}) collective-permute-start(bf16[2,128,512]{2,1,0:T(8,128)(2,1)S(1)} %pick.1), channel_id=1, source_target_pairs={{0,2},{2,0},{1,3},{3,1},{4,6},{6,4},{5,7},{7,5},{8,10},{10,8},{9,1... | collective-permute-start | bytes 786440 | tf_op jit(solution)/shard_map/ppermute | solution.py:252
  28.4 8.4 %collective-permute-start.6 = (bf16[3,128,512]{2,1,0:T(8,128)(2,1)S(1)}, bf16[3,128,512]{2,1,0:T(8,128)(2,1)S(1)}, u32[]{:S(2)}, u32[]{:S(2)}) collective-permute-start(bf16[3,128,512]{2,1,0:T(8,128)(2,1)S(1)} %collective-permute-done.1.mid), channel_id=1, source_target_pairs={{0,1},{1,0},{2,3},{3,2},{4,5},{5,4},{6,7},{7,6},{8,9},{9,8},{10,11... | collective-permute-start | bytes 1179656 | tf_op jit(solution)/shard_map/ppermute | solution.py:252
  35.0 1.9 %collective-permute-start.7 = (bf16[2,128,512]{2,1,0:T(8,128)(2,1)S(1)}, bf16[2,128,512]{2,1,0:T(8,128)(2,1)S(1)}, u32[]{:S(2)}, u32[]{:S(2)}) collective-permute-start(bf16[2,128,512]{2,1,0:T(8,128)(2,1)S(1)} %collective-permute-done.2.mid_x), channel_id=1, source_target_pairs={{0,1},{1,0},{2,3},{3,2},{4,5},{5,4},{6,7},{7,6},{8,9},{9,8},{10,11... | collective-permute-start | bytes 786440 | tf_op jit(solution)/shard_map/ppermute | solution.py:252
  35.0 2.2 %collective-permute-start.11 = (bf16[2,256,512]{2,1,0:T(8,128)(2,1)S(1)}, bf16[2,256,512]{2,1,0:T(8,128)(2,1)S(1)}, u32[]{:S(2)}, u32[]{:S(2)}) collective-permute-start(bf16[2,256,512]{2,1,0:T(8,128)(2,1)S(1)} %slice.3), channel_id=1, source_target_pairs={{0,1},{1,0},{2,3},{3,2},{4,5},{5,4},{6,7},{7,6},{8,9},{9,8},{10,11... | collective-permute-start | bytes 1572872 | tf_op jit(solution)/shard_map/ppermute | solution.py:252
  35.6 2.4 %collective-permute-start.5 = (bf16[2,256,512]{2,1,0:T(8,128)(2,1)S(1)}, bf16[2,256,512]{2,1,0:T(8,128)(2,1)S(1)}, u32[]{:S(2)}, u32[]{:S(2)}) collective-permute-start(bf16[2,256,512]{2,1,0:T(8,128)(2,1)S(1)} %collective-permute-done.near), channel_id=1, source_target_pairs={{0,1},{1,0},{2,3},{3,2},{4,5},{5,4},{6,7},{7,6},{8,9},{9,8},{10,11... | collective-permute-start | bytes 1572872 | tf_op jit(solution)/shard_map/ppermute | solution.py:252
  36.9 1.7 %collective-permute-start.9 = (bf16[3,128,512]{2,1,0:T(8,128)(2,1)S(1)}, bf16[3,128,512]{2,1,0:T(8,128)(2,1)S(1)}, u32[]{:S(2)}, u32[]{:S(2)}) collective-permute-start(bf16[3,128,512]{2,1,0:T(8,128)(2,1)S(1)} %collective-permute-done.8.far), channel_id=1, source_target_pairs={{0,1},{1,0},{2,3},{3,2},{4,5},{5,4},{6,7},{7,6},{8,9},{9,8},{10,11... | collective-permute-start | bytes 1179656 | tf_op jit(solution)/shard_map/ppermute | solution.py:252
  41.0 11.3 %collective-permute-start.12 = (bf16[3,256,256]{2,1,0:T(8,128)(2,1)S(1)}, bf16[3,256,256]{2,1,0:T(8,128)(2,1)S(1)}, u32[]{:S(2)}, u32[]{:S(2)}) collective-permute-start(bf16[3,256,256]{2,1,0:T(8,128)(2,1)S(1)} %late_sent.1), channel_id=1, source_target_pairs={{0,2},{2,0},{1,3},{3,1},{4,6},{6,4},{5,7},{7,5},{8,10},{10,8},{9,1... | collective-permute-start | bytes 1179656 | tf_op jit(solution)/shard_map/ppermute | solution.py:252

commit v8 on v7

--- a/solution.py
+++ b/solution.py
@@ -187,50 +187,88 @@
             acc[t] += jnp.dot(left[k, t], part, preferred_element_type=F32)
 
 
-def late_kernel(
-    kept, sizes, source, left_dims, right_dims, near, near_far, mid, mid_x, mid_far, mid_x_far, far, far_far,
-    left, right, right_far, env_x, env_x_far, early, out, total,
-):
-    pairs, secs, half_rows, blk = sizes
-    quarter = half_rows // 2
-    z, o, h = place()
-    mine = slots_of(sizes, source, z, o)
-    theirs = slots_of(sizes, source, z, 1 - o)
-    side = o if kept else 1 - o
+class Late:
+    def __init__(self, sizes, dims, side, left, right, right_far):
+        self.sizes, self.dims, self.side = sizes, dims, side
+        self.left, self.right, self.right_far = left, right, right_far
+        z, self.o, self.h = place()
+        self.mine = slots_of(sizes, dims[0], z, self.o)
+        self.theirs = slots_of(sizes, dims[0], z, 1 - self.o)
+        quarter = sizes[2] // 2
+        self.halves = [self.h * sizes[2], (1 - self.h) * sizes[2]]
+        self.ops = [self.o * quarter, (1 - self.o) * quarter]
+        self.parts = []
+
+    def target(self, n):
+        n = jnp.maximum(n, 0)
+        return n // self.sizes[1], n % self.sizes[1]
+
+    def sided(self, mine, far):
+        return jnp.where(self.side == self.h, mine, far)
+
+    def add(self, slot, pieces, firsts, r, lefts):
+        n, _, src = slot
+        at = lax.broadcasted_iota(jnp.int32, (pieces[0].shape[0], 1), 0)
+        row = jnp.concatenate([at + first for first in firsts], axis=0)
+        left_live = jnp.where(n >= 0, self.dims[1][src], 0)
+        live = live_columns(self.sizes, self.dims[2], src)
+        part = times_right(jnp.concatenate(pieces, axis=0), r * live, row, left_live)
+        self.parts.append((self.target(n)[1], jnp.concatenate(lefts, axis=1), part))
+
+    def add_own(self, slot, pieces, firsts):
+        k, t = self.target(slot[0])
+        size = pieces[0].shape[0]
+        lefts = [self.left[k, t, :, pl.ds(pl.multiple_of(first, size), size)] for first in firsts]
+        self.add(slot, pieces, firsts, self.sided(self.right[k, t], self.right_far[k, t]), lefts)
+
+    def add_near(self, near, near_far):
+        for j in range(2):
+            self.add_own(ranked(self.mine, 1, j), [near[j], near_far[j]], self.halves)
+
+    def add_mid(self, mid, mid_x, mid_far, mid_x_far):
+        for j in range(2):
+            slot = ranked(self.mine, 2, j)
+            pieces = [mid[slot[1]], mid_x[j], mid_far[slot[1]], mid_x_far[j]]
+            self.add_own(slot, pieces, [half + op for half in self.halves for op in self.ops])
+
+    def add_far(self, far, far_far, env_x, env_x_far):
+        half_rows = self.sizes[2]
+        quarter = half_rows // 2
+        firsts = [half + self.ops[0] for half in self.halves]
+        for j in range(2):
+            slot = ranked(self.mine, 3, j)
+            self.add_own(slot, [far[slot[1]], far_far[slot[1]]], firsts)
+            slot = ranked(self.theirs, 3, j)
+            lefts = [
+                env_x[2, :, pl.ds(pl.multiple_of(j * half_rows + half * quarter, quarter), quarter)]
+                for half in (self.h, 1 - self.h)
+            ]
+            r = self.sided(env_x[j], env_x_far[j])
+            self.add(slot, [far[slot[1]], far_far[slot[1]]], firsts, r, lefts)
+
+    def sum_into(self, total):
+        for t, left, part in self.parts:
+            total[t] += jnp.dot(left, part, preferred_element_type=F32)
+
+
+def begin_kernel(kept, sizes, source, left_dims, right_dims, *refs):
+    near, mid, envs, early, total = refs[:2], refs[2:6], refs[6:9], refs[9], refs[10]
+    o = place()[1]
+    side, half_rows = (o if kept else 1 - o), sizes[2]
     total[...] = early[:, :, pl.ds(pl.multiple_of(side * half_rows, half_rows), half_rows)]
-    parts = []
-
-    def add(slot, pieces, firsts, env=None):
-        n, _, src = slot
-        k, t = jnp.maximum(n, 0) // secs, jnp.maximum(n, 0) % secs
-        size = pieces[0].shape[0]
-        if env is None:
-            r = jnp.where(side == h, right[k, t], right_far[k, t])
-            lefts = [left[k, t, :, pl.ds(pl.multiple_of(first, size), size)] for first in firsts]
-        else:
-            r = jnp.where(side == h, env_x[env], env_x_far[env])
-            lefts = [
-                env_x[2, :, pl.ds(pl.multiple_of(env * half_rows + half * quarter, quarter), quarter)]
-                for half in (h, 1 - h)
-            ]
-        at = lax.broadcasted_iota(jnp.int32, (size, 1), 0)
-        row = jnp.concatenate([at + first for first in firsts], axis=0)
-        live = live_columns(sizes, right_dims, src)
-        left_live = jnp.where(n >= 0, left_dims[src], 0)
-        part = times_right(jnp.concatenate(pieces, axis=0), r * live, row, left_live)
-        parts.append((t, jnp.concatenate(lefts, axis=1), part))
-
-    halves = [h * half_rows, (1 - h) * half_rows]
-    ops = [o * quarter, (1 - o) * quarter]
-    for j in range(2):
-        add(ranked(mine, 1, j), [near[j], near_far[j]], halves)
-        slot = ranked(mine, 2, j)
-        pieces = [mid[slot[1]], mid_x[j], mid_far[slot[1]], mid_x_far[j]]
-        add(slot, pieces, [half + op for half in halves for op in ops])
-        for slot, env in ((ranked(mine, 3, j), None), (ranked(theirs, 3, j), j)):
-            add(slot, [far[slot[1]], far_far[slot[1]]], [half + ops[0] for half in halves], env)
-    for t, l, part in parts:
-        total[t] += jnp.dot(l, part, preferred_element_type=F32)
+    late = Late(sizes, (source, left_dims, right_dims), side, *envs)
+    late.add_near(*near)
+    late.add_mid(*mid)
+    late.sum_into(total)
+
+
+def finish_kernel(kept, sizes, source, left_dims, right_dims, *refs):
+    fars, envs, begun, out, total = refs[:4], refs[4:7], refs[7], refs[8], refs[9]
+    o = place()[1]
+    total[...] = begun[...]
+    late = Late(sizes, (source, left_dims, right_dims), o if kept else 1 - o, *envs)
+    late.add_far(*fars)
+    late.sum_into(total)
     out[...] = total[...].astype(out.dtype)
 
 
@@ -302,8 +340,8 @@
     mid = exchange(share, 2)
     near = exchange(near_out, 1)
     env_x = swap(env_out, "op")
-    own_far = swap(after(wavefunction, share), "half")
-    right_far = swap(after(right_env, share), "half")
+    own_far = swap(after(wavefunction, near_out), "half")
+    right_far = swap(after(right_env, env_out), "half")
     loaded = (after(wavefunction, env_out), left_env, right_env)
     own, left, right = call(
         load_kernel,
@@ -331,26 +369,31 @@
         [pltpu.VMEM((blk, blk), BF16)],
         flops=FILL,
     )
-    mid_far = swap(mid, "half")
+    mid_far = swap(after(mid, early), "half")
     mid_x, env_x = after(mid_x, early), after(env_x, early)
     mid_x_far = swap(mid_x, "half")
     env_x_far = swap(after(env_x[:2], early), "half")
     far = after(far, early, mid_x_far, mid_far)
     near = after(near, mid_x)
-    arrays = (
-        near, swap(near, "half"), mid, mid_x, mid_far, mid_x_far, far, swap(far, "half"),
-        *envs, env_x, env_x_far, early,
-    )
-    buffers = [pltpu.VMEM((secs, half_rows, half_rows), F32)]
-    flops = 2 * 3 * half_rows * blk * blk * 2
+    arrivals = (near, swap(near, "half"), mid, mid_x, mid_far, mid_x_far)
+    fars = (far, swap(far, "half"), env_x, env_x_far)
     columns = (secs, half_rows, half_rows)
-    (send,) = call(
-        functools.partial(late_kernel, False), "late_sent", [(columns, BF16)], dims, arrays, buffers, flops
-    )
-    received = swap(send, "op")
-    (keep,) = call(
-        functools.partial(late_kernel, True), "late_kept", [(columns, F32)], dims, arrays, buffers, flops
-    )
+
+    def side(kept, dtype, fill):
+        (begun,) = call(
+            functools.partial(begin_kernel, kept), "begin", [(columns, F32)], dims, (*arrivals, *envs, early), flops=fill
+        )
+        return call(
+            functools.partial(finish_kernel, kept),
+            "finish",
+            [(columns, dtype)],
+            dims,
+            (*fars, *envs, begun),
+            [pltpu.VMEM(columns, F32)],
+        )[0]
+
+    received = swap(side(False, BF16, 0), "op")
+    keep = side(True, F32, 0)
     (out,) = call(
         join_kernel,
         "join",

time: 53.8 us -> 53.3 us (level)
  waiting for transfers between devices: 27.2 us -> 24.9 us
  Pallas kernels: 14.3 us -> 16.1 us
    ppermute x10, waiting for transfers between devices: 13.5 us -> 11.1 us  [swap(): return lax.ppermute(x, axis, [(0, 1), (1, 0)])]
    pallas_call x7 -> x9, Pallas kernels: 14.3 us -> 16.1 us  [call(): pl.pallas_call(functools.partial(kernel, sizes), out_shape=shapes, in_spe...]
  transfers between devices with their start and end apart: 13 -> 13, of which waited for: 7 -> 5; matrix products, arithmetic and copies ran while one was open for 0% -> 0% of each run, Pallas kernels for 13% -> 18%
where the time goes in v8:
time: 53.3 us; the launch traced here: 53.2 us
  waiting for transfers between devices  24.9 us (47%)
  Pallas kernels  16.1 us (30%)
  starting transfers between devices  12 us (23%)
    pallas_call x9, Pallas kernels, call(): pl.pallas_call(functools.partial(kernel, sizes), out_shape=shapes, in_spe...  16.1 us
    ppermute x3, waiting for transfers between devices, exchange(): return lax.ppermute(x, 'sector', [(i, i ^ kind) for i in range(4)])  13.8 us
    ppermute x10, waiting for transfers between devices, swap(): return lax.ppermute(x, axis, [(0, 1), (1, 0)])  11.1 us
    ppermute x3, starting transfers between devices, exchange(): return lax.ppermute(x, 'sector', [(i, i ^ kind) for i in range(4)])  6.51 us
    ppermute x10, starting transfers between devices, swap(): return lax.ppermute(x, axis, [(0, 1), (1, 0)])  5.48 us
  transfers between devices with their start and end apart: 13, of which 5 were waited for; matrix products, arithmetic and copies ran while one was open for 0% of the time, Pallas kernels for 18%

profile of v8, /device:TPU:0, one launch (start us, length us, event | category | flops | bytes accessed | tf_op | source)
XLA Modules:
  0.0 53.2 jit_solution(7366524905145725304)
XLA Ops:
  0.0 0.0 copy-start
  0.0 0.0 copy-start.4
  0.0 3.5 %first.1 = (bf16[3,128,512]{2,1,0:T(8,128)(2,1)}, bf16[2,256,512]{2,1,0:T(8,128)(2,1)}, bf16[3,256,512]{2,1,0:T(8,128)(2,1)}) custom-call(s32[4,12]{1,0:T(4,128)} %source.11, bf16[3,256,512]{2,1,0:T(8,128)(2,1)} %refs_0_, bf16[2,3,256,512]{3,2,1,0:T(8,128)(2,1)} %refs_1_.1, bf16[2,3,256,512]{3,2,1,0:T(8,128)(2,1)} %refs_2_.1), custom_call_target="tpu_custom_call" | custom-call | bytes 5636288 | tf_op jit(solution)/shard_map/first/pallas_call | solution.py:312
  3.5 4.1 %collective-permute-start = (bf16[3,128,512]{2,1,0:T(8,128)(2,1)}, bf16[3,128,512]{2,1,0:T(8,128)(2,1)S(1)}, u32[]{:S(2)}, u32[]{:S(2)}) collective-permute-start(bf16[3,128,512]{2,1,0:T(8,128)(2,1)} %get-tuple-element.26), channel_id=1, source_target_pairs={{0,8},{4,12},{8,0},{12,4},{1,9},{5,13},{9,1},{13,5},{2,10},{6,14},... | collective-permute-start | bytes 1179656 | tf_op jit(solution)/shard_map/ppermute | solution.py:298
  7.6 1.6 %collective-permute-start.10 = (bf16[2,256,512]{2,1,0:T(8,128)(2,1)}, bf16[2,256,512]{2,1,0:T(8,128)(2,1)S(1)}, u32[]{:S(2)}, u32[]{:S(2)}) collective-permute-start(bf16[2,256,512]{2,1,0:T(8,128)(2,1)} %get-tuple-element.31), channel_id=1, source_target_pairs={{0,4},{4,0},{8,12},{12,8},{1,5},{5,1},{9,13},{13,9},{2,6},{6,2},{1... | collective-permute-start | bytes 1572872 | tf_op jit(solution)/shard_map/ppermute | solution.py:298
  9.2 0.0 copy-done
  9.2 0.0 collective-permute-start.2
  9.2 0.0 copy-start.1
  9.2 0.0 copy-start.2
  9.2 0.0 copy-start.3
  9.2 1.6 %collective-permute-start.8 = (bf16[3,256,512]{2,1,0:T(8,128)(2,1)}, bf16[3,256,512]{2,1,0:T(8,128)(2,1)S(1)}, u32[]{:S(2)}, u32[]{:S(2)}) collective-permute-start(bf16[3,256,512]{2,1,0:T(8,128)(2,1)} %get-tuple-element.27), channel_id=1, source_target_pairs={{0,2},{2,0},{1,3},{3,1},{4,6},{6,4},{5,7},{7,5},{8,10},{10,8},{9,1... | collective-permute-start | bytes 2359304 | tf_op jit(solution)/shard_map/ppermute | solution.py:290
  10.7 0.0 copy-done.4
  10.7 0.2 collective-permute-start.3
  10.9 2.0 %load.1 = (bf16[3,256,512]{2,1,0:T(8,128)(2,1)S(1)}, bf16[2,3,256,512]{3,2,1,0:T(8,128)(2,1)S(1)}, bf16[2,3,256,512]{3,2,1,0:T(8,128)(2,1)S(1)}) custom-call(bf16[3,256,512]{2,1,0:T(8,128)(2,1)S(1)} %copy-done, bf16[2,3,256,512]{3,2,1,0:T(8,128)(2,1)} %refs_1_.1, bf16[2,3,256,512]{3,2,1,0:T(8,128)(2,1)} %refs_2_.1), custom_call_target="tpu_custom_call" | custom-call | flops 30000001024 | bytes 7864320 | tf_op jit(solution)/shard_map/load/pallas_call | solution.py:312
  12.9 12.6 %collective-permute-done.mid.refs_2_ = bf16[3,128,512]{2,1,0:T(8,128)(2,1)S(1)} collective-permute-done((bf16[3,128,512]{2,1,0:T(8,128)(2,1)}, bf16[3,128,512]{2,1,0:T(8,128)(2,1)S(1)}, u32[]{:S(2)}, u32[]{:S(2)}) %collective-permute-start) | collective-permute-done | bytes 393248 | tf_op jit(solution)/shard_map/ppermute | solution.py:298
  25.4 0.0 copy-done.1
  25.4 0.7 %pick.1 = bf16[2,128,512]{2,1,0:T(8,128)(2,1)S(1)} custom-call(s32[4,12]{1,0:T(4,128)S(1)} %copy-done.1, bf16[3,128,512]{2,1,0:T(8,128)(2,1)S(1)} %collective-permute-done.mid.refs_2_), custom_call_target="tpu_custom_call" | custom-call | bytes 655360 | tf_op jit(solution)/shard_map/pick/pallas_call | solution.py:312
  26.1 0.8 %collective-permute-start.1 = (bf16[3,128,512]{2,1,0:T(8,128)(2,1)S(1)}, bf16[3,128,512]{2,1,0:T(8,128)(2,1)S(1)}, u32[]{:S(2)}, u32[]{:S(2)}) collective-permute-start(bf16[3,128,512]{2,1,0:T(8,128)(2,1)S(1)} %collective-permute-done.mid.refs_2_), channel_id=1, source_target_pairs={{0,4},{4,0},{8,12},{12,8},{1,5},{5,1},{9,13},{13,9},{2,6},{6,2},{1... | collective-permute-start | bytes 1179656 | tf_op jit(solution)/shard_map/ppermute | solution.py:298
  26.9 0.0 collective-permute-done.2.own_far
  26.9 1.5 %collective-permute-start.4 = (bf16[2,128,512]{2,1,0:T(8,128)(2,1)S(1)}, bf16[2,128,512]{2,1,0:T(8,128)(2,1)S(1)}, u32[]{:S(2)}, u32[]{:S(2)}) collective-permute-start(bf16[2,128,512]{2,1,0:T(8,128)(2,1)S(1)} %pick.1), channel_id=1, source_target_pairs={{0,2},{2,0},{1,3},{3,1},{4,6},{6,4},{5,7},{7,5},{8,10},{10,8},{9,1... | collective-permute-start | bytes 786440 | tf_op jit(solution)/shard_map/ppermute | solution.py:290
  28.4 0.0 collective-permute-done.3.right_far.refs_8_.refs_6_
  28.4 0.0 copy-done.2
  28.4 0.0 copy-done.3
  28.4 2.1 %own_slots.1.refs_9_ = f32[3,256,512]{2,1,0:T(8,128)S(1)} custom-call(s32[4,12]{1,0:T(4,128)S(1)} %copy-done.1, s32[12]{0:T(128)S(1)} %copy-done.2, s32[12]{0:T(128)S(1)} %copy-done.3, bf16[3,256,512]{2,1,0:T(8,128)(2,1)S(1)} %get-tuple-element.29.own, bf16[3,256,512]{2,1,0:T(8,128)(2,1)S(1)} %collective-permute-done.2.own_far, ...), custom_call_target="tpu_custom_call" | custom-call | flops 30000001024 | bytes 7864320 | tf_op jit(solution)/shard_map/own_slots/pallas_call | solution.py:312
  30.6 0.1 collective-permute-start.6
  30.6 4.3 %collective-permute-done.4.refs_3_ = bf16[2,128,512]{2,1,0:T(8,128)(2,1)S(1)} collective-permute-done((bf16[2,128,512]{2,1,0:T(8,128)(2,1)S(1)}, bf16[2,128,512]{2,1,0:T(8,128)(2,1)S(1)}, u32[]{:S(2)}, u32[]{:S(2)}) %collective-permute-start.4) | collective-permute-done | bytes 262176 | tf_op jit(solution)/shard_map/ppermute | solution.py:290
  35.0 0.0 collective-permute-start.5
  35.0 0.0 collective-permute-done.10.refs_0_
  35.0 0.0 collective-permute-done.8.refs_2_
  35.0 0.5 collective-permute-start.11
  35.5 0.1 collective-permute-start.9
  35.7 1.2 %collective-permute-done.1.refs_0_ = bf16[3,128,512]{2,1,0:T(8,128)(2,1)S(1)} collective-permute-done((bf16[3,128,512]{2,1,0:T(8,128)(2,1)S(1)}, bf16[3,128,512]{2,1,0:T(8,128)(2,1)S(1)}, u32[]{:S(2)}, u32[]{:S(2)}) %collective-permute-start.1) | collective-permute-done | bytes 393248 | tf_op jit(solution)/shard_map/ppermute | solution.py:298
  36.9 0.0 collective-permute-done.5.refs_5_
  36.9 0.0 collective-permute-done.6.refs_4_
  36.9 0.0 collective-permute-start.7
  36.9 0.4 collective-permute-done.11.refs_1_
  37.3 1.8 %begin.3.refs_7_ = f32[3,256,256]{2,1,0:T(8,128)S(1)} custom-call(s32[4,12]{1,0:T(4,128)S(1)} %copy-done.1, s32[12]{0:T(128)S(1)} %copy-done.2, s32[12]{0:T(128)S(1)} %copy-done.3, bf16[2,256,512]{2,1,0:T(8,128)(2,1)S(1)} %collective-permute-done.10.refs_0_, bf16[2,256,512]{2,1,0:T(8,128)(2,1)S(1)} %collective-permute-done.11.refs_1_, ...), custom_call_target="tpu_custom_call" | custom-call | bytes 9437184 | tf_op jit(solution)/shard_map/begin/pallas_call | solution.py:312
  39.0 0.0 collective-permute-done.9.refs_3_
  39.0 0.0 collective-permute-done.7.refs_1_
  39.0 1.5 %finish.3 = bf16[3,256,256]{2,1,0:T(8,128)(2,1)S(1)} custom-call(s32[4,12]{1,0:T(4,128)S(1)} %copy-done.1, s32[12]{0:T(128)S(1)} %copy-done.2, s32[12]{0:T(128)S(1)} %copy-done.3, bf16[3,128,512]{2,1,0:T(8,128)(2,1)S(1)} %collective-permute-done.1.refs_0_, bf16[3,128,512]{2,1,0:T(8,128)(2,1)S(1)} %collective-permute-done.7.refs_1_, ...), custom_call_target="tpu_custom_call" | custom-call | bytes 7995392 | tf_op jit(solution)/shard_map/finish/pallas_call | solution.py:312
  40.5 1.6 %collective-permute-start.12 = (bf16[3,256,256]{2,1,0:T(8,128)(2,1)S(1)}, bf16[3,256,256]{2,1,0:T(8,128)(2,1)S(1)}, u32[]{:S(2)}, u32[]{:S(2)}) collective-permute-start(bf16[3,256,256]{2,1,0:T(8,128)(2,1)S(1)} %finish.3), channel_id=1, source_target_pairs={{0,2},{2,0},{1,3},{3,1},{4,6},{6,4},{5,7},{7,5},{8,10},{10,8},{9,1... | collective-permute-start | bytes 1179656 | tf_op jit(solution)/shard_map/ppermute | solution.py:290
  42.1 1.8 %begin.2.refs_7_ = f32[3,256,256]{2,1,0:T(8,128)S(1)} custom-call(s32[4,12]{1,0:T(4,128)S(1)} %copy-done.1, s32[12]{0:T(128)S(1)} %copy-done.2, s32[12]{0:T(128)S(1)} %copy-done.3, bf16[2,256,512]{2,1,0:T(8,128)(2,1)S(1)} %collective-permute-done.10.refs_0_, bf16[2,256,512]{2,1,0:T(8,128)(2,1)S(1)} %collective-permute-done.11.refs_1_, ...), custom_call_target="tpu_custom_call" | custom-call | bytes 9437184 | tf_op jit(solution)/shard_map/begin/pallas_call | solution.py:312
  43.9 1.5 %finish.2.keep = f32[3,256,256]{2,1,0:T(8,128)S(1)} custom-call(s32[4,12]{1,0:T(4,128)S(1)} %copy-done.1, s32[12]{0:T(128)S(1)} %copy-done.2, s32[12]{0:T(128)S(1)} %copy-done.3, bf16[3,128,512]{2,1,0:T(8,128)(2,1)S(1)} %collective-permute-done.1.refs_0_, bf16[3,128,512]{2,1,0:T(8,128)(2,1)S(1)} %collective-permute-done.7.refs_1_, ...), custom_call_target="tpu_custom_call" | custom-call | bytes 8388608 | tf_op jit(solution)/shard_map/finish/pallas_call | solution.py:312
  45.4 6.4 %collective-permute-done.12.received = bf16[3,256,256]{2,1,0:T(8,128)(2,1)S(1)} collective-permute-done((bf16[3,256,256]{2,1,0:T(8,128)(2,1)S(1)}, bf16[3,256,256]{2,1,0:T(8,128)(2,1)S(1)}, u32[]{:S(2)}, u32[]{:S(2)}) %collective-permute-start.12) | collective-permute-done | bytes 393248 | tf_op jit(solution)/shard_map/ppermute | solution.py:290
  51.8 1.4 %join.1 = bf16[3,256,256]{2,1,0:T(8,128)(2,1)} custom-call(s32[12]{0:T(128)S(1)} %copy-done.2, s32[12]{0:T(128)S(1)} %copy-done.3, f32[3,256,256]{2,1,0:T(8,128)S(1)} %finish.2.keep, bf16[3,256,256]{2,1,0:T(8,128)(2,1)S(1)} %collective-permute-done.12.received), custom_call_target="tpu_custom_call" | custom-call | bytes 1572864 | tf_op jit(solution)/shard_map/join/pallas_call | solution.py:312
  (1 shorter events, 0.0 us)
Async XLA Ops:
  0.0 9.2 %copy-start = (bf16[3,256,512]{2,1,0:T(8,128)(2,1)S(1)}, bf16[3,256,512]{2,1,0:T(8,128)(2,1)}, u32[]{:S(2)}) copy-start(bf16[3,256,512]{2,1,0:T(8,128)(2,1)} %refs_0_) | copy-start | bytes 2359300
  0.0 10.7 %copy-start.4 = (bf16[2,3,256,512]{3,2,1,0:T(8,128)(2,1)S(1)}, bf16[2,3,256,512]{3,2,1,0:T(8,128)(2,1)}, u32[]{:S(2)}) copy-start(bf16[2,3,256,512]{3,2,1,0:T(8,128)(2,1)} %refs_2_.1) | copy-start | bytes 4718596
  3.5 22.0 %collective-permute-start = (bf16[3,128,512]{2,1,0:T(8,128)(2,1)}, bf16[3,128,512]{2,1,0:T(8,128)(2,1)S(1)}, u32[]{:S(2)}, u32[]{:S(2)}) collective-permute-start(bf16[3,128,512]{2,1,0:T(8,128)(2,1)} %get-tuple-element.26), channel_id=1, source_target_pairs={{0,8},{4,12},{8,0},{12,4},{1,9},{5,13},{9,1},{13,5},{2,10},{6,14},... | collective-permute-start | bytes 1179656 | tf_op jit(solution)/shard_map/ppermute | solution.py:298
  7.6 27.4 %collective-permute-start.10 = (bf16[2,256,512]{2,1,0:T(8,128)(2,1)}, bf16[2,256,512]{2,1,0:T(8,128)(2,1)S(1)}, u32[]{:S(2)}, u32[]{:S(2)}) collective-permute-start(bf16[2,256,512]{2,1,0:T(8,128)(2,1)} %get-tuple-element.31), channel_id=1, source_target_pairs={{0,4},{4,0},{8,12},{12,8},{1,5},{5,1},{9,13},{13,9},{2,6},{6,2},{1... | collective-permute-start | bytes 1572872 | tf_op jit(solution)/shard_map/ppermute | solution.py:298
  9.2 17.8 %collective-permute-start.2 = (bf16[3,256,512]{2,1,0:T(8,128)(2,1)S(1)}, bf16[3,256,512]{2,1,0:T(8,128)(2,1)S(1)}, u32[]{:S(2)}, u32[]{:S(2)}) collective-permute-start(bf16[3,256,512]{2,1,0:T(8,128)(2,1)S(1)} %copy-done), channel_id=1, source_target_pairs={{0,1},{1,0},{2,3},{3,2},{4,5},{5,4},{6,7},{7,6},{8,9},{9,8},{10,11... | collective-permute-start | bytes 2359304 | tf_op jit(solution)/shard_map/ppermute | solution.py:290
  9.2 16.3 %copy-start.1 = (s32[4,12]{1,0:T(4,128)S(1)}, s32[4,12]{1,0:T(4,128)}, u32[]{:S(2)}) copy-start(s32[4,12]{1,0:T(4,128)} %source.11) | copy-start | bytes 580
  9.2 19.3 %copy-start.2 = (s32[12]{0:T(128)S(1)}, s32[12]{0:T(128)}, u32[]{:S(2)}) copy-start(s32[12]{0:T(128)} %left_dims.11) | copy-start | bytes 148
  9.2 19.3 %copy-start.3 = (s32[12]{0:T(128)S(1)}, s32[12]{0:T(128)}, u32[]{:S(2)}) copy-start(s32[12]{0:T(128)} %right_dims.11) | copy-start | bytes 148
  9.2 25.8 %collective-permute-start.8 = (bf16[3,256,512]{2,1,0:T(8,128)(2,1)}, bf16[3,256,512]{2,1,0:T(8,128)(2,1)S(1)}, u32[]{:S(2)}, u32[]{:S(2)}) collective-permute-start(bf16[3,256,512]{2,1,0:T(8,128)(2,1)} %get-tuple-element.27), channel_id=1, source_target_pairs={{0,2},{2,0},{1,3},{3,1},{4,6},{6,4},{5,7},{7,5},{8,10},{10,8},{9,1... | collective-permute-start | bytes 2359304 | tf_op jit(solution)/shard_map/ppermute | solution.py:290
  10.7 17.7 %collective-permute-start.3 = (bf16[2,3,256,512]{3,2,1,0:T(8,128)(2,1)S(1)}, bf16[2,3,256,512]{3,2,1,0:T(8,128)(2,1)S(1)}, u32[]{:S(2)}, u32[]{:S(2)}) collective-permute-start(bf16[2,3,256,512]{3,2,1,0:T(8,128)(2,1)S(1)} %copy-done.4), channel_id=1, source_target_pairs={{0,1},{1,0},{2,3},{3,2},{4,5},{5,4},{6,7},{7,6},{8,9},{9,8},{10,11... | collective-permute-start | bytes 4718600 | tf_op jit(solution)/shard_map/ppermute | solution.py:290
  26.1 10.8 %collective-permute-start.1 = (bf16[3,128,512]{2,1,0:T(8,128)(2,1)S(1)}, bf16[3,128,512]{2,1,0:T(8,128)(2,1)S(1)}, u32[]{:S(2)}, u32[]{:S(2)}) collective-permute-start(bf16[3,128,512]{2,1,0:T(8,128)(2,1)S(1)} %collective-permute-done.mid.refs_2_), channel_id=1, source_target_pairs={{0,4},{4,0},{8,12},{12,8},{1,5},{5,1},{9,13},{13,9},{2,6},{6,2},{1... | collective-permute-start | bytes 1179656 | tf_op jit(solution)/shard_map/ppermute | solution.py:298
  26.9 8.0 %collective-permute-start.4 = (bf16[2,128,512]{2,1,0:T(8,128)(2,1)S(1)}, bf16[2,128,512]{2,1,0:T(8,128)(2,1)S(1)}, u32[]{:S(2)}, u32[]{:S(2)}) collective-permute-start(bf16[2,128,512]{2,1,0:T(8,128)(2,1)S(1)} %pick.1), channel_id=1, source_target_pairs={{0,2},{2,0},{1,3},{3,1},{4,6},{6,4},{5,7},{7,5},{8,10},{10,8},{9,1... | collective-permute-start | bytes 786440 | tf_op jit(solution)/shard_map/ppermute | solution.py:290
  30.6 6.3 %collective-permute-start.6 = (bf16[3,128,512]{2,1,0:T(8,128)(2,1)S(1)}, bf16[3,128,512]{2,1,0:T(8,128)(2,1)S(1)}, u32[]{:S(2)}, u32[]{:S(2)}) collective-permute-start(bf16[3,128,512]{2,1,0:T(8,128)(2,1)S(1)} %collective-permute-done.mid.refs_2_), channel_id=1, source_target_pairs={{0,1},{1,0},{2,3},{3,2},{4,5},{5,4},{6,7},{7,6},{8,9},{9,8},{10,11... | collective-permute-start | bytes 1179656 | tf_op jit(solution)/shard_map/ppermute | solution.py:290
  35.0 1.9 %collective-permute-start.5 = (bf16[2,128,512]{2,1,0:T(8,128)(2,1)S(1)}, bf16[2,128,512]{2,1,0:T(8,128)(2,1)S(1)}, u32[]{:S(2)}, u32[]{:S(2)}) collective-permute-start(bf16[2,128,512]{2,1,0:T(8,128)(2,1)S(1)} %collective-permute-done.4.refs_3_), channel_id=1, source_target_pairs={{0,1},{1,0},{2,3},{3,2},{4,5},{5,4},{6,7},{7,6},{8,9},{9,8},{10,11... | collective-permute-start | bytes 786440 | tf_op jit(solution)/shard_map/ppermute | solution.py:290
  35.0 2.3 %collective-permute-start.11 = (bf16[2,256,512]{2,1,0:T(8,128)(2,1)S(1)}, bf16[2,256,512]{2,1,0:T(8,128)(2,1)S(1)}, u32[]{:S(2)}, u32[]{:S(2)}) collective-permute-start(bf16[2,256,512]{2,1,0:T(8,128)(2,1)S(1)} %collective-permute-done.10.refs_0_), channel_id=1, source_target_pairs={{0,1},{1,0},{2,3},{3,2},{4,5},{5,4},{6,7},{7,6},{8,9},{9,8},{10,11... | collective-permute-start | bytes 1572872 | tf_op jit(solution)/shard_map/ppermute | solution.py:290
  35.5 3.5 %collective-permute-start.9 = (bf16[2,256,512]{2,1,0:T(8,128)(2,1)S(1)}, bf16[2,256,512]{2,1,0:T(8,128)(2,1)S(1)}, u32[]{:S(2)}, u32[]{:S(2)}) collective-permute-start(bf16[2,256,512]{2,1,0:T(8,128)(2,1)S(1)} %slice.3), channel_id=1, source_target_pairs={{0,1},{1,0},{2,3},{3,2},{4,5},{5,4},{6,7},{7,6},{8,9},{9,8},{10,11... | collective-permute-start | bytes 1572872 | tf_op jit(solution)/shard_map/ppermute | solution.py:290
  36.9 2.2 %collective-permute-start.7 = (bf16[3,128,512]{2,1,0:T(8,128)(2,1)S(1)}, bf16[3,128,512]{2,1,0:T(8,128)(2,1)S(1)}, u32[]{:S(2)}, u32[]{:S(2)}) collective-permute-start(bf16[3,128,512]{2,1,0:T(8,128)(2,1)S(1)} %collective-permute-done.1.refs_0_), channel_id=1, source_target_pairs={{0,1},{1,0},{2,3},{3,2},{4,5},{5,4},{6,7},{7,6},{8,9},{9,8},{10,11... | collective-permute-start | bytes 1179656 | tf_op jit(solution)/shard_map/ppermute | solution.py:290
  40.5 11.2 %collective-permute-start.12 = (bf16[3,256,256]{2,1,0:T(8,128)(2,1)S(1)}, bf16[3,256,256]{2,1,0:T(8,128)(2,1)S(1)}, u32[]{:S(2)}, u32[]{:S(2)}) collective-permute-start(bf16[3,256,256]{2,1,0:T(8,128)(2,1)S(1)} %finish.3), channel_id=1, source_target_pairs={{0,2},{2,0},{1,3},{3,1},{4,6},{6,4},{5,7},{7,5},{8,10},{10,8},{9,1... | collective-permute-start | bytes 1179656 | tf_op jit(solution)/shard_map/ppermute | solution.py:290

commit v9 on v8

--- a/solution.py
+++ b/solution.py
@@ -263,13 +263,13 @@
 
 
 def finish_kernel(kept, sizes, source, left_dims, right_dims, *refs):
-    fars, envs, begun, out, total = refs[:4], refs[4:7], refs[7], refs[8], refs[9]
+    fars, envs, total = refs[:4], refs[4:7], refs[8]
     o = place()[1]
-    total[...] = begun[...]
     late = Late(sizes, (source, left_dims, right_dims), o if kept else 1 - o, *envs)
     late.add_far(*fars)
     late.sum_into(total)
-    out[...] = total[...].astype(out.dtype)
+    if not kept:
+        refs[9][...] = total[...].astype(BF16)
 
 
 def join_kernel(sizes, left_dims, right_dims, keep, received, out, held, sem):
@@ -305,7 +305,8 @@
     sizes = (pairs, secs, half_rows, blk)
 
     def call(
-        kernel, name, outs, scalars, arrays, scratch=(), flops=0, space=pltpu.VMEM, limit=VMEM_LIMIT, to=pltpu.VMEM
+        kernel, name, outs, scalars, arrays, scratch=(), flops=0, space=pltpu.VMEM, limit=VMEM_LIMIT, to=pltpu.VMEM,
+        aliases=None,
     ):
         shapes = [jax.ShapeDtypeStruct(shape, dtype) for shape, dtype in outs]
         nbytes = sum(s.size * s.dtype.itemsize for s in [*shapes, *arrays])
@@ -319,6 +320,7 @@
             compiler_params=pltpu.CompilerParams(vmem_limit_bytes=limit),
             cost_estimate=pl.CostEstimate(flops=flops, bytes_accessed=nbytes, transcendentals=0),
             name=name,
+            input_output_aliases=aliases or {},
         )(*scalars, *arrays)
 
     dims = (source, left_dims, right_dims)
@@ -383,14 +385,15 @@
         (begun,) = call(
             functools.partial(begin_kernel, kept), "begin", [(columns, F32)], dims, (*arrivals, *envs, early), flops=fill
         )
+        arrays = (*fars, *envs, begun)
         return call(
             functools.partial(finish_kernel, kept),
             "finish",
-            [(columns, dtype)],
+            [(columns, F32)] if kept else [(columns, F32), (columns, dtype)],
             dims,
-            (*fars, *envs, begun),
-            [pltpu.VMEM(columns, F32)],
-        )[0]
+            arrays,
+            aliases={len(dims) + len(arrays) - 1: 0},
+        )[-1]
 
     received = swap(side(False, BF16, 0), "op")
     keep = side(True, F32, 0)

time: 53.3 us -> 53.3 us (level)
  no operation moved by 1% of the time
where the time goes in v9:
time: 53.3 us; the launch traced here: 53.2 us
  waiting for transfers between devices  25.1 us (47%)
  Pallas kernels  15.9 us (30%)
  starting transfers between devices  12 us (23%)
    pallas_call x9, Pallas kernels, call(): pl.pallas_call(functools.partial(kernel, sizes), out_shape=shapes, in_spe...  15.9 us
    ppermute x3, waiting for transfers between devices, exchange(): return lax.ppermute(x, 'sector', [(i, i ^ kind) for i in range(4)])  13.8 us
    ppermute x10, waiting for transfers between devices, swap(): return lax.ppermute(x, axis, [(0, 1), (1, 0)])  11.3 us
    ppermute x3, starting transfers between devices, exchange(): return lax.ppermute(x, 'sector', [(i, i ^ kind) for i in range(4)])  6.51 us
    ppermute x10, starting transfers between devices, swap(): return lax.ppermute(x, axis, [(0, 1), (1, 0)])  5.49 us
  transfers between devices with their start and end apart: 13, of which 5 were waited for; matrix products, arithmetic and copies ran while one was open for 0% of the time, Pallas kernels for 18%

profile of v9, /device:TPU:0, one launch (start us, length us, event | category | flops | bytes accessed | tf_op | source)
XLA Modules:
  0.0 53.2 jit_solution(3068669060675640634)
XLA Ops:
  0.0 0.0 copy-start.4
  0.0 0.0 copy-start
  0.0 3.5 %first.1 = (bf16[3,128,512]{2,1,0:T(8,128)(2,1)}, bf16[2,256,512]{2,1,0:T(8,128)(2,1)}, bf16[3,256,512]{2,1,0:T(8,128)(2,1)}) custom-call(s32[4,12]{1,0:T(4,128)} %source.11, bf16[3,256,512]{2,1,0:T(8,128)(2,1)} %refs_0_, bf16[2,3,256,512]{3,2,1,0:T(8,128)(2,1)} %refs_1_.1, bf16[2,3,256,512]{3,2,1,0:T(8,128)(2,1)} %refs_2_.1), custom_call_target="tpu_custom_call" | custom-call | bytes 5636288 | tf_op jit(solution)/shard_map/first/pallas_call | solution.py:313
  3.5 4.1 %collective-permute-start = (bf16[3,128,512]{2,1,0:T(8,128)(2,1)}, bf16[3,128,512]{2,1,0:T(8,128)(2,1)S(1)}, u32[]{:S(2)}, u32[]{:S(2)}) collective-permute-start(bf16[3,128,512]{2,1,0:T(8,128)(2,1)} %get-tuple-element.27), channel_id=1, source_target_pairs={{0,8},{4,12},{8,0},{12,4},{1,9},{5,13},{9,1},{13,5},{2,10},{6,14},... | collective-permute-start | bytes 1179656 | tf_op jit(solution)/shard_map/ppermute | solution.py:298
  7.6 1.6 %collective-permute-start.10 = (bf16[2,256,512]{2,1,0:T(8,128)(2,1)}, bf16[2,256,512]{2,1,0:T(8,128)(2,1)S(1)}, u32[]{:S(2)}, u32[]{:S(2)}) collective-permute-start(bf16[2,256,512]{2,1,0:T(8,128)(2,1)} %get-tuple-element.32), channel_id=1, source_target_pairs={{0,4},{4,0},{8,12},{12,8},{1,5},{5,1},{9,13},{13,9},{2,6},{6,2},{1... | collective-permute-start | bytes 1572872 | tf_op jit(solution)/shard_map/ppermute | solution.py:298
  9.1 0.0 copy-done
  9.1 0.0 collective-permute-start.2
  9.1 0.0 copy-start.1
  9.2 0.0 copy-start.2
  9.2 0.0 copy-start.3
  9.2 1.6 %collective-permute-start.8 = (bf16[3,256,512]{2,1,0:T(8,128)(2,1)}, bf16[3,256,512]{2,1,0:T(8,128)(2,1)S(1)}, u32[]{:S(2)}, u32[]{:S(2)}) collective-permute-start(bf16[3,256,512]{2,1,0:T(8,128)(2,1)} %get-tuple-element.28), channel_id=1, source_target_pairs={{0,2},{2,0},{1,3},{3,1},{4,6},{6,4},{5,7},{7,5},{8,10},{10,8},{9,1... | collective-permute-start | bytes 2359304 | tf_op jit(solution)/shard_map/ppermute | solution.py:290
  10.7 0.0 copy-done.4
  10.7 0.2 collective-permute-start.3
  10.9 2.0 %load.1 = (bf16[3,256,512]{2,1,0:T(8,128)(2,1)S(1)}, bf16[2,3,256,512]{3,2,1,0:T(8,128)(2,1)S(1)}, bf16[2,3,256,512]{3,2,1,0:T(8,128)(2,1)S(1)}) custom-call(bf16[3,256,512]{2,1,0:T(8,128)(2,1)S(1)} %copy-done, bf16[2,3,256,512]{3,2,1,0:T(8,128)(2,1)} %refs_1_.1, bf16[2,3,256,512]{3,2,1,0:T(8,128)(2,1)} %refs_2_.1), custom_call_target="tpu_custom_call" | custom-call | flops 30000001024 | bytes 7864320 | tf_op jit(solution)/shard_map/load/pallas_call | solution.py:313
  12.9 12.6 %collective-permute-done.mid.refs_2_ = bf16[3,128,512]{2,1,0:T(8,128)(2,1)S(1)} collective-permute-done((bf16[3,128,512]{2,1,0:T(8,128)(2,1)}, bf16[3,128,512]{2,1,0:T(8,128)(2,1)S(1)}, u32[]{:S(2)}, u32[]{:S(2)}) %collective-permute-start) | collective-permute-done | bytes 393248 | tf_op jit(solution)/shard_map/ppermute | solution.py:298
  25.4 0.0 copy-done.1
  25.4 0.7 %pick.1 = bf16[2,128,512]{2,1,0:T(8,128)(2,1)S(1)} custom-call(s32[4,12]{1,0:T(4,128)S(1)} %copy-done.1, bf16[3,128,512]{2,1,0:T(8,128)(2,1)S(1)} %collective-permute-done.mid.refs_2_), custom_call_target="tpu_custom_call" | custom-call | bytes 655360 | tf_op jit(solution)/shard_map/pick/pallas_call | solution.py:313
  26.1 0.8 %collective-permute-start.1 = (bf16[3,128,512]{2,1,0:T(8,128)(2,1)S(1)}, bf16[3,128,512]{2,1,0:T(8,128)(2,1)S(1)}, u32[]{:S(2)}, u32[]{:S(2)}) collective-permute-start(bf16[3,128,512]{2,1,0:T(8,128)(2,1)S(1)} %collective-permute-done.mid.refs_2_), channel_id=1, source_target_pairs={{0,4},{4,0},{8,12},{12,8},{1,5},{5,1},{9,13},{13,9},{2,6},{6,2},{1... | collective-permute-start | bytes 1179656 | tf_op jit(solution)/shard_map/ppermute | solution.py:298
  26.9 0.0 collective-permute-done.2.own_far
  26.9 1.5 %collective-permute-start.4 = (bf16[2,128,512]{2,1,0:T(8,128)(2,1)S(1)}, bf16[2,128,512]{2,1,0:T(8,128)(2,1)S(1)}, u32[]{:S(2)}, u32[]{:S(2)}) collective-permute-start(bf16[2,128,512]{2,1,0:T(8,128)(2,1)S(1)} %pick.1), channel_id=1, source_target_pairs={{0,2},{2,0},{1,3},{3,1},{4,6},{6,4},{5,7},{7,5},{8,10},{10,8},{9,1... | collective-permute-start | bytes 786440 | tf_op jit(solution)/shard_map/ppermute | solution.py:290
  28.4 0.0 collective-permute-done.3.right_far.refs_8_.refs_6_
  28.4 0.0 copy-done.2
  28.4 0.0 copy-done.3
  28.4 2.1 %own_slots.1.refs_9_ = f32[3,256,512]{2,1,0:T(8,128)S(1)} custom-call(s32[4,12]{1,0:T(4,128)S(1)} %copy-done.1, s32[12]{0:T(128)S(1)} %copy-done.2, s32[12]{0:T(128)S(1)} %copy-done.3, bf16[3,256,512]{2,1,0:T(8,128)(2,1)S(1)} %get-tuple-element.30.own, bf16[3,256,512]{2,1,0:T(8,128)(2,1)S(1)} %collective-permute-done.2.own_far, ...), custom_call_target="tpu_custom_call" | custom-call | flops 30000001024 | bytes 7864320 | tf_op jit(solution)/shard_map/own_slots/pallas_call | solution.py:313
  30.5 0.1 collective-permute-start.6
  30.6 4.4 %collective-permute-done.4.refs_3_ = bf16[2,128,512]{2,1,0:T(8,128)(2,1)S(1)} collective-permute-done((bf16[2,128,512]{2,1,0:T(8,128)(2,1)S(1)}, bf16[2,128,512]{2,1,0:T(8,128)(2,1)S(1)}, u32[]{:S(2)}, u32[]{:S(2)}) %collective-permute-start.4) | collective-permute-done | bytes 262176 | tf_op jit(solution)/shard_map/ppermute | solution.py:290
  35.0 0.0 collective-permute-start.5
  35.0 0.0 collective-permute-done.10.refs_0_
  35.0 0.0 collective-permute-done.8.refs_2_
  35.0 0.6 %collective-permute-start.11 = (bf16[2,256,512]{2,1,0:T(8,128)(2,1)S(1)}, bf16[2,256,512]{2,1,0:T(8,128)(2,1)S(1)}, u32[]{:S(2)}, u32[]{:S(2)}) collective-permute-start(bf16[2,256,512]{2,1,0:T(8,128)(2,1)S(1)} %collective-permute-done.10.refs_0_), channel_id=1, source_target_pairs={{0,1},{1,0},{2,3},{3,2},{4,5},{5,4},{6,7},{7,6},{8,9},{9,8},{10,11... | collective-permute-start | bytes 1572872 | tf_op jit(solution)/shard_map/ppermute | solution.py:290
  35.6 0.1 collective-permute-start.9
  35.7 1.2 %collective-permute-done.1.refs_0_ = bf16[3,128,512]{2,1,0:T(8,128)(2,1)S(1)} collective-permute-done((bf16[3,128,512]{2,1,0:T(8,128)(2,1)S(1)}, bf16[3,128,512]{2,1,0:T(8,128)(2,1)S(1)}, u32[]{:S(2)}, u32[]{:S(2)}) %collective-permute-start.1) | collective-permute-done | bytes 393248 | tf_op jit(solution)/shard_map/ppermute | solution.py:298
  36.9 0.0 collective-permute-done.5.refs_5_
  36.9 0.0 collective-permute-done.6.refs_4_
  36.9 0.0 collective-permute-start.7
  36.9 0.4 collective-permute-done.11.refs_1_
  37.2 1.8 %begin.3.refs_7_ = f32[3,256,256]{2,1,0:T(8,128)S(1)} custom-call(s32[4,12]{1,0:T(4,128)S(1)} %copy-done.1, s32[12]{0:T(128)S(1)} %copy-done.2, s32[12]{0:T(128)S(1)} %copy-done.3, bf16[2,256,512]{2,1,0:T(8,128)(2,1)S(1)} %collective-permute-done.10.refs_0_, bf16[2,256,512]{2,1,0:T(8,128)(2,1)S(1)} %collective-permute-done.11.refs_1_, ...), custom_call_target="tpu_custom_call" | custom-call | bytes 9437184 | tf_op jit(solution)/shard_map/begin/pallas_call | solution.py:313
  39.0 0.0 collective-permute-done.9.refs_3_
  39.0 0.0 collective-permute-done.7.refs_1_
  39.0 1.5 %finish.3 = (f32[3,256,256]{2,1,0:T(8,128)S(1)}, bf16[3,256,256]{2,1,0:T(8,128)(2,1)S(1)}) custom-call(s32[4,12]{1,0:T(4,128)S(1)} %copy-done.1, s32[12]{0:T(128)S(1)} %copy-done.2, s32[12]{0:T(128)S(1)} %copy-done.3, bf16[3,128,512]{2,1,0:T(8,128)(2,1)S(1)} %collective-permute-done.1.refs_0_, ...), custom_call_target="tpu_custom_call", output_to_operand_aliasing={{0}: (10, {})} | custom-call | bytes 8781824 | tf_op jit(solution)/shard_map/finish/pallas_call | solution.py:313
  40.5 1.6 %collective-permute-start.12 = (bf16[3,256,256]{2,1,0:T(8,128)(2,1)S(1)}, bf16[3,256,256]{2,1,0:T(8,128)(2,1)S(1)}, u32[]{:S(2)}, u32[]{:S(2)}) collective-permute-start(bf16[3,256,256]{2,1,0:T(8,128)(2,1)S(1)} %get-tuple-element.48), channel_id=1, source_target_pairs={{0,2},{2,0},{1,3},{3,1},{4,6},{6,4},{5,7},{7,5},{8,10},{10,8},{9,1... | collective-permute-start | bytes 1179656 | tf_op jit(solution)/shard_map/ppermute | solution.py:290
  42.1 1.8 %begin.2.refs_7_ = f32[3,256,256]{2,1,0:T(8,128)S(1)} custom-call(s32[4,12]{1,0:T(4,128)S(1)} %copy-done.1, s32[12]{0:T(128)S(1)} %copy-done.2, s32[12]{0:T(128)S(1)} %copy-done.3, bf16[2,256,512]{2,1,0:T(8,128)(2,1)S(1)} %collective-permute-done.10.refs_0_, bf16[2,256,512]{2,1,0:T(8,128)(2,1)S(1)} %collective-permute-done.11.refs_1_, ...), custom_call_target="tpu_custom_call" | custom-call | bytes 9437184 | tf_op jit(solution)/shard_map/begin/pallas_call | solution.py:313
  43.8 1.4 %finish.2.keep = f32[3,256,256]{2,1,0:T(8,128)S(1)} custom-call(s32[4,12]{1,0:T(4,128)S(1)} %copy-done.1, s32[12]{0:T(128)S(1)} %copy-done.2, s32[12]{0:T(128)S(1)} %copy-done.3, bf16[3,128,512]{2,1,0:T(8,128)(2,1)S(1)} %collective-permute-done.1.refs_0_, bf16[3,128,512]{2,1,0:T(8,128)(2,1)S(1)} %collective-permute-done.7.refs_1_, ...), custom_call_target="tpu_custom_call", output_to_operand_aliasing={{}: (10, {})} | custom-call | bytes 8388608 | tf_op jit(solution)/shard_map/finish/pallas_call | solution.py:313
  45.3 6.6 %collective-permute-done.12.received = bf16[3,256,256]{2,1,0:T(8,128)(2,1)S(1)} collective-permute-done((bf16[3,256,256]{2,1,0:T(8,128)(2,1)S(1)}, bf16[3,256,256]{2,1,0:T(8,128)(2,1)S(1)}, u32[]{:S(2)}, u32[]{:S(2)}) %collective-permute-start.12) | collective-permute-done | bytes 393248 | tf_op jit(solution)/shard_map/ppermute | solution.py:290
  51.8 1.4 %join.1 = bf16[3,256,256]{2,1,0:T(8,128)(2,1)} custom-call(s32[12]{0:T(128)S(1)} %copy-done.2, s32[12]{0:T(128)S(1)} %copy-done.3, f32[3,256,256]{2,1,0:T(8,128)S(1)} %finish.2.keep, bf16[3,256,256]{2,1,0:T(8,128)(2,1)S(1)} %collective-permute-done.12.received), custom_call_target="tpu_custom_call" | custom-call | bytes 1572864 | tf_op jit(solution)/shard_map/join/pallas_call | solution.py:313
  (1 shorter events, 0.0 us)
Async XLA Ops:
  0.0 10.7 %copy-start.4 = (bf16[2,3,256,512]{3,2,1,0:T(8,128)(2,1)S(1)}, bf16[2,3,256,512]{3,2,1,0:T(8,128)(2,1)}, u32[]{:S(2)}) copy-start(bf16[2,3,256,512]{3,2,1,0:T(8,128)(2,1)} %refs_2_.1) | copy-start | bytes 4718596
  0.0 9.1 %copy-start = (bf16[3,256,512]{2,1,0:T(8,128)(2,1)S(1)}, bf16[3,256,512]{2,1,0:T(8,128)(2,1)}, u32[]{:S(2)}) copy-start(bf16[3,256,512]{2,1,0:T(8,128)(2,1)} %refs_0_) | copy-start | bytes 2359300
  3.5 22.0 %collective-permute-start = (bf16[3,128,512]{2,1,0:T(8,128)(2,1)}, bf16[3,128,512]{2,1,0:T(8,128)(2,1)S(1)}, u32[]{:S(2)}, u32[]{:S(2)}) collective-permute-start(bf16[3,128,512]{2,1,0:T(8,128)(2,1)} %get-tuple-element.27), channel_id=1, source_target_pairs={{0,8},{4,12},{8,0},{12,4},{1,9},{5,13},{9,1},{13,5},{2,10},{6,14},... | collective-permute-start | bytes 1179656 | tf_op jit(solution)/shard_map/ppermute | solution.py:298
  7.6 27.4 %collective-permute-start.10 = (bf16[2,256,512]{2,1,0:T(8,128)(2,1)}, bf16[2,256,512]{2,1,0:T(8,128)(2,1)S(1)}, u32[]{:S(2)}, u32[]{:S(2)}) collective-permute-start(bf16[2,256,512]{2,1,0:T(8,128)(2,1)} %get-tuple-element.32), channel_id=1, source_target_pairs={{0,4},{4,0},{8,12},{12,8},{1,5},{5,1},{9,13},{13,9},{2,6},{6,2},{1... | collective-permute-start | bytes 1572872 | tf_op jit(solution)/shard_map/ppermute | solution.py:298
  9.1 17.8 %collective-permute-start.2 = (bf16[3,256,512]{2,1,0:T(8,128)(2,1)S(1)}, bf16[3,256,512]{2,1,0:T(8,128)(2,1)S(1)}, u32[]{:S(2)}, u32[]{:S(2)}) collective-permute-start(bf16[3,256,512]{2,1,0:T(8,128)(2,1)S(1)} %copy-done), channel_id=1, source_target_pairs={{0,1},{1,0},{2,3},{3,2},{4,5},{5,4},{6,7},{7,6},{8,9},{9,8},{10,11... | collective-permute-start | bytes 2359304 | tf_op jit(solution)/shard_map/ppermute | solution.py:290
  9.1 16.3 %copy-start.1 = (s32[4,12]{1,0:T(4,128)S(1)}, s32[4,12]{1,0:T(4,128)}, u32[]{:S(2)}) copy-start(s32[4,12]{1,0:T(4,128)} %source.11) | copy-start | bytes 580
  9.2 19.3 %copy-start.2 = (s32[12]{0:T(128)S(1)}, s32[12]{0:T(128)}, u32[]{:S(2)}) copy-start(s32[12]{0:T(128)} %left_dims.11) | copy-start | bytes 148
  9.2 19.3 %copy-start.3 = (s32[12]{0:T(128)S(1)}, s32[12]{0:T(128)}, u32[]{:S(2)}) copy-start(s32[12]{0:T(128)} %right_dims.11) | copy-start | bytes 148
  9.2 25.8 %collective-permute-start.8 = (bf16[3,256,512]{2,1,0:T(8,128)(2,1)}, bf16[3,256,512]{2,1,0:T(8,128)(2,1)S(1)}, u32[]{:S(2)}, u32[]{:S(2)}) collective-permute-start(bf16[3,256,512]{2,1,0:T(8,128)(2,1)} %get-tuple-element.28), channel_id=1, source_target_pairs={{0,2},{2,0},{1,3},{3,1},{4,6},{6,4},{5,7},{7,5},{8,10},{10,8},{9,1... | collective-permute-start | bytes 2359304 | tf_op jit(solution)/shard_map/ppermute | solution.py:290
  10.7 17.7 %collective-permute-start.3 = (bf16[2,3,256,512]{3,2,1,0:T(8,128)(2,1)S(1)}, bf16[2,3,256,512]{3,2,1,0:T(8,128)(2,1)S(1)}, u32[]{:S(2)}, u32[]{:S(2)}) collective-permute-start(bf16[2,3,256,512]{3,2,1,0:T(8,128)(2,1)S(1)} %copy-done.4), channel_id=1, source_target_pairs={{0,1},{1,0},{2,3},{3,2},{4,5},{5,4},{6,7},{7,6},{8,9},{9,8},{10,11... | collective-permute-start | bytes 4718600 | tf_op jit(solution)/shard_map/ppermute | solution.py:290
  26.1 10.8 %collective-permute-start.1 = (bf16[3,128,512]{2,1,0:T(8,128)(2,1)S(1)}, bf16[3,128,512]{2,1,0:T(8,128)(2,1)S(1)}, u32[]{:S(2)}, u32[]{:S(2)}) collective-permute-start(bf16[3,128,512]{2,1,0:T(8,128)(2,1)S(1)} %collective-permute-done.mid.refs_2_), channel_id=1, source_target_pairs={{0,4},{4,0},{8,12},{12,8},{1,5},{5,1},{9,13},{13,9},{2,6},{6,2},{1... | collective-permute-start | bytes 1179656 | tf_op jit(solution)/shard_map/ppermute | solution.py:298
  26.9 8.0 %collective-permute-start.4 = (bf16[2,128,512]{2,1,0:T(8,128)(2,1)S(1)}, bf16[2,128,512]{2,1,0:T(8,128)(2,1)S(1)}, u32[]{:S(2)}, u32[]{:S(2)}) collective-permute-start(bf16[2,128,512]{2,1,0:T(8,128)(2,1)S(1)} %pick.1), channel_id=1, source_target_pairs={{0,2},{2,0},{1,3},{3,1},{4,6},{6,4},{5,7},{7,5},{8,10},{10,8},{9,1... | collective-permute-start | bytes 786440 | tf_op jit(solution)/shard_map/ppermute | solution.py:290
  30.5 6.3 %collective-permute-start.6 = (bf16[3,128,512]{2,1,0:T(8,128)(2,1)S(1)}, bf16[3,128,512]{2,1,0:T(8,128)(2,1)S(1)}, u32[]{:S(2)}, u32[]{:S(2)}) collective-permute-start(bf16[3,128,512]{2,1,0:T(8,128)(2,1)S(1)} %collective-permute-done.mid.refs_2_), channel_id=1, source_target_pairs={{0,1},{1,0},{2,3},{3,2},{4,5},{5,4},{6,7},{7,6},{8,9},{9,8},{10,11... | collective-permute-start | bytes 1179656 | tf_op jit(solution)/shard_map/ppermute | solution.py:290
  35.0 1.9 %collective-permute-start.5 = (bf16[2,128,512]{2,1,0:T(8,128)(2,1)S(1)}, bf16[2,128,512]{2,1,0:T(8,128)(2,1)S(1)}, u32[]{:S(2)}, u32[]{:S(2)}) collective-permute-start(bf16[2,128,512]{2,1,0:T(8,128)(2,1)S(1)} %collective-permute-done.4.refs_3_), channel_id=1, source_target_pairs={{0,1},{1,0},{2,3},{3,2},{4,5},{5,4},{6,7},{7,6},{8,9},{9,8},{10,11... | collective-permute-start | bytes 786440 | tf_op jit(solution)/shard_map/ppermute | solution.py:290
  35.0 2.2 %collective-permute-start.11 = (bf16[2,256,512]{2,1,0:T(8,128)(2,1)S(1)}, bf16[2,256,512]{2,1,0:T(8,128)(2,1)S(1)}, u32[]{:S(2)}, u32[]{:S(2)}) collective-permute-start(bf16[2,256,512]{2,1,0:T(8,128)(2,1)S(1)} %collective-permute-done.10.refs_0_), channel_id=1, source_target_pairs={{0,1},{1,0},{2,3},{3,2},{4,5},{5,4},{6,7},{7,6},{8,9},{9,8},{10,11... | collective-permute-start | bytes 1572872 | tf_op jit(solution)/shard_map/ppermute | solution.py:290
  35.6 3.4 %collective-permute-start.9 = (bf16[2,256,512]{2,1,0:T(8,128)(2,1)S(1)}, bf16[2,256,512]{2,1,0:T(8,128)(2,1)S(1)}, u32[]{:S(2)}, u32[]{:S(2)}) collective-permute-start(bf16[2,256,512]{2,1,0:T(8,128)(2,1)S(1)} %slice.3), channel_id=1, source_target_pairs={{0,1},{1,0},{2,3},{3,2},{4,5},{5,4},{6,7},{7,6},{8,9},{9,8},{10,11... | collective-permute-start | bytes 1572872 | tf_op jit(solution)/shard_map/ppermute | solution.py:290
  36.9 2.2 %collective-permute-start.7 = (bf16[3,128,512]{2,1,0:T(8,128)(2,1)S(1)}, bf16[3,128,512]{2,1,0:T(8,128)(2,1)S(1)}, u32[]{:S(2)}, u32[]{:S(2)}) collective-permute-start(bf16[3,128,512]{2,1,0:T(8,128)(2,1)S(1)} %collective-permute-done.1.refs_0_), channel_id=1, source_target_pairs={{0,1},{1,0},{2,3},{3,2},{4,5},{5,4},{6,7},{7,6},{8,9},{9,8},{10,11... | collective-permute-start | bytes 1179656 | tf_op jit(solution)/shard_map/ppermute | solution.py:290
  40.5 11.3 %collective-permute-start.12 = (bf16[3,256,256]{2,1,0:T(8,128)(2,1)S(1)}, bf16[3,256,256]{2,1,0:T(8,128)(2,1)S(1)}, u32[]{:S(2)}, u32[]{:S(2)}) collective-permute-start(bf16[3,256,256]{2,1,0:T(8,128)(2,1)S(1)} %get-tuple-element.48), channel_id=1, source_target_pairs={{0,2},{2,0},{1,3},{3,1},{4,6},{6,4},{5,7},{7,5},{8,10},{10,8},{9,1... | collective-permute-start | bytes 1179656 | tf_op jit(solution)/shard_map/ppermute | solution.py:290
